TPU v7x, 32 devices: a whole 2x2x4 slice. The times are simulated.
32 devices in a mesh: seq: 4 (over x, core), fsdp: 8 (over z, y).
Axes of the slice: x: 2, y: 2, z: 4, core: 2. Of those that a mesh axis runs over, the one named last changes fastest.
Arguments:
- tokens: bfloat16 [8, 2560, 1280], P('fsdp', 'seq'), may hold values from -6 to 6
- cont_lengths: int32 [8, 2], P('fsdp'), may hold values from 128 to 384, as said below
- adapter_ids: int32 [8, 3], P('fsdp'), may hold values from 0 to 7
- attn_gain: float32 [2, 1280], replicated, may hold values from 0.25 to 1.75
- mlp_gain: float32 [2, 1280], replicated, may hold values from 0.25 to 1.75
- query_scale: float32 [2, 80], replicated, may hold values from -1 to 1
- w_qkv: bfloat16 [2, 1280, 3840], P(None, 'fsdp'), may hold values from -0.15625 to 0.15625
- output_weight: bfloat16 [2, 1280, 1280], P(None, 'fsdp'), may hold values from -1.25 to 1.25
- inward_weight: bfloat16 [2, 1280, 1280], P(None, 'fsdp'), may hold values from -0.15625 to 0.15625
- down_weight: bfloat16 [2, 1280, 1280], P(None, 'fsdp'), may hold values from -0.15625 to 0.15625
- projection_first_factor: bfloat16 [2, 1280, 384], P(None, 'fsdp'), may hold values from -0.15625 to 0.15625
- b_qkv: bfloat16 [2, 3, 128, 1280], P(None, None, None, 'fsdp'), may hold values from -0.75 to 0.75
- output_first_factor: bfloat16 [2, 1280, 128], P(None, 'fsdp'), may hold values from -0.15625 to 0.15625
- output_second_factor: bfloat16 [2, 128, 1280], P(None, None, 'fsdp'), may hold values from -2 to 2
- inward_first_factor: bfloat16 [2, 1280, 128], P(None, 'fsdp'), may hold values from -0.15625 to 0.15625
- inward_second_factor: bfloat16 [2, 128, 1280], P(None, None, 'fsdp'), may hold values from -0.75 to 0.75
- down_first_factor: bfloat16 [2, 1280, 128], P(None, 'fsdp'), may hold values from -0.15625 to 0.15625
- down_second_factor: bfloat16 [2, 128, 1280], P(None, None, 'fsdp'), may hold values from -0.75 to 0.75
- cotangent: bfloat16 [8, 2560, 1280], P('fsdp', 'seq'), may hold values from -6 to 6
Outputs:
- layer_output: bfloat16 [8, 2560, 1280], P('fsdp', 'seq')
- input_grad: float32 [8, 2560, 1280], P('fsdp', 'seq')
- projection_first_gradient: float32 [2, 1280, 384], P(None, 'fsdp')
- grad_b_qkv: float32 [2, 3, 128, 1280], P(None, None, None, 'fsdp')
- output_first_gradient: float32 [2, 1280, 128], P(None, 'fsdp')
- grad_b_out: float32 [2, 128, 1280], P(None, None, 'fsdp')
- inward_first_gradient: float32 [2, 1280, 128], P(None, 'fsdp')
- grad_b_in: float32 [2, 128, 1280], P(None, None, 'fsdp')
- down_first_gradient: float32 [2, 1280, 128], P(None, 'fsdp')
- grad_b_down: float32 [2, 128, 1280], P(None, None, 'fsdp')
Inputs may be any that keep to these rules, and one draw needn't show every extreme that they name: `cont_lengths`: each group's 2 continuation lengths add up to 512; in every group one continuation has exactly 384 tokens and one exactly 128.
All inputs are finite; a program needn't handle non-finite values.
Results may differ from a plain program's by a relative error of at most 0.023.
Values may be sent and summed in bfloat16 or wider, within the bound.
No kernel may reach another device: no remote copies, remote signals or barrier semaphores. Data moves between devices by JAX's collectives and lax.ppermute only.
A program may use at most 320 MiB of HBM per device.

v0:
```python
from functools import partial
import math

import jax
import jax.numpy as jnp
from jax import lax
from jax.sharding import PartitionSpec as P

D = 1280
HEADS = 16
HD = 80
R = 16
LAYERS = 2
PROMPT = 2048
CONTS = 2
AR = 128
GLEN = 2560


def product(left, right):
    return jnp.dot(left, right, preferred_element_type=jnp.float32)


def backward_product(left, right):
    return lax.dot_general(
        left, right, (((1,), (1,)), ((), ())), preferred_element_type=jnp.float32
    )


def product_across(left, right):
    return lax.dot_general(
        left, right, (((0,), (0,)), ((), ())), preferred_element_type=jnp.float32
    )


def rms_scale(hidden, gain):
    return hidden * lax.rsqrt(jnp.mean(hidden * hidden, axis=-1, keepdims=True) + 1e-06) * gain


def norm_grad(hidden, gain, grad_out):
    norm_value, norm_back = jax.vjp(partial(rms_scale, gain=gain), hidden)
    return norm_back(grad_out)[0]


def segment_ids(lengths):
    seg_ends = PROMPT + jnp.cumsum(lengths)
    places = jnp.arange(GLEN, dtype=jnp.int32)
    later = jnp.sum((places[:, None] >= seg_ends[None, :-1]).astype(jnp.int32), axis=1)
    return (places >= PROMPT).astype(jnp.int32) + later


def block_scores(heads, segments, row_start, block_rows):
    local_heads = heads.shape[2] // HD
    query_block = lax.dynamic_slice_in_dim(heads[0], row_start, block_rows, 0).reshape(
        block_rows, local_heads, HD
    )
    key_heads = heads[1].reshape(GLEN, local_heads, HD)
    row_index = row_start + jnp.arange(block_rows, dtype=jnp.int32)
    col_index = jnp.arange(GLEN, dtype=jnp.int32)
    row_segments = lax.dynamic_slice_in_dim(segments, row_start, block_rows)
    same_seq = segments[None, :] == row_segments[:, None]
    allowed = (col_index[None, :] <= row_index[:, None]) & (same_seq | (segments[None, :] == 0))
    scores = jnp.einsum("qhd,khd->hqk", query_block, key_heads, preferred_element_type=jnp.float32)
    return (query_block, key_heads, jnp.where(allowed[None], scores, -1e30))


def attend(heads, segments):
    local_heads = heads.shape[2] // HD
    block_rows = math.gcd(GLEN, 512)
    starts = jnp.arange(GLEN // block_rows, dtype=jnp.int32) * block_rows
    value_heads = heads[2].reshape(GLEN, local_heads, HD)

    def one_block(row_start):
        query_block, key_heads, scores = block_scores(heads, segments, row_start, block_rows)
        row_peak = jnp.max(scores, axis=-1, keepdims=True)
        row_exp = jnp.exp(scores - row_peak)
        row_total = jnp.sum(row_exp, axis=-1, keepdims=True)
        attn_probs = (row_exp / row_total).astype(jnp.bfloat16)
        mixed_rows = jnp.einsum(
            "hqk,khd->qhd", attn_probs, value_heads, preferred_element_type=jnp.float32
        )
        return (
            mixed_rows.astype(jnp.bfloat16).reshape(block_rows, local_heads * HD),
            (row_peak + jnp.log(row_total))[:, :, 0],
        )

    outputs, log_sums = lax.map(one_block, starts)
    return (outputs.reshape(GLEN, local_heads * HD), log_sums)


def attend_back(heads, grad_heads, log_sums, segments, factor_wide):
    local_heads = heads.shape[2] // HD
    block_rows = math.gcd(GLEN, 512)
    starts = jnp.arange(GLEN // block_rows, dtype=jnp.int32) * block_rows
    value_heads = heads[2].reshape(GLEN, local_heads, HD)

    def one_block(carried, inputs):
        key_grad, value_grad = carried
        row_start, lse_block = inputs
        query_block, key_heads, scores = block_scores(heads, segments, row_start, block_rows)
        grad_block = lax.dynamic_slice_in_dim(grad_heads, row_start, block_rows, 0).reshape(
            block_rows, local_heads, HD
        )
        attn_probs = jnp.exp(scores - lse_block[:, :, None])
        grad_probs = jnp.einsum(
            "qhd,khd->hqk", grad_block, value_heads, preferred_element_type=jnp.float32
        )
        row_delta = jnp.sum(attn_probs * grad_probs, axis=-1, keepdims=True)
        dscore = (attn_probs * (grad_probs - row_delta)).astype(jnp.bfloat16)
        query_grad = jnp.einsum(
            "hqk,khd->qhd", dscore, key_heads, preferred_element_type=jnp.float32
        )
        key_grad = key_grad + jnp.einsum(
            "hqk,qhd->khd", dscore, query_block, preferred_element_type=jnp.float32
        )
        value_grad = value_grad + jnp.einsum(
            "hqk,qhd->khd",
            attn_probs.astype(jnp.bfloat16),
            grad_block,
            preferred_element_type=jnp.float32,
        )
        query_grad = (query_grad.reshape(block_rows, local_heads * HD) * factor_wide).astype(
            jnp.bfloat16
        )
        return ((key_grad, value_grad), query_grad)

    empty = jnp.zeros((GLEN, local_heads, HD), jnp.float32)
    (key_grad, value_grad), query_grads = lax.scan(one_block, (empty, empty), (starts, log_sums))
    width = local_heads * HD
    return jnp.stack(
        [
            query_grads.reshape(GLEN, width),
            key_grad.reshape(GLEN, width).astype(jnp.bfloat16),
            value_grad.reshape(GLEN, width).astype(jnp.bfloat16),
        ]
    )


def forward_layer(hidden, pieces, gain_pair, factor, segments, mask_low):
    (
        w_qkv,
        output_weight,
        inward_weight,
        down_weight,
        projection_first_factor,
        output_first_factor,
        inward_first_factor,
        down_first_factor,
        b_qkv,
        output_second_factor,
        inward_second_factor,
        down_second_factor,
    ) = pieces
    row_count = hidden.shape[0]
    normed_rows = rms_scale(hidden, gain_pair[0]).astype(jnp.bfloat16)
    low_qkv = product(normed_rows, projection_first_factor).astype(jnp.bfloat16) * jnp.tile(
        mask_low, (1, 3)
    )
    projected = jnp.einsum(
        "td,dce->cte", normed_rows, w_qkv.reshape(D, 3, D), preferred_element_type=jnp.float32
    )
    projected = projected + jnp.einsum(
        "tca,cae->cte", low_qkv.reshape(row_count, 3, AR), b_qkv, preferred_element_type=jnp.float32
    )
    scaling = jnp.concatenate([jnp.tile(factor, HEADS), jnp.ones((2 * D,), jnp.float32)]).reshape(
        3, 1, D
    )
    heads = lax.all_to_all(
        (projected * scaling).astype(jnp.bfloat16), "seq", split_axis=2, concat_axis=1, tiled=True
    )
    mixed_heads, log_sums = attend(heads, segments)
    mixed_rows = lax.all_to_all(mixed_heads, "seq", split_axis=0, concat_axis=1, tiled=True)
    low_out = product(mixed_rows, output_first_factor).astype(jnp.bfloat16) * mask_low
    middle = hidden + product(mixed_rows, output_weight) + product(low_out, output_second_factor)
    normed_feed_rows = rms_scale(middle, gain_pair[1]).astype(jnp.bfloat16)
    low_in = product(normed_feed_rows, inward_first_factor).astype(jnp.bfloat16) * mask_low
    inner = product(normed_feed_rows, inward_weight) + product(low_in, inward_second_factor)
    active_adapter = jax.nn.silu(inner).astype(jnp.bfloat16)
    low_down = product(active_adapter, down_first_factor).astype(jnp.bfloat16) * mask_low
    result = middle + product(active_adapter, down_weight) + product(low_down, down_second_factor)
    return (
        result,
        (
            hidden,
            normed_rows,
            low_qkv,
            heads,
            log_sums,
            mixed_rows,
            low_out,
            middle,
            normed_feed_rows,
            low_in,
            inner,
            active_adapter,
            low_down,
        ),
    )


def backward_layer(grad_flow, stored, pieces, gain_pair, factor, segments, adapter_select_mask):
    (
        w_qkv,
        output_weight,
        inward_weight,
        down_weight,
        projection_first_factor,
        output_first_factor,
        inward_first_factor,
        down_first_factor,
        b_qkv,
        output_second_factor,
        inward_second_factor,
        down_second_factor,
    ) = pieces
    (
        hidden,
        normed_rows,
        low_qkv,
        heads,
        log_sums,
        mixed_rows,
        low_out,
        middle,
        normed_feed_rows,
        low_in,
        inner,
        active_adapter,
        low_down,
    ) = stored
    row_count = hidden.shape[0]
    low_rank_gradient = grad_flow.astype(jnp.bfloat16)
    down_adapter_term = (
        adapter_select_mask * backward_product(low_rank_gradient, down_second_factor)
    ).astype(jnp.bfloat16)
    active_adapter_gradient = backward_product(low_rank_gradient, down_weight) + backward_product(
        down_adapter_term, down_first_factor
    )
    grad_b_down = product_across(low_down, low_rank_gradient)
    down_first_gradient = product_across(active_adapter, down_adapter_term)
    silu_value, silu_back = jax.vjp(jax.nn.silu, inner)
    inner_gradient = silu_back(active_adapter_gradient)[0].astype(jnp.bfloat16)
    inward_adapter_term = (
        adapter_select_mask * backward_product(inner_gradient, inward_second_factor)
    ).astype(jnp.bfloat16)
    normed_feed_gradient = backward_product(inner_gradient, inward_weight) + backward_product(
        inward_adapter_term, inward_first_factor
    )
    grad_b_in = product_across(low_in, inner_gradient)
    inward_first_gradient = product_across(normed_feed_rows, inward_adapter_term)
    grad_flow = grad_flow + norm_grad(middle, gain_pair[1], normed_feed_gradient)
    low_rank_gradient = grad_flow.astype(jnp.bfloat16)
    output_adapter_term = (
        adapter_select_mask * backward_product(low_rank_gradient, output_second_factor)
    ).astype(jnp.bfloat16)
    mixed_gradient = (
        backward_product(low_rank_gradient, output_weight)
        + backward_product(output_adapter_term, output_first_factor)
    ).astype(jnp.bfloat16)
    grad_b_out = product_across(low_out, low_rank_gradient)
    output_first_gradient = product_across(mixed_rows, output_adapter_term)
    grad_heads = lax.all_to_all(mixed_gradient, "seq", split_axis=1, concat_axis=0, tiled=True)
    factor_wide = jnp.tile(factor, heads.shape[2] // HD)
    head_grads = attend_back(heads, grad_heads, log_sums, segments, factor_wide)
    grad_proj = lax.all_to_all(head_grads, "seq", split_axis=1, concat_axis=2, tiled=True)
    adapter_terms = jnp.einsum(
        "ctd,cad->tca", grad_proj, b_qkv, preferred_element_type=jnp.float32
    ).reshape(row_count, 3 * AR)
    projection_adapter_term = (jnp.tile(adapter_select_mask, (1, 3)) * adapter_terms).astype(
        jnp.bfloat16
    )
    normed_gradient = lax.dot_general(
        grad_proj,
        w_qkv.reshape(D, 3, D),
        (((0, 2), (1, 2)), ((), ())),
        preferred_element_type=jnp.float32,
    )
    normed_gradient = normed_gradient + backward_product(
        projection_adapter_term, projection_first_factor
    )
    grad_b_qkv = jnp.einsum(
        "tca,ctd->cad",
        low_qkv.reshape(row_count, 3, AR),
        grad_proj,
        preferred_element_type=jnp.float32,
    )
    projection_first_gradient = product_across(normed_rows, projection_adapter_term)
    grad_flow = grad_flow + norm_grad(hidden, gain_pair[0], normed_gradient)
    return (
        grad_flow,
        (
            projection_first_gradient,
            grad_b_qkv,
            output_first_gradient,
            grad_b_out,
            inward_first_gradient,
            grad_b_in,
            down_first_gradient,
            grad_b_down,
        ),
    )


def reduce_layer(grads):
    shared = (
        lax.psum_scatter(
            grads[0].astype(jnp.bfloat16), "fsdp", scatter_dimension=0, tiled=True
        ).astype(jnp.float32),
        lax.psum_scatter(
            grads[1].astype(jnp.bfloat16), "fsdp", scatter_dimension=2, tiled=True
        ).astype(jnp.float32),
        lax.psum_scatter(
            grads[2].astype(jnp.bfloat16), "fsdp", scatter_dimension=0, tiled=True
        ).astype(jnp.float32),
        lax.psum_scatter(
            grads[3].astype(jnp.bfloat16), "fsdp", scatter_dimension=1, tiled=True
        ).astype(jnp.float32),
        lax.psum_scatter(
            grads[4].astype(jnp.bfloat16), "fsdp", scatter_dimension=0, tiled=True
        ).astype(jnp.float32),
        lax.psum_scatter(
            grads[5].astype(jnp.bfloat16), "fsdp", scatter_dimension=1, tiled=True
        ).astype(jnp.float32),
        lax.psum_scatter(
            grads[6].astype(jnp.bfloat16), "fsdp", scatter_dimension=0, tiled=True
        ).astype(jnp.float32),
        lax.psum_scatter(
            grads[7].astype(jnp.bfloat16), "fsdp", scatter_dimension=1, tiled=True
        ).astype(jnp.float32),
    )
    return (
        lax.psum(shared[0].astype(jnp.bfloat16), "seq").astype(jnp.float32),
        lax.psum(shared[1].astype(jnp.bfloat16), "seq").astype(jnp.float32),
        lax.psum(shared[2].astype(jnp.bfloat16), "seq").astype(jnp.float32),
        lax.psum(shared[3].astype(jnp.bfloat16), "seq").astype(jnp.float32),
        lax.psum(shared[4].astype(jnp.bfloat16), "seq").astype(jnp.float32),
        lax.psum(shared[5].astype(jnp.bfloat16), "seq").astype(jnp.float32),
        lax.psum(shared[6].astype(jnp.bfloat16), "seq").astype(jnp.float32),
        lax.psum(shared[7].astype(jnp.bfloat16), "seq").astype(jnp.float32),
    )


def local(
    tokens,
    cont_lengths,
    adapter_ids,
    attn_gain,
    mlp_gain,
    query_scale,
    w_qkv,
    output_weight,
    inward_weight,
    down_weight,
    projection_first_factor,
    b_qkv,
    output_first_factor,
    output_second_factor,
    inward_first_factor,
    inward_second_factor,
    down_first_factor,
    down_second_factor,
    cotangent,
):
    row_count = tokens.shape[1]
    segments = segment_ids(cont_lengths[0])
    local_segments = lax.dynamic_slice_in_dim(
        segments, lax.axis_index("seq") * row_count, row_count
    )
    matches = local_segments[:, None] == jnp.arange(CONTS + 1, dtype=jnp.int32)[None, :]
    chosen = jnp.sum(jnp.where(matches, adapter_ids[0][None, :], 0), axis=1)
    adapter_select_mask = (
        (jnp.arange(AR, dtype=jnp.int32) // R)[None, :] == chosen[:, None]
    ).astype(jnp.float32)
    mask_low = adapter_select_mask.astype(jnp.bfloat16)
    hidden = tokens[0].astype(jnp.float32)
    kept_pieces = []
    stored_all = []
    factors = []
    for layer_index in range(LAYERS):
        pieces = (
            lax.all_gather(w_qkv[layer_index], "fsdp", axis=0, tiled=True),
            lax.all_gather(output_weight[layer_index], "fsdp", axis=0, tiled=True),
            lax.all_gather(inward_weight[layer_index], "fsdp", axis=0, tiled=True),
            lax.all_gather(down_weight[layer_index], "fsdp", axis=0, tiled=True),
            lax.all_gather(projection_first_factor[layer_index], "fsdp", axis=0, tiled=True),
            lax.all_gather(output_first_factor[layer_index], "fsdp", axis=0, tiled=True),
            lax.all_gather(inward_first_factor[layer_index], "fsdp", axis=0, tiled=True),
            lax.all_gather(down_first_factor[layer_index], "fsdp", axis=0, tiled=True),
            lax.all_gather(b_qkv[layer_index], "fsdp", axis=2, tiled=True),
            lax.all_gather(output_second_factor[layer_index], "fsdp", axis=1, tiled=True),
            lax.all_gather(inward_second_factor[layer_index], "fsdp", axis=1, tiled=True),
            lax.all_gather(down_second_factor[layer_index], "fsdp", axis=1, tiled=True),
        )
        factor = 1.442695041 / math.sqrt(HD) * jax.nn.softplus(query_scale[layer_index])
        hidden, stored = forward_layer(
            hidden,
            pieces,
            (attn_gain[layer_index], mlp_gain[layer_index]),
            factor,
            segments,
            mask_low,
        )
        kept_pieces.append(pieces)
        stored_all.append(stored)
        factors.append(factor)
    layer_output = hidden.astype(jnp.bfloat16)[None]
    grad_flow = cotangent[0].astype(jnp.float32)
    layer_sums = [None] * LAYERS
    for layer_index in reversed(range(LAYERS)):
        pieces = (
            lax.all_gather(w_qkv[layer_index], "fsdp", axis=0, tiled=True),
            lax.all_gather(output_weight[layer_index], "fsdp", axis=0, tiled=True),
            lax.all_gather(inward_weight[layer_index], "fsdp", axis=0, tiled=True),
            lax.all_gather(down_weight[layer_index], "fsdp", axis=0, tiled=True),
            lax.all_gather(projection_first_factor[layer_index], "fsdp", axis=0, tiled=True),
            lax.all_gather(output_first_factor[layer_index], "fsdp", axis=0, tiled=True),
            lax.all_gather(inward_first_factor[layer_index], "fsdp", axis=0, tiled=True),
            lax.all_gather(down_first_factor[layer_index], "fsdp", axis=0, tiled=True),
            lax.all_gather(b_qkv[layer_index], "fsdp", axis=2, tiled=True),
            lax.all_gather(output_second_factor[layer_index], "fsdp", axis=1, tiled=True),
            lax.all_gather(inward_second_factor[layer_index], "fsdp", axis=1, tiled=True),
            lax.all_gather(down_second_factor[layer_index], "fsdp", axis=1, tiled=True),
        )
        grad_flow, grads = backward_layer(
            grad_flow,
            stored_all[layer_index],
            pieces,
            (attn_gain[layer_index], mlp_gain[layer_index]),
            factors[layer_index],
            segments,
            adapter_select_mask,
        )
        layer_sums[layer_index] = reduce_layer(grads)
    stacked = [
        jnp.stack([layer_sums[depth_index][member] for depth_index in range(LAYERS)])
        for member in range(8)
    ]
    return (
        layer_output,
        grad_flow[None],
        stacked[0],
        stacked[1],
        stacked[2],
        stacked[3],
        stacked[4],
        stacked[5],
        stacked[6],
        stacked[7],
    )


def solution(mesh):
    return jax.shard_map(
        local,
        mesh=mesh,
        in_specs=(
            P("fsdp", "seq", None),
            P("fsdp", None),
            P("fsdp", None),
            P(),
            P(),
            P(),
            P(None, "fsdp", None),
            P(None, "fsdp", None),
            P(None, "fsdp", None),
            P(None, "fsdp", None),
            P(None, "fsdp", None),
            P(None, None, None, "fsdp"),
            P(None, "fsdp", None),
            P(None, None, "fsdp"),
            P(None, "fsdp", None),
            P(None, None, "fsdp"),
            P(None, "fsdp", None),
            P(None, None, "fsdp"),
            P("fsdp", "seq", None),
        ),
        out_specs=(
            P("fsdp", "seq", None),
            P("fsdp", "seq", None),
            P(None, "fsdp", None),
            P(None, None, None, "fsdp"),
            P(None, "fsdp", None),
            P(None, None, "fsdp"),
            P(None, "fsdp", None),
            P(None, None, "fsdp"),
            P(None, "fsdp", None),
            P(None, None, "fsdp"),
        ),
        check_vma=False,
    )
```

profile of v0, /device:TPU:0, one launch (start us, length us, event | category | flops | bytes accessed | tf_op | source)
XLA Modules:
  0.0 2820.1 jit_solution(10540973289782975531)
XLA Ops:
  20.3 39.0 %all-gather.1 = bf16[1,1280,384]{2,1,0:T(8,128)(2,1)S(1)} all-gather(bf16[1,160,384]{2,1,0:T(8,128)(2,1)S(1)} %get-tuple-element.411), channel_id=3, replica_groups=mesh['seq'=4,'fsdp'=8] {'fsdp'}, dimensions={1}, use_global_device_ids=true | all-gather | bytes 1105920 | tf_op jit(solution)/shard_map/all_gather | solution.py:385
  60.5 34.9 %all-gather.2 = bf16[1,3,128,1280]{2,3,1,0:T(8,128)(2,1)S(1)} all-gather(bf16[1,3,128,160]{2,3,1,0:T(8,128)(2,1)S(1)} %get-tuple-element.409), channel_id=4, replica_groups=mesh['seq'=4,'fsdp'=8] {'fsdp'}, dimensions={3}, use_global_device_ids=true | all-gather | bytes 1105920 | tf_op jit(solution)/shard_map/all_gather | solution.py:389
  95.4 77.6 %all-gather.33.cloned.1.call-done = bf16[1,1280,3840]{2,1,0:T(8,128)(2,1)} async-done(((bf16[1,160,3840]{2,1,0:T(8,128)(2,1)}), bf16[1,1280,3840]{2,1,0:T(8,128)(2,1)}) %all-gather.33.cloned.1.call-update) | async-done | bytes 9830416 | tf_op jit(solution)/shard_map/all_gather | solution.py:381
  220.0 34.1 %all-gather.4 = bf16[1,1280,128]{2,1,0:T(8,128)(2,1)} all-gather(bf16[1,160,128]{2,1,0:T(8,128)(2,1)S(1)} %get-tuple-element.423), channel_id=6, replica_groups=mesh['seq'=4,'fsdp'=8] {'fsdp'}, dimensions={1}, use_global_device_ids=true | all-gather | bytes 368640 | tf_op jit(solution)/shard_map/all_gather | solution.py:386
  254.8 34.1 %all-gather.5 = bf16[1,128,1280]{1,2,0:T(8,128)(2,1)} all-gather(bf16[1,128,160]{1,2,0:T(8,128)(2,1)S(1)} %get-tuple-element.421), channel_id=7, replica_groups=mesh['seq'=4,'fsdp'=8] {'fsdp'}, dimensions={2}, use_global_device_ids=true | all-gather | bytes 368640 | tf_op jit(solution)/shard_map/all_gather | solution.py:390
  289.6 34.2 %all-gather.7 = bf16[1,1280,128]{2,1,0:T(8,128)(2,1)} all-gather(bf16[1,160,128]{2,1,0:T(8,128)(2,1)S(1)} %get-tuple-element.419), channel_id=9, replica_groups=mesh['seq'=4,'fsdp'=8] {'fsdp'}, dimensions={1}, use_global_device_ids=true | all-gather | bytes 368640 | tf_op jit(solution)/shard_map/all_gather | solution.py:387
  324.4 33.7 %all-gather.8 = bf16[1,128,1280]{1,2,0:T(8,128)(2,1)} all-gather(bf16[1,128,160]{1,2,0:T(8,128)(2,1)S(1)} %get-tuple-element.417), channel_id=10, replica_groups=mesh['seq'=4,'fsdp'=8] {'fsdp'}, dimensions={2}, use_global_device_ids=true | all-gather | bytes 368640 | tf_op jit(solution)/shard_map/all_gather | solution.py:391
  358.7 33.9 %all-gather.10 = bf16[1,1280,128]{2,1,0:T(8,128)(2,1)} all-gather(bf16[1,160,128]{2,1,0:T(8,128)(2,1)S(1)} %get-tuple-element.415), channel_id=12, replica_groups=mesh['seq'=4,'fsdp'=8] {'fsdp'}, dimensions={1}, use_global_device_ids=true | all-gather | bytes 368640 | tf_op jit(solution)/shard_map/all_gather | solution.py:388
  403.3 179.9 %while.54 = (s32[]{:T(128)}, bf16[5,512,320]{1,2,0:T(8,128)(2,1)}, f32[5,4,512]{2,1,0:T(4,128)S(1)}, s32[5]{0:T(128)S(1)}, s32[2560]{0:T(1024)S(1)}, /*index=5*/...) while((s32[]{:T(128)}, bf16[5,512,320]{1,2,0:T(8,128)(2,1)}, ...), condition=%wide.region_6.7_spmd, body=%wide.region_3.6_spmd.sunk | while | flops 1730315264 | bytes 170495200 | solution.py:87
  592.6 33.8 %all-gather.11 = bf16[1,128,1280]{1,2,0:T(8,128)(2,1)} all-gather(bf16[1,128,160]{1,2,0:T(8,128)(2,1)S(1)} %get-tuple-element.413), channel_id=13, replica_groups=mesh['seq'=4,'fsdp'=8] {'fsdp'}, dimensions={2}, use_global_device_ids=true | all-gather | bytes 368640 | tf_op jit(solution)/shard_map/all_gather | solution.py:392
  626.4 37.0 %all-gather.13 = bf16[1,1280,384]{2,1,0:T(8,128)(2,1)} all-gather(bf16[1,160,384]{2,1,0:T(8,128)(2,1)S(1)} %copy-done.94), channel_id=15, replica_groups=mesh['seq'=4,'fsdp'=8] {'fsdp'}, dimensions={1}, use_global_device_ids=true | all-gather | bytes 1105920 | tf_op jit(solution)/shard_map/all_gather | solution.py:385
  663.3 35.9 %all-gather.14 = bf16[1,3,128,1280]{2,3,1,0:T(8,128)(2,1)} all-gather(bf16[1,3,128,160]{2,3,1,0:T(8,128)(2,1)S(1)} %copy-done.95), channel_id=16, replica_groups=mesh['seq'=4,'fsdp'=8] {'fsdp'}, dimensions={3}, use_global_device_ids=true | all-gather | bytes 1105920 | tf_op jit(solution)/shard_map/all_gather | solution.py:389
  777.3 33.4 %all-gather.16 = bf16[1,1280,128]{2,1,0:T(8,128)(2,1)} all-gather(bf16[1,160,128]{2,1,0:T(8,128)(2,1)S(1)} %copy-done.110), channel_id=18, replica_groups=mesh['seq'=4,'fsdp'=8] {'fsdp'}, dimensions={1}, use_global_device_ids=true | all-gather | bytes 368640 | tf_op jit(solution)/shard_map/all_gather | solution.py:386
  810.7 34.0 %all-gather.17 = bf16[1,128,1280]{1,2,0:T(8,128)(2,1)} all-gather(bf16[1,128,160]{1,2,0:T(8,128)(2,1)S(1)} %copy-done.111), channel_id=19, replica_groups=mesh['seq'=4,'fsdp'=8] {'fsdp'}, dimensions={2}, use_global_device_ids=true | all-gather | bytes 368640 | tf_op jit(solution)/shard_map/all_gather | solution.py:390
  888.2 178.4 %while.55 = (s32[]{:T(128)}, bf16[5,512,320]{1,2,0:T(8,128)(2,1)}, f32[5,4,512]{2,1,0:T(4,128)S(1)}, s32[5]{0:T(128)S(1)}, s32[2560]{0:T(1024)S(1)}, /*index=5*/...) while((s32[]{:T(128)}, bf16[5,512,320]{1,2,0:T(8,128)(2,1)}, ...), condition=%wide.region_12.13_spmd, body=%wide.region_9.12_spmd.sunk | while | flops 1730315264 | bytes 170495200 | solution.py:87
  1240.9 414.7 %while.56 = (s32[]{:T(128)}, f32[2560,4,80]{0,2,1:T(8,128)}, f32[2560,4,80]{0,2,1:T(8,128)}, bf16[5,512,320]{1,2,0:T(8,128)(2,1)}, bf16[3,2560,320]{1,2,0:T(8,12...) while((s32[]{:T(128)}, f32[2560,4,80]{0,2,1:T(8,128)}, ...), condition=%wide.region_17.18_spmd.clone, body=%wide.region_15.17_spmd.clone.sunk | while | flops 4266066944 | bytes 225542816 | solution.py:128
  1732.0 65.7 %all-to-all-done.5 = bf16[3,2560,320]{2,0,1:T(4,128)(2,1)} async-done(((bf16[3,2560,320]{2,0,1:T(4,128)(2,1)}), bf16[3,2560,320]{2,0,1:T(4,128)(2,1)}, u32[]{:S(2)}, u32[]{:S(2)}) %all-to-all-start.5) | async-done | bytes 4915232 | tf_op jit(solution)/shard_map/all_to_all | solution.py:265
  1887.1 418.2 %while.57 = (s32[]{:T(128)}, f32[2560,4,80]{0,2,1:T(8,128)}, f32[2560,4,80]{0,2,1:T(8,128)}, bf16[5,512,320]{1,2,0:T(8,128)(2,1)}, bf16[3,2560,320]{1,2,0:T(8,12...) while((s32[]{:T(128)}, f32[2560,4,80]{0,2,1:T(8,128)}, ...), condition=%wide.region_22.23_spmd.clone, body=%wide.region_20.22_spmd.clone.sunk | while | flops 4266066944 | bytes 225542816 | solution.py:128
  2360.1 50.2 %reduce-scatter.41.cloned.1.call-done = bf16[160,128]{1,0:T(8,128)(2,1)} async-done(((bf16[1280,128]{1,0:T(8,128)(2,1)}), bf16[160,128]{1,0:T(8,128)(2,1)}) %reduce-scatter.41.cloned.1.call-update) | async-done | bytes 40976 | tf_op jit(solution)/shard_map/reduce_scatter | solution.py:324
  2410.3 63.5 %reduce-scatter.45.cloned.1.call-done = bf16[128,160]{0,1:T(8,128)(2,1)} async-done(((bf16[128,1280]{0,1:T(8,128)(2,1)}), bf16[128,160]{0,1:T(8,128)(2,1)}) %reduce-scatter.45.cloned.1.call-update) | async-done | bytes 40976 | tf_op jit(solution)/shard_map/reduce_scatter | solution.py:327
  2534.8 42.8 %reduce-scatter.19.cloned.1.call-done = bf16[160,384]{1,0:T(8,128)(2,1)} async-done(((bf16[1280,384]{1,0:T(8,128)(2,1)}), bf16[160,384]{1,0:T(8,128)(2,1)}) %reduce-scatter.19.cloned.1.call-update) | async-done | bytes 122896 | tf_op jit(solution)/shard_map/reduce_scatter | solution.py:306
  2577.6 65.7 %reduce-scatter.23.cloned.1.call-done = bf16[3,128,160]{1,2,0:T(8,128)(2,1)} async-done(((bf16[3,128,1280]{1,2,0:T(8,128)(2,1)}), bf16[3,128,160]{1,2,0:T(8,128)(2,1)}) %reduce-scatter.23.cloned.1.call-update) | async-done | bytes 122896 | tf_op jit(solution)/shard_map/reduce_scatter | solution.py:309
  2643.3 65.9 %reduce-scatter.17.cloned.1.call-done = bf16[160,384]{1,0:T(8,128)(2,1)} async-done(((bf16[1280,384]{1,0:T(8,128)(2,1)}), bf16[160,384]{1,0:T(8,128)(2,1)}) %reduce-scatter.17.cloned.1.call-update) | async-done | bytes 122896 | tf_op jit(solution)/shard_map/reduce_scatter | solution.py:306
  2709.1 65.8 %reduce-scatter.21.cloned.1.call-done = bf16[3,128,160]{1,2,0:T(8,128)(2,1)} async-done(((bf16[3,128,1280]{1,2,0:T(8,128)(2,1)}), bf16[3,128,160]{1,2,0:T(8,128)(2,1)}) %reduce-scatter.21.cloned.1.call-update) | async-done | bytes 122896 | tf_op jit(solution)/shard_map/reduce_scatter | solution.py:309
  (989 shorter events, 1847.5 us)
Async XLA Ops:
  10.6 688.7 %all-gather.41.cloned.1.call-start = ((), (), s32[]{:S(2)}) async-start(), calls=%async_computation.44 | async-start | bytes 11059200 | tf_op jit(solution)/shard_map/all_gather | solution.py:381
  11.4 703.8 %all-gather.35.cloned.1.call-start = ((), (), s32[]{:S(2)}) async-start(), calls=%async_computation.41 | async-start | bytes 3686400 | tf_op jit(solution)/shard_map/all_gather | solution.py:382
  12.4 711.1 %all-gather.37.cloned.1.call-start = ((), (), s32[]{:S(2)}) async-start(), calls=%async_computation.42 | async-start | bytes 3686400 | tf_op jit(solution)/shard_map/all_gather | solution.py:383
  13.5 719.4 %all-gather.39.cloned.1.call-start = ((), (), s32[]{:S(2)}) async-start(), calls=%async_computation.43 | async-start | bytes 3686400 | tf_op jit(solution)/shard_map/all_gather | solution.py:384
  15.7 1159.0 %all-gather.47.cloned.1.call-start = ((), (), s32[]{:S(2)}) async-start(), calls=%async_computation.47 | async-start | bytes 3686400 | tf_op jit(solution)/shard_map/all_gather | solution.py:384
  211.9 180.7 %all-to-all-start = ((bf16[3,640,1280]{1,0,2:T(4,128)(2,1)}), bf16[3,640,1280]{1,0,2:T(4,128)(2,1)}, u32[]{:S(2)}, u32[]{:S(2)}) async-start(bf16[3,640,1280]{1,0,2:T(4,128)(2,1)} %copy.174), calls=%async_computation | async-start | bytes 13107200 | tf_op jit(solution)/shard_map/all_to_all | solution.py:168
  217.3 966.2 %all-gather.43.cloned.1.call-start = ((), (), s32[]{:S(2)}) async-start(), calls=%async_computation.45 | async-start | bytes 3686400 | tf_op jit(solution)/shard_map/all_gather | solution.py:382
  776.5 415.1 %all-gather.45.cloned.1.call-start = ((), (), s32[]{:S(2)}) async-start(), calls=%async_computation.46 | async-start | bytes 3686400 | tf_op jit(solution)/shard_map/all_gather | solution.py:383
  1710.2 649.6 %reduce-scatter.27.cloned.1.call-start = ((), (), s32[]{:S(2)}) async-start(), calls=%async_computation.29 | async-start | bytes 368640 | tf_op jit(solution)/shard_map/reduce_scatter | solution.py:312
  1713.1 646.8 %reduce-scatter.31.cloned.1.call-start = ((), (), s32[]{:S(2)}) async-start(), calls=%async_computation.31 | async-start | bytes 368640 | tf_op jit(solution)/shard_map/reduce_scatter | solution.py:315
  1715.6 644.4 %reduce-scatter.35.cloned.1.call-start = ((), (), s32[]{:S(2)}) async-start(), calls=%async_computation.33 | async-start | bytes 368640 | tf_op jit(solution)/shard_map/reduce_scatter | solution.py:318
  1718.5 641.5 %reduce-scatter.39.cloned.1.call-start = ((), (), s32[]{:S(2)}) async-start(), calls=%async_computation.35 | async-start | bytes 368640 | tf_op jit(solution)/shard_map/reduce_scatter | solution.py:321
  1721.5 638.4 %reduce-scatter.43.cloned.1.call-start = ((), (), s32[]{:S(2)}) async-start(), calls=%async_computation.37 | async-start | bytes 368640 | tf_op jit(solution)/shard_map/reduce_scatter | solution.py:324
  1724.4 635.6 %reduce-scatter.47.cloned.1.call-start = ((), (), s32[]{:S(2)}) async-start(), calls=%async_computation.39 | async-start | bytes 368640 | tf_op jit(solution)/shard_map/reduce_scatter | solution.py:327
  1732.0 628.0 %reduce-scatter.25.cloned.1.call-start = ((), (), s32[]{:S(2)}) async-start(), calls=%async_computation.28 | async-start | bytes 368640 | tf_op jit(solution)/shard_map/reduce_scatter | solution.py:312
  1841.6 518.4 %reduce-scatter.29.cloned.1.call-start = ((), (), s32[]{:S(2)}) async-start(), calls=%async_computation.30 | async-start | bytes 368640 | tf_op jit(solution)/shard_map/reduce_scatter | solution.py:315
  1844.1 516.0 %reduce-scatter.33.cloned.1.call-start = ((), (), s32[]{:S(2)}) async-start(), calls=%async_computation.32 | async-start | bytes 368640 | tf_op jit(solution)/shard_map/reduce_scatter | solution.py:318
  1847.0 513.1 %reduce-scatter.37.cloned.1.call-start = ((), (), s32[]{:S(2)}) async-start(), calls=%async_computation.34 | async-start | bytes 368640 | tf_op jit(solution)/shard_map/reduce_scatter | solution.py:321
  1862.2 548.0 %reduce-scatter.41.cloned.1.call-start = ((), (), s32[]{:S(2)}) async-start(), calls=%async_computation.36 | async-start | bytes 368640 | tf_op jit(solution)/shard_map/reduce_scatter | solution.py:324
  1865.1 608.7 %reduce-scatter.45.cloned.1.call-start = ((), (), s32[]{:S(2)}) async-start(), calls=%async_computation.38 | async-start | bytes 368640 | tf_op jit(solution)/shard_map/reduce_scatter | solution.py:327
  2476.0 167.3 %reduce-scatter.23.cloned.1.call-start = ((), (), s32[]{:S(2)}) async-start(), calls=%async_computation.27 | async-start | bytes 1105920 | tf_op jit(solution)/shard_map/reduce_scatter | solution.py:309
  2480.9 228.2 %reduce-scatter.17.cloned.1.call-start = ((), (), s32[]{:S(2)}) async-start(), calls=%async_computation.24 | async-start | bytes 1105920 | tf_op jit(solution)/shard_map/reduce_scatter | solution.py:306
  2500.0 274.9 %reduce-scatter.21.cloned.1.call-start = ((), (), s32[]{:S(2)}) async-start(), calls=%async_computation.26 | async-start | bytes 1105920 | tf_op jit(solution)/shard_map/reduce_scatter | solution.py:309
  2520.1 289.6 %all-reduce.9.cloned.1.call-start = ((), (), s32[]{:S(2)}) async-start(), calls=%async_computation.49 | async-start | bytes 983040 | tf_op jit(solution)/shard_map/psum | solution.py:332
  (225 other events, 4582.6 us)
Sparse Core Ops, SparseCore 0:
  10.8 162.1 all-gather.32
  175.8 157.5 all-gather.40
  336.2 64.0 all-gather.34
  402.3 60.5 all-gather.36
  464.9 60.4 all-gather.38
  527.5 60.5 all-gather.46
  590.3 81.3 all-gather.42
  779.5 67.7 all-gather.44
  1714.3 60.4 reduce-scatter.26
  1777.9 60.3 reduce-scatter.30
  1841.6 60.3 reduce-scatter.34
  1905.2 60.2 reduce-scatter.38
  1968.8 60.3 reduce-scatter.42
  2032.3 60.3 reduce-scatter.46
  2095.8 60.3 reduce-scatter.24
  2159.3 60.2 reduce-scatter.28
  2222.8 60.3 reduce-scatter.32
  2286.3 60.3 reduce-scatter.36
  2349.9 60.2 reduce-scatter.40
  2413.4 60.3 reduce-scatter.44
  2514.3 63.2 reduce-scatter.18
  2580.9 62.2 reduce-scatter.22
  2646.8 62.2 reduce-scatter.16
  2712.5 62.3 reduce-scatter.20
  (2 shorter events, 65.8 us)
where the time goes:
time: 2830 us; the launch traced here: 2820 us
  matrix products  815 us (29%)
  waiting for transfers between devices  571 us (20%)
  blocking collectives  548 us (19%)
  local copies, waits for them, and re-layouts  436 us (15%)
  other arithmetic  352 us (12%)
  loops' own time  41 us (1%)
  starting transfers between devices  40.4 us (1%)
    convert_element_type x10, other arithmetic, one_block(): dscore = (attn_probs * (grad_probs - row_delta)).astype(jnp.bfloat16)  199 us
    dot_general x10, matrix products, one_block(): jnp.einsum('qhd,khd->hqk', grad_block, value_heads, preferred_element_typ...  146 us
    reduce_scatter x2, waiting for transfers between devices, reduce_layer(): lax.psum_scatter(grads[1].astype(jnp.bfloat16), 'fsdp', scatter_dimension...  131 us
    dot_general x20, matrix products, block_scores(): jnp.einsum('qhd,khd->hqk', query_block, key_heads, preferred_element_type...  131 us
    reduce_scatter x2, waiting for transfers between devices, reduce_layer(): lax.psum_scatter(grads[0].astype(jnp.bfloat16), 'fsdp', scatter_dimension...  109 us
    dot_general x10, matrix products, one_block(): jnp.einsum('hqk,qhd->khd', attn_probs.astype(jnp.bfloat16), grad_block, p...  100 us
    dot_general x10, matrix products, one_block(): jnp.einsum('hqk,khd->qhd', attn_probs, value_heads, preferred_element_typ...  97.4 us
    while x120, local copies, waits for them, and re-layouts  87.6 us
  transfers between devices with their start and end apart: 34, of which 12 were waited for; matrix products, arithmetic and copies ran while one was open for 36% of the time, Pallas kernels for 0%

commit v1 on v0

--- a/solution.py
+++ b/solution.py
@@ -4,6 +4,8 @@
 import jax
 import jax.numpy as jnp
 from jax import lax
+from jax.experimental import pallas as pl
+from jax.experimental.pallas import tpu as pltpu
 from jax.sharding import PartitionSpec as P
 
 D = 1280
@@ -15,6 +17,7 @@
 CONTS = 2
 AR = 128
 GLEN = 2560
+LOG2E = 1.4426950408889634
 
 
 def product(left, right):
@@ -49,91 +52,126 @@
     return (places >= PROMPT).astype(jnp.int32) + later
 
 
-def block_scores(heads, segments, row_start, block_rows):
-    local_heads = heads.shape[2] // HD
-    query_block = lax.dynamic_slice_in_dim(heads[0], row_start, block_rows, 0).reshape(
-        block_rows, local_heads, HD
-    )
-    key_heads = heads[1].reshape(GLEN, local_heads, HD)
-    row_index = row_start + jnp.arange(block_rows, dtype=jnp.int32)
-    col_index = jnp.arange(GLEN, dtype=jnp.int32)
-    row_segments = lax.dynamic_slice_in_dim(segments, row_start, block_rows)
-    same_seq = segments[None, :] == row_segments[:, None]
-    allowed = (col_index[None, :] <= row_index[:, None]) & (same_seq | (segments[None, :] == 0))
-    scores = jnp.einsum("qhd,khd->hqk", query_block, key_heads, preferred_element_type=jnp.float32)
-    return (query_block, key_heads, jnp.where(allowed[None], scores, -1e30))
-
-
-def attend(heads, segments):
-    local_heads = heads.shape[2] // HD
-    block_rows = math.gcd(GLEN, 512)
-    starts = jnp.arange(GLEN // block_rows, dtype=jnp.int32) * block_rows
-    value_heads = heads[2].reshape(GLEN, local_heads, HD)
-
-    def one_block(row_start):
-        query_block, key_heads, scores = block_scores(heads, segments, row_start, block_rows)
-        row_peak = jnp.max(scores, axis=-1, keepdims=True)
-        row_exp = jnp.exp(scores - row_peak)
-        row_total = jnp.sum(row_exp, axis=-1, keepdims=True)
-        attn_probs = (row_exp / row_total).astype(jnp.bfloat16)
-        mixed_rows = jnp.einsum(
-            "hqk,khd->qhd", attn_probs, value_heads, preferred_element_type=jnp.float32
-        )
-        return (
-            mixed_rows.astype(jnp.bfloat16).reshape(block_rows, local_heads * HD),
-            (row_peak + jnp.log(row_total))[:, :, 0],
-        )
-
-    outputs, log_sums = lax.map(one_block, starts)
-    return (outputs.reshape(GLEN, local_heads * HD), log_sums)
-
-
-def attend_back(heads, grad_heads, log_sums, segments, factor_wide):
-    local_heads = heads.shape[2] // HD
-    block_rows = math.gcd(GLEN, 512)
-    starts = jnp.arange(GLEN // block_rows, dtype=jnp.int32) * block_rows
-    value_heads = heads[2].reshape(GLEN, local_heads, HD)
-
-    def one_block(carried, inputs):
-        key_grad, value_grad = carried
-        row_start, lse_block = inputs
-        query_block, key_heads, scores = block_scores(heads, segments, row_start, block_rows)
-        grad_block = lax.dynamic_slice_in_dim(grad_heads, row_start, block_rows, 0).reshape(
-            block_rows, local_heads, HD
-        )
-        attn_probs = jnp.exp(scores - lse_block[:, :, None])
-        grad_probs = jnp.einsum(
-            "qhd,khd->hqk", grad_block, value_heads, preferred_element_type=jnp.float32
-        )
-        row_delta = jnp.sum(attn_probs * grad_probs, axis=-1, keepdims=True)
-        dscore = (attn_probs * (grad_probs - row_delta)).astype(jnp.bfloat16)
-        query_grad = jnp.einsum(
-            "hqk,khd->qhd", dscore, key_heads, preferred_element_type=jnp.float32
-        )
-        key_grad = key_grad + jnp.einsum(
-            "hqk,qhd->khd", dscore, query_block, preferred_element_type=jnp.float32
-        )
-        value_grad = value_grad + jnp.einsum(
-            "hqk,qhd->khd",
-            attn_probs.astype(jnp.bfloat16),
-            grad_block,
-            preferred_element_type=jnp.float32,
-        )
-        query_grad = (query_grad.reshape(block_rows, local_heads * HD) * factor_wide).astype(
-            jnp.bfloat16
-        )
-        return ((key_grad, value_grad), query_grad)
-
-    empty = jnp.zeros((GLEN, local_heads, HD), jnp.float32)
-    (key_grad, value_grad), query_grads = lax.scan(one_block, (empty, empty), (starts, log_sums))
-    width = local_heads * HD
-    return jnp.stack(
-        [
-            query_grads.reshape(GLEN, width),
-            key_grad.reshape(GLEN, width).astype(jnp.bfloat16),
-            value_grad.reshape(GLEN, width).astype(jnp.bfloat16),
-        ]
-    )
+NEG=-1e30
+NT=(((1,),(1,)),((),()))
+NN=(((1,),(0,)),((),()))
+TN=(((0,),(0,)),((),()))
+def dg(a,b,d): return lax.dot_general(a,b,d,preferred_element_type=jnp.float32)
+
+def fwd_kernel(bound_ref, heads_ref, out_ref, lse_ref, q_s, k_s, v_s, *, LH, BQ, UN):
+    bound=bound_ref[0]
+    lane=lax.broadcasted_iota(jnp.int32,(BQ,128),1)
+    for h in range(LH):
+        for i in range(GLEN//BQ):
+            r=slice(i*BQ,(i+1)*BQ)
+            for c,s in ((0,q_s),(1,k_s),(2,v_s)):
+                x=heads_ref[c,r,h*HD:(h+1)*HD]
+                pad=jnp.zeros((BQ,128-HD),jnp.bfloat16) if c<2 else jnp.ones((BQ,128-HD),jnp.bfloat16)
+                s[h,r,:]=jnp.concatenate([x,pad],axis=1)
+    for i in range(GLEN//BQ):
+        q0=i*BQ
+        nk=q0+BQ
+        d0=q0 if q0<PROMPT else PROMPT
+        rows=lax.broadcasted_iota(jnp.int32,(BQ,nk-d0),0)+q0
+        cols=lax.broadcasted_iota(jnp.int32,(BQ,nk-d0),1)+d0
+        allowed=cols<=rows
+        if q0>=PROMPT:
+            allowed=allowed&((cols>=bound)|(rows<bound))
+        outs=[];lses=jnp.zeros((BQ,128),jnp.float32)
+        for h in range(LH):
+            qb=q_s[h,q0:q0+BQ,:]
+            sd=jnp.where(allowed,dg(qb,k_s[h,d0:nk,:],NT),NEG)
+            m=jnp.max(sd,axis=1,keepdims=True)
+            if d0>0:
+                sp=dg(qb,k_s[h,0:d0,:],NT)
+                m=jnp.maximum(m,jnp.max(sp,axis=1,keepdims=True))
+                pp=jnp.exp2(sp-m).astype(jnp.bfloat16)
+            pd=jnp.exp2(sd-m).astype(jnp.bfloat16)
+            acc=dg(pd,v_s[h,d0:nk,:],NN)
+            if d0>0: acc=acc+dg(pp,v_s[h,0:d0,:],NN)
+            l=acc[:,HD:HD+1]
+            outs.append((acc/l)[:,:HD].astype(jnp.bfloat16))
+            lses=jnp.where(lane==h,m+jnp.log2(l),lses)
+        out_ref[q0:q0+BQ,:]=jnp.concatenate(outs,axis=1)
+        lse_ref[q0:q0+BQ,:]=lses
+
+def attend(heads,bound,BQ=256,UN=1):
+    LH=heads.shape[2]//HD
+    return pl.pallas_call(partial(fwd_kernel,LH=LH,BQ=BQ,UN=UN),
+        out_shape=(jax.ShapeDtypeStruct((GLEN,LH*HD),jnp.bfloat16),jax.ShapeDtypeStruct((GLEN,128),jnp.float32)),
+        in_specs=[pl.BlockSpec(memory_space=pltpu.SMEM),pl.BlockSpec(memory_space=pltpu.VMEM)],
+        out_specs=(pl.BlockSpec(memory_space=pltpu.VMEM),)*2,
+        scratch_shapes=[pltpu.VMEM((LH,GLEN,128),jnp.bfloat16)]*3,
+        compiler_params=pltpu.CompilerParams(vmem_limit_bytes=56<<20),
+        name="attend")(bound,heads)
+
+def split3(x):
+    hi=x.astype(jnp.bfloat16); r=x-hi.astype(jnp.float32)
+    mid=r.astype(jnp.bfloat16); lo=(r-mid.astype(jnp.float32)).astype(jnp.bfloat16)
+    return hi,mid,lo
+
+def bwd_kernel(bound_ref, factor_ref, heads_ref, o_ref, do_ref, lse_ref, out_ref, q_s,k_s,v_s,d_s,kt_s,dqt_s,dq_s, *, LH,BK,QC):
+    bound=bound_ref[0]
+    BQ=256
+    hlane=lax.broadcasted_iota(jnp.int32,(BQ,128),1)
+    W=128-HD
+    zl=lax.broadcasted_iota(jnp.int32,(BQ,W),1)
+    for h in range(LH):
+        for i in range(GLEN//BQ):
+            r=slice(i*BQ,(i+1)*BQ); cs=slice(h*HD,(h+1)*HD)
+            lse=-jnp.sum(jnp.where(hlane==h,lse_ref[r,:],0.0),axis=1,keepdims=True)
+            hi,mid,lo=[t.astype(jnp.float32) for t in split3(lse)]
+            ext=jnp.where(zl==0,hi,jnp.where(zl==1,mid,jnp.where(zl==2,lo,0.0))).astype(jnp.bfloat16)
+            q_s[h,r,:]=jnp.concatenate([heads_ref[0,r,cs],ext],axis=1)
+            k_s[h,r,:]=jnp.concatenate([heads_ref[1,r,cs],jnp.ones((BQ,W),jnp.bfloat16)],axis=1)
+            v_s[h,r,:]=jnp.concatenate([heads_ref[2,r,cs],jnp.ones((BQ,W),jnp.bfloat16)],axis=1)
+            do=do_ref[r,cs]
+            delta=-jnp.sum(do.astype(jnp.float32)*o_ref[r,cs].astype(jnp.float32),axis=1,keepdims=True)
+            hi,mid,lo=[t.astype(jnp.float32) for t in split3(delta)]
+            ext=jnp.where(zl==0,hi,jnp.where(zl==1,mid,jnp.where(zl==2,lo,0.0))).astype(jnp.bfloat16)
+            d_s[h,r,:]=jnp.concatenate([do,ext],axis=1)
+    for h in range(LH):
+        kt_s[...]=k_s[h].T
+        for j in range(GLEN//BK):
+            k0=j*BK
+            kb=k_s[h,k0:k0+BK,:]; vb=v_s[h,k0:k0+BK,:]; ktb=kt_s[:,k0:k0+BK]
+            dk=jnp.zeros((BK,128),jnp.float32); dv=jnp.zeros((BK,128),jnp.float32)
+            q0=k0
+            while q0<GLEN:
+                n=BK if q0==k0 else min(QC,GLEN-q0)
+                qs=slice(q0,q0+n)
+                qb=q_s[h,qs,:]; db=d_s[h,qs,:]
+                st=dg(kb,qb,NT)
+                p=jnp.exp2(st)
+                if q0==k0 or k0>=PROMPT:
+                    krow=lax.broadcasted_iota(jnp.int32,(BK,n),0)+k0
+                    qcol=lax.broadcasted_iota(jnp.int32,(BK,n),1)+q0
+                    al=krow<=qcol
+                    if k0>=PROMPT: al=al&((krow>=bound)|(qcol<bound))
+                    p=jnp.where(al,p,0.0)
+                dp=dg(vb,db,NT)
+                ds=(p*dp).astype(jnp.bfloat16)
+                dv=dv+dg(p.astype(jnp.bfloat16),db,NN)
+                dk=dk+dg(ds,qb,NN)
+                dqt=dg(ktb,ds,NN)
+                if j==0: dqt_s[:,qs]=dqt
+                else: dqt_s[:,qs]+=dqt
+                q0+=n
+            out_ref[1,k0:k0+BK,h*HD:(h+1)*HD]=(dk[:,:HD]*0.6931471805599453).astype(jnp.bfloat16)
+            out_ref[2,k0:k0+BK,h*HD:(h+1)*HD]=dv[:,:HD].astype(jnp.bfloat16)
+        for i in range(GLEN//256):
+            out_ref[0,i*256:(i+1)*256,h*HD:(h+1)*HD]=(dqt_s[:,i*256:(i+1)*256].T[:,:HD]*factor_ref[0:1,:HD]).astype(jnp.bfloat16)
+
+def attend_back(heads,mixed,grad_heads,lse,bound,factor,BK=256,QC=512):
+    LH=heads.shape[2]//HD
+    f=jnp.pad(factor.reshape(1,HD),((0,0),(0,128-HD)))
+    return pl.pallas_call(partial(bwd_kernel,LH=LH,BK=BK,QC=QC),
+        out_shape=jax.ShapeDtypeStruct((3,GLEN,LH*HD),jnp.bfloat16),
+        in_specs=[pl.BlockSpec(memory_space=pltpu.SMEM)]+[pl.BlockSpec(memory_space=pltpu.VMEM)]*5,
+        out_specs=pl.BlockSpec(memory_space=pltpu.VMEM),
+        scratch_shapes=[pltpu.VMEM((LH,GLEN,128),jnp.bfloat16)]*4+[pltpu.VMEM((128,GLEN),jnp.bfloat16),pltpu.VMEM((128,GLEN),jnp.float32),pltpu.VMEM((8,128),jnp.float32)],
+        compiler_params=pltpu.CompilerParams(vmem_limit_bytes=60<<20),
+        name="attend_back")(bound,f,heads,mixed,grad_heads,lse)
 
 
 def forward_layer(hidden, pieces, gain_pair, factor, segments, mask_low):
@@ -162,7 +200,7 @@
     projected = projected + jnp.einsum(
         "tca,cae->cte", low_qkv.reshape(row_count, 3, AR), b_qkv, preferred_element_type=jnp.float32
     )
-    scaling = jnp.concatenate([jnp.tile(factor, HEADS), jnp.ones((2 * D,), jnp.float32)]).reshape(
+    scaling = jnp.concatenate([jnp.tile(factor * LOG2E, HEADS), jnp.ones((2 * D,), jnp.float32)]).reshape(
         3, 1, D
     )
     heads = lax.all_to_all(
@@ -185,6 +223,7 @@
             normed_rows,
             low_qkv,
             heads,
+            mixed_heads,
             log_sums,
             mixed_rows,
             low_out,
@@ -218,6 +257,7 @@
         normed_rows,
         low_qkv,
         heads,
+        mixed_heads,
         log_sums,
         mixed_rows,
         low_out,
@@ -260,8 +300,7 @@
     grad_b_out = product_across(low_out, low_rank_gradient)
     output_first_gradient = product_across(mixed_rows, output_adapter_term)
     grad_heads = lax.all_to_all(mixed_gradient, "seq", split_axis=1, concat_axis=0, tiled=True)
-    factor_wide = jnp.tile(factor, heads.shape[2] // HD)
-    head_grads = attend_back(heads, grad_heads, log_sums, segments, factor_wide)
+    head_grads = attend_back(heads, mixed_heads, grad_heads, log_sums, segments, factor)
     grad_proj = lax.all_to_all(head_grads, "seq", split_axis=1, concat_axis=2, tiled=True)
     adapter_terms = jnp.einsum(
         "ctd,cad->tca", grad_proj, b_qkv, preferred_element_type=jnp.float32
@@ -362,6 +401,7 @@
     cotangent,
 ):
     row_count = tokens.shape[1]
+    bound = PROMPT + cont_lengths[0, :1]
     segments = segment_ids(cont_lengths[0])
     local_segments = lax.dynamic_slice_in_dim(
         segments, lax.axis_index("seq") * row_count, row_count
@@ -397,7 +437,7 @@
             pieces,
             (attn_gain[layer_index], mlp_gain[layer_index]),
             factor,
-            segments,
+            bound,
             mask_low,
         )
         kept_pieces.append(pieces)
@@ -427,7 +467,7 @@
             pieces,
             (attn_gain[layer_index], mlp_gain[layer_index]),
             factors[layer_index],
-            segments,
+            bound,
             adapter_select_mask,
         )
         layer_sums[layer_index] = reduce_layer(grads)

time: 2830 us -> 2210 us (0.78)
  matrix products: 815 us -> 191 us
  waiting for transfers between devices: 571 us -> 1000 us
  other arithmetic: 352 us -> 21.7 us
  local copies, waits for them, and re-layouts: 436 us -> 212 us
  Pallas kernels: 0 us -> 162 us
  loops' own time: 41 us -> 0 us
    dot_general x70 -> x0, matrix products: 633 us -> none  [the longest x10 146 us: one_block(): jnp.einsum('qhd,khd->hqk', grad_block, value_heads, preferred_element_typ...]
    convert_element_type x14 -> x0, other arithmetic: 209 us -> none  [the longest x10 199 us: one_block(): dscore = (attn_probs * (grad_probs - row_delta)).astype(jnp.bfloat16)]
    pallas_call x0 -> x4, Pallas kernels: none -> 162 us  [the longest x2 102 us: attend_back(): pl.pallas_call(partial(bwd_kernel, LH=LH, BK=BK, QC=QC), out_shape=jax.Sh...]
    reduce_scatter x2, waiting for transfers between devices: 0.03 us -> 127 us  [reduce_layer(): lax.psum_scatter(grads[3].astype(jnp.bfloat16), 'fsdp', scatter_dimension...]
    reduce_scatter x2, waiting for transfers between devices: 0.03 us -> 127 us  [reduce_layer(): lax.psum_scatter(grads[4].astype(jnp.bfloat16), 'fsdp', scatter_dimension...]
    while x124 -> x0, local copies, waits for them, and re-layouts: 100 us -> none
    reduce_scatter x2, waiting for transfers between devices: 0.03 us -> 93.6 us  [reduce_layer(): lax.psum_scatter(grads[5].astype(jnp.bfloat16), 'fsdp', scatter_dimension...]
    all_to_all x2, waiting for transfers between devices: 65.7 us -> 145 us  [backward_layer(): lax.all_to_all(head_grads, 'seq', split_axis=1, concat_axis=2, tiled=True)]
  transfers between devices with their start and end apart: 34 -> 34, of which waited for: 12 -> 17; matrix products, arithmetic and copies ran while one was open for 36% -> 16% of each run, Pallas kernels for 0% -> 5%
where the time goes in v1:
time: 2210 us; the launch traced here: 2200 us
  waiting for transfers between devices  1000 us (45%)
  blocking collectives  554 us (25%)
  local copies, waits for them, and re-layouts  212 us (10%)
  matrix products  191 us (9%)
  Pallas kernels  162 us (7%)
  starting transfers between devices  41.6 us (2%)
    all_to_all x2, waiting for transfers between devices, backward_layer(): lax.all_to_all(head_grads, 'seq', split_axis=1, concat_axis=2, tiled=True)  145 us
    reduce_scatter x2, waiting for transfers between devices, reduce_layer(): lax.psum_scatter(grads[3].astype(jnp.bfloat16), 'fsdp', scatter_dimension...  127 us
    reduce_scatter x2, waiting for transfers between devices, reduce_layer(): lax.psum_scatter(grads[7].astype(jnp.bfloat16), 'fsdp', scatter_dimension...  127 us
    reduce_scatter x2, waiting for transfers between devices, reduce_layer(): lax.psum_scatter(grads[4].astype(jnp.bfloat16), 'fsdp', scatter_dimension...  127 us
    pallas_call x2, Pallas kernels, attend_back(): pl.pallas_call(partial(bwd_kernel, LH=LH, BK=BK, QC=QC), out_shape=jax.Sh...  102 us
    reduce_scatter x2, waiting for transfers between devices, reduce_layer(): lax.psum_scatter(grads[5].astype(jnp.bfloat16), 'fsdp', scatter_dimension...  93.6 us
    all_gather x2, waiting for transfers between devices, local(): lax.all_gather(w_qkv[layer_index], 'fsdp', axis=0, tiled=True)  78.7 us
    all_gather x2, blocking collectives, local(): lax.all_gather(projection_first_factor[layer_index], 'fsdp', axis=0, tile...  76.1 us
  transfers between devices with their start and end apart: 34, of which 17 were waited for; matrix products, arithmetic and copies ran while one was open for 16% of the time, Pallas kernels for 5%

profile of v1, /device:TPU:0, one launch (start us, length us, event | category | flops | bytes accessed | tf_op | source)
XLA Modules:
  0.0 2201.6 jit_solution(11286286027740604243)
XLA Ops:
  19.0 39.0 %all-gather.1 = bf16[1,1280,384]{2,1,0:T(8,128)(2,1)S(1)} all-gather(bf16[1,160,384]{2,1,0:T(8,128)(2,1)S(1)} %get-tuple-element.53), channel_id=3, replica_groups=mesh['seq'=4,'fsdp'=8] {'fsdp'}, dimensions={1}, use_global_device_ids=true | all-gather | bytes 1105920 | tf_op jit(solution)/shard_map/all_gather | solution.py:425
  59.2 35.2 %all-gather.2 = bf16[1,3,128,1280]{2,3,1,0:T(8,128)(2,1)S(1)} all-gather(bf16[1,3,128,160]{2,3,1,0:T(8,128)(2,1)S(1)} %get-tuple-element.51), channel_id=4, replica_groups=mesh['seq'=4,'fsdp'=8] {'fsdp'}, dimensions={3}, use_global_device_ids=true | all-gather | bytes 1105920 | tf_op jit(solution)/shard_map/all_gather | solution.py:429
  94.4 78.7 %all-gather.33.cloned.1.call-done = bf16[1,1280,3840]{2,1,0:T(8,128)(2,1)} async-done(((bf16[1,160,3840]{2,1,0:T(8,128)(2,1)}), bf16[1,1280,3840]{2,1,0:T(8,128)(2,1)}) %all-gather.33.cloned.1.call-update) | async-done | bytes 9830416 | tf_op jit(solution)/shard_map/all_gather | solution.py:421
  254.1 34.6 %all-gather.10 = bf16[1,1280,128]{2,1,0:T(8,128)(2,1)} all-gather(bf16[1,160,128]{2,1,0:T(8,128)(2,1)S(1)} %get-tuple-element.57), channel_id=12, replica_groups=mesh['seq'=4,'fsdp'=8] {'fsdp'}, dimensions={1}, use_global_device_ids=true | all-gather | bytes 368640 | tf_op jit(solution)/shard_map/all_gather | solution.py:428
  289.3 34.2 %all-gather.8 = bf16[1,128,1280]{1,2,0:T(8,128)(2,1)} all-gather(bf16[1,128,160]{1,2,0:T(8,128)(2,1)S(1)} %get-tuple-element.59), channel_id=10, replica_groups=mesh['seq'=4,'fsdp'=8] {'fsdp'}, dimensions={2}, use_global_device_ids=true | all-gather | bytes 368640 | tf_op jit(solution)/shard_map/all_gather | solution.py:431
  358.3 34.0 %all-gather.5 = bf16[1,128,1280]{1,2,0:T(8,128)(2,1)} all-gather(bf16[1,128,160]{1,2,0:T(8,128)(2,1)S(1)} %get-tuple-element.63), channel_id=7, replica_groups=mesh['seq'=4,'fsdp'=8] {'fsdp'}, dimensions={2}, use_global_device_ids=true | all-gather | bytes 368640 | tf_op jit(solution)/shard_map/all_gather | solution.py:430
  480.4 37.8 %all-gather.14 = bf16[1,3,128,1280]{2,3,1,0:T(8,128)(2,1)} all-gather(bf16[1,3,128,160]{2,3,1,0:T(8,128)(2,1)S(1)} %get-tuple-element.50), channel_id=16, replica_groups=mesh['seq'=4,'fsdp'=8] {'fsdp'}, dimensions={3}, use_global_device_ids=true | all-gather | bytes 1105920 | tf_op jit(solution)/shard_map/all_gather | solution.py:429
  518.1 37.1 %all-gather.13 = bf16[1,1280,384]{2,1,0:T(8,128)(2,1)} all-gather(bf16[1,160,384]{2,1,0:T(8,128)(2,1)S(1)} %get-tuple-element.52), channel_id=15, replica_groups=mesh['seq'=4,'fsdp'=8] {'fsdp'}, dimensions={1}, use_global_device_ids=true | all-gather | bytes 1105920 | tf_op jit(solution)/shard_map/all_gather | solution.py:425
  632.1 34.0 %all-gather.23 = bf16[1,128,1280]{1,2,0:T(8,128)(2,1)} all-gather(bf16[1,128,160]{1,2,0:T(8,128)(2,1)S(1)} %copy-done.83), channel_id=25, replica_groups=mesh['seq'=4,'fsdp'=8] {'fsdp'}, dimensions={2}, use_global_device_ids=true | all-gather | bytes 368640 | tf_op jit(solution)/shard_map/all_gather | solution.py:432
  960.7 50.9 %attend_back.2 = bf16[3,2560,320]{2,1,0:T(8,128)(2,1)} custom-call(s32[1]{0:T(128)} %bitcast.1.bound_ref, f32[1,128]{1,0:T(1,128)} %pad.9.factor_ref, bf16[3,2560,320]{2,1,0:T(8,128)(2,1)} %bitcast.350, bf16[2560,320]{1,0:T(8,128)(2,1)} %get-tuple-element.15.o_ref, bf16[2560,320]{1,0:T(8,128)(2,1)} %bitcast.365, f32[2560,128]{1,0:T(8,128)} %get-tuple-element.16.lse_ref), custom_call_target="tpu_custom_call" | custom-call | tf_op jit(solution)/shard_map/attend_back/pallas_call | solution.py:168
  1066.0 64.5 %all-to-all-done.5 = bf16[3,2560,320]{2,0,1:T(4,128)(2,1)} async-done(((bf16[3,2560,320]{2,0,1:T(4,128)(2,1)}), bf16[3,2560,320]{2,0,1:T(4,128)(2,1)}, u32[]{:S(2)}, u32[]{:S(2)}) %all-to-all-start.5) | async-done | bytes 4915232 | tf_op jit(solution)/shard_map/all_to_all | solution.py:304
  1233.3 63.5 %reduce-scatter.35.cloned.1.call-done = bf16[160,128]{1,0:T(8,128)(2,1)} async-done(((bf16[1280,128]{1,0:T(8,128)(2,1)}), bf16[160,128]{1,0:T(8,128)(2,1)}) %reduce-scatter.35.cloned.1.call-update) | async-done | bytes 40976 | tf_op jit(solution)/shard_map/reduce_scatter | solution.py:357
  1296.8 63.6 %reduce-scatter.47.cloned.1.call-done = bf16[128,160]{0,1:T(8,128)(2,1)} async-done(((bf16[128,1280]{0,1:T(8,128)(2,1)}), bf16[128,160]{0,1:T(8,128)(2,1)}) %reduce-scatter.47.cloned.1.call-update) | async-done | bytes 40976 | tf_op jit(solution)/shard_map/reduce_scatter | solution.py:366
  1360.4 63.5 %reduce-scatter.31.cloned.1.call-done = bf16[128,160]{0,1:T(8,128)(2,1)} async-done(((bf16[128,1280]{0,1:T(8,128)(2,1)}), bf16[128,160]{0,1:T(8,128)(2,1)}) %reduce-scatter.31.cloned.1.call-update) | async-done | bytes 40976 | tf_op jit(solution)/shard_map/reduce_scatter | solution.py:354
  1423.9 63.4 %reduce-scatter.25.cloned.1.call-done = bf16[160,128]{1,0:T(8,128)(2,1)} async-done(((bf16[1280,128]{1,0:T(8,128)(2,1)}), bf16[160,128]{1,0:T(8,128)(2,1)}) %reduce-scatter.25.cloned.1.call-update) | async-done | bytes 40976 | tf_op jit(solution)/shard_map/reduce_scatter | solution.py:351
  1487.3 63.5 %reduce-scatter.45.cloned.1.call-done = bf16[128,160]{0,1:T(8,128)(2,1)} async-done(((bf16[128,1280]{0,1:T(8,128)(2,1)}), bf16[128,160]{0,1:T(8,128)(2,1)}) %reduce-scatter.45.cloned.1.call-update) | async-done | bytes 40976 | tf_op jit(solution)/shard_map/reduce_scatter | solution.py:366
  1550.7 63.4 %reduce-scatter.37.cloned.1.call-done = bf16[128,160]{0,1:T(8,128)(2,1)} async-done(((bf16[128,1280]{0,1:T(8,128)(2,1)}), bf16[128,160]{0,1:T(8,128)(2,1)}) %reduce-scatter.37.cloned.1.call-update) | async-done | bytes 40976 | tf_op jit(solution)/shard_map/reduce_scatter | solution.py:360
  1614.2 63.4 %reduce-scatter.33.cloned.1.call-done = bf16[160,128]{1,0:T(8,128)(2,1)} async-done(((bf16[1280,128]{1,0:T(8,128)(2,1)}), bf16[160,128]{1,0:T(8,128)(2,1)}) %reduce-scatter.33.cloned.1.call-update) | async-done | bytes 40976 | tf_op jit(solution)/shard_map/reduce_scatter | solution.py:357
  1677.6 63.6 %reduce-scatter.41.cloned.1.call-done = bf16[160,128]{1,0:T(8,128)(2,1)} async-done(((bf16[1280,128]{1,0:T(8,128)(2,1)}), bf16[160,128]{1,0:T(8,128)(2,1)}) %reduce-scatter.41.cloned.1.call-update) | async-done | bytes 40976 | tf_op jit(solution)/shard_map/reduce_scatter | solution.py:363
  1741.2 64.0 %reduce-scatter.29.cloned.1.call-done = bf16[128,160]{0,1:T(8,128)(2,1)} async-done(((bf16[128,1280]{0,1:T(8,128)(2,1)}), bf16[128,160]{0,1:T(8,128)(2,1)}) %reduce-scatter.29.cloned.1.call-update) | async-done | bytes 40976 | tf_op jit(solution)/shard_map/reduce_scatter | solution.py:354
  1809.0 50.9 %attend_back.3 = bf16[3,2560,320]{2,1,0:T(8,128)(2,1)} custom-call(s32[1]{0:T(128)} %bitcast.1.bound_ref, f32[1,128]{1,0:T(1,128)} %pad.10.factor_ref, bf16[3,2560,320]{2,1,0:T(8,128)(2,1)} %bitcast.348, bf16[2560,320]{1,0:T(8,128)(2,1)} %get-tuple-element.14.o_ref, bf16[2560,320]{1,0:T(8,128)(2,1)} %bitcast.364, f32[2560,128]{1,0:T(8,128)} %get-tuple-element.17.lse_ref), custom_call_target="tpu_custom_call" | custom-call | tf_op jit(solution)/shard_map/attend_back/pallas_call | solution.py:168
  1898.7 80.2 %all-to-all-done.7 = bf16[3,2560,320]{2,0,1:T(4,128)(2,1)} async-done(((bf16[3,2560,320]{2,0,1:T(4,128)(2,1)}), bf16[3,2560,320]{2,0,1:T(4,128)(2,1)}, u32[]{:S(2)}, u32[]{:S(2)}) %all-to-all-start.7) | async-done | bytes 4915232 | tf_op jit(solution)/shard_map/all_to_all | solution.py:304
  2032.2 58.4 %reduce-scatter.21.cloned.1.call-done = bf16[3,128,160]{1,2,0:T(8,128)(2,1)} async-done(((bf16[3,128,1280]{1,2,0:T(8,128)(2,1)}), bf16[3,128,160]{1,2,0:T(8,128)(2,1)}) %reduce-scatter.21.cloned.1.call-update) | async-done | bytes 122896 | tf_op jit(solution)/shard_map/reduce_scatter | solution.py:348
  2090.6 65.8 %reduce-scatter.17.cloned.1.call-done = bf16[160,384]{1,0:T(8,128)(2,1)} async-done(((bf16[1280,384]{1,0:T(8,128)(2,1)}), bf16[160,384]{1,0:T(8,128)(2,1)}) %reduce-scatter.17.cloned.1.call-update) | async-done | bytes 122896 | tf_op jit(solution)/shard_map/reduce_scatter | solution.py:345
  (482 shorter events, 878.3 us)
Async XLA Ops:
  7.2 165.9 %all-gather.33.cloned.1.call-start = ((), (), s32[]{:S(2)}) async-start(), calls=%async_computation.40 | async-start | bytes 11059200 | tf_op jit(solution)/shard_map/all_gather | solution.py:421
  10.6 544.7 %all-gather.41.cloned.1.call-start = ((), (), s32[]{:S(2)}) async-start(), calls=%async_computation.44 | async-start | bytes 11059200 | tf_op jit(solution)/shard_map/all_gather | solution.py:421
  11.4 559.6 %all-gather.35.cloned.1.call-start = ((), (), s32[]{:S(2)}) async-start(), calls=%async_computation.41 | async-start | bytes 3686400 | tf_op jit(solution)/shard_map/all_gather | solution.py:422
  12.4 565.9 %all-gather.37.cloned.1.call-start = ((), (), s32[]{:S(2)}) async-start(), calls=%async_computation.42 | async-start | bytes 3686400 | tf_op jit(solution)/shard_map/all_gather | solution.py:423
  13.5 572.8 %all-gather.39.cloned.1.call-start = ((), (), s32[]{:S(2)}) async-start(), calls=%async_computation.43 | async-start | bytes 3686400 | tf_op jit(solution)/shard_map/all_gather | solution.py:424
  15.7 873.0 %all-gather.47.cloned.1.call-start = ((), (), s32[]{:S(2)}) async-start(), calls=%async_computation.47 | async-start | bytes 3686400 | tf_op jit(solution)/shard_map/all_gather | solution.py:424
  211.8 180.6 %all-to-all-start = ((bf16[3,640,1280]{1,0,2:T(4,128)(2,1)}), bf16[3,640,1280]{1,0,2:T(4,128)(2,1)}, u32[]{:S(2)}, u32[]{:S(2)}) async-start(bf16[3,640,1280]{1,0,2:T(4,128)(2,1)} %copy.148), calls=%async_computation | async-start | bytes 13107200 | tf_op jit(solution)/shard_map/all_to_all | solution.py:206
  217.3 680.1 %all-gather.43.cloned.1.call-start = ((), (), s32[]{:S(2)}) async-start(), calls=%async_computation.45 | async-start | bytes 3686400 | tf_op jit(solution)/shard_map/all_gather | solution.py:422
  631.4 275.5 %all-gather.45.cloned.1.call-start = ((), (), s32[]{:S(2)}) async-start(), calls=%async_computation.46 | async-start | bytes 3686400 | tf_op jit(solution)/shard_map/all_gather | solution.py:423
  1043.0 160.2 %reduce-scatter.27.cloned.1.call-start = ((), (), s32[]{:S(2)}) async-start(), calls=%async_computation.29 | async-start | bytes 368640 | tf_op jit(solution)/shard_map/reduce_scatter | solution.py:351
  1048.7 184.6 %reduce-scatter.39.cloned.1.call-start = ((), (), s32[]{:S(2)}) async-start(), calls=%async_computation.35 | async-start | bytes 368640 | tf_op jit(solution)/shard_map/reduce_scatter | solution.py:360
  1052.0 244.8 %reduce-scatter.35.cloned.1.call-start = ((), (), s32[]{:S(2)}) async-start(), calls=%async_computation.33 | async-start | bytes 368640 | tf_op jit(solution)/shard_map/reduce_scatter | solution.py:357
  1054.9 305.5 %reduce-scatter.47.cloned.1.call-start = ((), (), s32[]{:S(2)}) async-start(), calls=%async_computation.39 | async-start | bytes 368640 | tf_op jit(solution)/shard_map/reduce_scatter | solution.py:366
  1060.6 363.3 %reduce-scatter.31.cloned.1.call-start = ((), (), s32[]{:S(2)}) async-start(), calls=%async_computation.31 | async-start | bytes 368640 | tf_op jit(solution)/shard_map/reduce_scatter | solution.py:354
  1066.0 421.3 %reduce-scatter.25.cloned.1.call-start = ((), (), s32[]{:S(2)}) async-start(), calls=%async_computation.28 | async-start | bytes 368640 | tf_op jit(solution)/shard_map/reduce_scatter | solution.py:351
  1173.9 376.8 %reduce-scatter.45.cloned.1.call-start = ((), (), s32[]{:S(2)}) async-start(), calls=%async_computation.38 | async-start | bytes 368640 | tf_op jit(solution)/shard_map/reduce_scatter | solution.py:366
  1177.5 436.7 %reduce-scatter.37.cloned.1.call-start = ((), (), s32[]{:S(2)}) async-start(), calls=%async_computation.34 | async-start | bytes 368640 | tf_op jit(solution)/shard_map/reduce_scatter | solution.py:360
  1180.6 497.0 %reduce-scatter.33.cloned.1.call-start = ((), (), s32[]{:S(2)}) async-start(), calls=%async_computation.32 | async-start | bytes 368640 | tf_op jit(solution)/shard_map/reduce_scatter | solution.py:357
  1183.9 557.3 %reduce-scatter.41.cloned.1.call-start = ((), (), s32[]{:S(2)}) async-start(), calls=%async_computation.36 | async-start | bytes 368640 | tf_op jit(solution)/shard_map/reduce_scatter | solution.py:363
  1196.5 608.8 %all-to-all-start.6 = ((bf16[640,4,320]{0,2,1:T(8,128)(2,1)}), bf16[640,4,320]{0,2,1:T(8,128)(2,1)}, u32[]{:S(2)}, u32[]{:S(2)}) async-start(bf16[640,4,320]{0,2,1:T(8,128)(2,1)} %bitcast.366), calls=%async_computation.6 | async-start | bytes 3276800 | tf_op jit(solution)/shard_map/all_to_all | solution.py:302
  1201.0 604.2 %reduce-scatter.29.cloned.1.call-start = ((), (), s32[]{:S(2)}) async-start(), calls=%async_computation.30 | async-start | bytes 368640 | tf_op jit(solution)/shard_map/reduce_scatter | solution.py:354
  1202.6 800.6 %all-reduce.9.cloned.1.call-start = ((), (), s32[]{:S(2)}) async-start(), calls=%async_computation.48 | async-start | bytes 983040 | tf_op jit(solution)/shard_map/psum | solution.py:373
  1898.7 192.0 %reduce-scatter.21.cloned.1.call-start = ((), (), s32[]{:S(2)}) async-start(), calls=%async_computation.26 | async-start | bytes 1105920 | tf_op jit(solution)/shard_map/reduce_scatter | solution.py:348
  2017.2 174.1 %all-reduce.11.cloned.1.call-start = ((), (), s32[]{:S(2)}) async-start(), calls=%async_computation.49 | async-start | bytes 983040 | tf_op jit(solution)/shard_map/psum | solution.py:371
  (135 other events, 3014.9 us)
Sparse Core Ops, SparseCore 0:
  10.8 162.2 all-gather.32
  175.8 157.6 all-gather.40
  336.2 64.4 all-gather.34
  402.7 63.0 all-gather.36
  467.9 83.6 all-gather.38
  553.6 61.7 all-gather.46
  617.6 66.6 all-gather.42
  686.5 63.3 all-gather.44
  1047.1 59.0 reduce-scatter.26
  1109.3 60.2 reduce-scatter.42
  1173.0 60.2 reduce-scatter.38
  1236.4 60.2 reduce-scatter.34
  1300.0 60.3 reduce-scatter.46
  1363.5 60.2 reduce-scatter.30
  1427.0 60.2 reduce-scatter.24
  1490.4 60.2 reduce-scatter.44
  1553.9 60.2 reduce-scatter.36
  1617.3 60.2 reduce-scatter.32
  1680.9 60.2 reduce-scatter.40
  1744.9 60.2 reduce-scatter.28
  1896.0 62.8 reduce-scatter.18
  1962.2 62.3 reduce-scatter.22
  2028.2 62.3 reduce-scatter.20
  2094.0 62.3 reduce-scatter.16
  (2 shorter events, 65.7 us)

commit v2 on v0

v2 whole, which is shorter than its diff:
```python
from functools import partial
import math

import jax
import jax.numpy as jnp
from jax import lax
from jax.experimental import pallas as pl
from jax.experimental.pallas import tpu as pltpu
from jax.sharding import PartitionSpec as P

D = 1280
HEADS = 16
HD = 80
R = 16
LAYERS = 2
PROMPT = 2048
AR = 128
GLEN = 2560
LOG2E = 1.4426950408889634
LN2 = 0.6931471805599453
ROFF = 8
NEG = -1e30
BLOCK = 256
CHUNK = 512
WIDE = D + AR
PART = D + 2 * AR
SIDE = 3 * PART
BF = jnp.bfloat16
F32 = jnp.float32
NN = (((1,), (0,)), ((), ()))
NT = (((1,), (1,)), ((), ()))
VMEM = pl.BlockSpec(memory_space=pltpu.VMEM)
SMEM = pl.BlockSpec(memory_space=pltpu.SMEM)
HBM = pl.BlockSpec(memory_space=pl.ANY)


def dot(left, right, dims=NN):
    return lax.dot_general(left, right, dims, preferred_element_type=F32)


def call(kernel, name, outs, specs, scratch, expected, out_specs=None):
    return pl.pallas_call(
        kernel,
        out_shape=outs,
        in_specs=specs,
        out_specs=tuple(VMEM for _ in outs) if out_specs is None else out_specs,
        scratch_shapes=scratch,
        compiler_params=pltpu.CompilerParams(vmem_limit_bytes=60 << 20),
        cost_estimate=pl.CostEstimate(
            flops=int(expected * 1.15e9), bytes_accessed=1024, transcendentals=0
        ),
        name=name,
    )


def shape(dims, kind=BF):
    return jax.ShapeDtypeStruct(dims, kind)


def sigmoid(v):
    return 1.0 / (1.0 + jnp.exp(-v))


def row_mask(meta, base, count):
    rows = lax.broadcasted_iota(jnp.int32, (count, AR), 0) + base
    lane = lax.broadcasted_iota(jnp.int32, (count, AR), 1)
    chosen = jnp.where(rows < PROMPT, meta[0], jnp.where(rows < meta[3], meta[1], meta[2]))
    low = chosen * R
    return jnp.where((lane >= low) & (lane < low + R), 1.0, 0.0).astype(F32)


def columns_of(ref, at, width):
    return ref if width == ref.shape[1] else ref.at[:, pl.ds(at, width)]


def head_copies(meta, pieces, wq_s, cb_s, sems):
    core, both = meta[5], 3 * AR
    n = len(pieces) // 2
    single = n == 1 and pieces[0].shape[0] == 1
    copies, block_at = [], 0
    for own, other in zip(pieces[:n], pieces[n:]):
        blocks, rows, columns = own.shape
        for block in range(blocks):
            at = 0 if single else pl.multiple_of(meta[ROFF + block_at], math.gcd(rows, 256))
            into = pl.ds(at, rows)
            for source, target in (
                (own.at[block, :, :both], cb_s.at[into, pl.ds(pl.multiple_of(core * both, both), both)]),
                (other.at[block], cb_s.at[into, pl.ds(pl.multiple_of((1 - core) * both, both), both)]),
                (own.at[block, :, both:], wq_s.at[into]),
            ):
                copies.append(pltpu.make_async_copy(source, target, sems.at[len(copies)]))
            block_at += 1
    return copies


def side_copies(meta, own, other, which, r_s, sems):
    half = PART // 2
    return [
        pltpu.make_async_copy(
            columns_of(ref, which * half, half),
            columns_of(r_s, pl.multiple_of(which * PART + side * half, half), half),
            sems.at[which, k],
        )
        for k, (ref, side) in enumerate(((own, meta[5]), (other, 1 - meta[5])))
    ]


def start_all(copies):
    for copy in copies:
        copy.start()
    return copies


def wait_all(copies):
    for copy in copies:
        copy.wait()


def run_copies(copies):
    wait_all(start_all(copies))


def fill_second(meta, cb_s, bd_s, width, group):
    bd_s[...] = jnp.zeros_like(bd_s)
    for p in range(width // group):
        start = pl.multiple_of(meta[4] * width + p * group, math.gcd(group, 256))
        for c in range(3):
            at = (p * 3 + c) * group
            bd_s[at : at + group, c * AR : (c + 1) * AR] = cb_s[
                pl.ds(start, group), (3 + c) * AR : (4 + c) * AR
            ]


def project_kernel(*refs, arrays, pieces, parts, block):
    meta, scale = refs[:2]
    tokens = refs[2 : 2 + arrays]
    weights = refs[2 + arrays : 2 + arrays + pieces]
    heads = refs[2 + arrays + pieces : 2 + arrays + pieces + parts]
    low_out, wq_s, cb_s, bd_s, sems = refs[2 + arrays + pieces + parts :]
    run_copies(head_copies(meta, weights, wq_s, cb_s, sems))
    columns = wq_s.shape[1]
    each = columns // parts
    fill_second(meta, cb_s, bd_s, columns // 3, each // 3)
    for k in range(arrays):
        rows = tokens[k].shape[0]
        local = 0 if arrays == 1 else (meta[5] if k == 0 else 1 - meta[5]) * rows

        def step(i, carry, k=k, local=local):
            x = tokens[k][pl.ds(pl.multiple_of(i * block, 64), block), :]
            place = pl.multiple_of(local + i * block, 64)
            mask = row_mask(meta, meta[7] + place, block)
            low = dot(x, cb_s[:, : 3 * AR]) * jnp.concatenate([mask] * 3, axis=1)
            low = low.astype(BF)
            low_out[pl.ds(place, block), :] = low
            both = ((dot(x, wq_s[...]) + dot(low, bd_s[...], NT)) * scale[...]).astype(BF)
            for p in range(parts):
                heads[p][pl.ds(place, block), :] = both[:, p * each : (p + 1) * each]
            return carry

        lax.fori_loop(0, rows // block, step, 0)


def project(meta, scale, tokens, weights, base, parts):
    arrays = len(tokens)
    rows = tokens[0].shape[0]
    count = rows * arrays
    columns = scale.shape[1]
    return call(
        partial(
            project_kernel, arrays=arrays, pieces=len(weights), parts=parts, block=320
        ),
        "project",
        (shape((count, columns // parts)),) * parts + (shape((count, 3 * AR)),),
        [SMEM, VMEM] + [VMEM] * arrays + [HBM] * len(weights),
        [
            pltpu.VMEM((D, columns), BF),
            pltpu.VMEM((D, 6 * AR), BF),
            pltpu.VMEM((columns, 3 * AR), BF),
            pltpu.SemaphoreType.DMA((3 * sum(w.shape[0] for w in weights),)),
        ],
        13,
    )(meta.at[7].set(base), scale, *tokens, *weights)


def load_rows(meta, sources, target, sems):
    copies = []
    for index, ref in enumerate(sources):
        rows = ref.shape[0]
        if len(sources) == 1:
            into = target
        else:
            into = target.at[pl.ds(pl.multiple_of(meta[6] * rows if index == 0 else (1 - meta[6]) * rows, 256), rows)]
        copies.append(pltpu.make_async_copy(ref, into, sems.at[index]))
    run_copies(copies)


def allowed_pairs(meta, queries, keys, query_at, key_at):
    same = (keys >= meta[3]) | (queries < meta[3])
    causal = keys <= queries
    return causal & same if key_at >= PROMPT else causal


def attend_kernel(*refs, groups, local_heads):
    meta = refs[0]
    sources = refs[1 : 1 + groups]
    out, lse, hs, q_s, k_s, v_s, sems = refs[1 + groups :]
    load_rows(meta, sources, hs, sems)
    width = local_heads * HD
    span = out.shape[2]
    lane = lax.broadcasted_iota(jnp.int32, (BLOCK, 128), 1)
    for h in range(local_heads):
        for i in range(GLEN // BLOCK):
            r = slice(i * BLOCK, (i + 1) * BLOCK)
            for c, ref in ((0, q_s), (1, k_s), (2, v_s)):
                x = hs[r, c * width + h * HD : c * width + (h + 1) * HD]
                fill = jnp.ones if c == 2 else jnp.zeros
                ref[h, r, :] = jnp.concatenate([x, fill((BLOCK, 128 - HD), BF)], axis=1)

    def head(h, carry):
        place = pl.multiple_of(h * HD, 16)
        for i in range(GLEN // BLOCK):
            q0 = i * BLOCK
            nk = q0 + BLOCK
            d0 = min(q0, PROMPT)
            rows = lax.broadcasted_iota(jnp.int32, (BLOCK, nk - d0), 0) + q0
            cols = lax.broadcasted_iota(jnp.int32, (BLOCK, nk - d0), 1) + d0
            qb = q_s[h, q0 : q0 + BLOCK, :]
            sd = jnp.where(
                allowed_pairs(meta, rows, cols, q0, d0), dot(qb, k_s[h, d0:nk, :], NT), NEG
            )
            peak = jnp.max(sd, axis=1, keepdims=True)
            if d0 > 0:
                sp = dot(qb, k_s[h, 0:d0, :], NT)
                peak = jnp.maximum(peak, jnp.max(sp, axis=1, keepdims=True))
            total = dot(jnp.exp2(sd - peak).astype(BF), v_s[h, d0:nk, :])
            if d0 > 0:
                total = total + dot(jnp.exp2(sp - peak).astype(BF), v_s[h, 0:d0, :])
            turned = jnp.where(lane == HD + 1, peak, total).T
            rowsum = turned[HD : HD + 1, :]
            lse[pl.ds(h, 1), q0 : q0 + BLOCK] = turned[HD + 1 : HD + 2, :] + jnp.log2(rowsum)
            result = (turned[:HD, :] * (1.0 / rowsum)).astype(BF)
            for part in range(BLOCK // 128):
                t = q0 + part * 128
                out[t // span, pl.ds(place, HD), t % span : t % span + 128] = result[
                    :, part * 128 : (part + 1) * 128
                ]
        return carry

    lax.fori_loop(0, local_heads, head, 0)


def attend(meta, heads, span):
    width = heads[0].shape[1]
    local_heads = width // (3 * HD)
    return call(
        partial(attend_kernel, groups=len(heads), local_heads=local_heads),
        "attend",
        (shape((GLEN // span, local_heads * HD, span)), shape((8, GLEN), F32)),
        [SMEM] + [HBM] * len(heads),
        [pltpu.VMEM((GLEN, width), BF)]
        + [pltpu.VMEM((local_heads, GLEN, 128), BF)] * 3
        + [pltpu.SemaphoreType.DMA((len(heads),))],
        16,
    )(meta, *heads)


def three_parts(x):
    high = x.astype(BF).astype(F32)
    rest = x - high
    middle = rest.astype(BF).astype(F32)
    return high, middle, (rest - middle).astype(BF).astype(F32)


def attend_back_kernel(*refs, groups, local_heads):
    meta, factor = refs[:2]
    sources = refs[2 : 2 + groups]
    o_ref, do_ref, lse = refs[2 + groups : 5 + groups]
    out, hs, q_s, k_s, v_s, d_s, qt_s, dt_s, kt_s, dqt_s, dq_s, dk_s, dv_s, sems = refs[5 + groups :]
    load_rows(meta, sources, hs, sems)
    width = local_heads * HD
    span = o_ref.shape[2]
    zero_row = lax.broadcasted_iota(jnp.int32, (128 - HD, 128), 0)

    def extra_rows(value):
        a, b, c = three_parts(value)
        return jnp.where(
            zero_row == 0, a, jnp.where(zero_row == 1, b, jnp.where(zero_row == 2, c, 0.0))
        ).astype(BF)

    for h in range(local_heads):
        cs = slice(h * HD, (h + 1) * HD)
        for i in range(GLEN // 128):
            r = slice(i * 128, (i + 1) * 128)
            t, inner = (i * 128) // span, slice((i * 128) % span, (i * 128) % span + 128)
            ones = jnp.ones((128, 128 - HD), BF)
            q = jnp.concatenate([hs[r, h * HD : (h + 1) * HD], jnp.zeros_like(ones)], axis=1)
            q_s[h, r, :] = q
            k_s[h, r, :] = jnp.concatenate(
                [hs[r, width + h * HD : width + (h + 1) * HD], ones], axis=1
            )
            v_s[h, r, :] = jnp.concatenate(
                [hs[r, 2 * width + h * HD : 2 * width + (h + 1) * HD], ones], axis=1
            )
            qt_s[h, :HD, r] = q.T[:HD, :]
            qt_s[h, HD:, r] = extra_rows(-lse[h : h + 1, r])
            do = do_ref[t, cs, inner]
            delta = jnp.sum(do.astype(F32) * o_ref[t, cs, inner].astype(F32), axis=0, keepdims=True)
            dt = jnp.concatenate([do, extra_rows(-delta)], axis=0)
            dt_s[h, :, r] = dt
            d_s[h, r, :] = dt.T

    def head(h, carry):
        for i in range(GLEN // BLOCK):
            kt_s[:, i * BLOCK : (i + 1) * BLOCK] = k_s[h, i * BLOCK : (i + 1) * BLOCK, :].T
        for j in range(GLEN // BLOCK):
            k0 = j * BLOCK
            kb = k_s[h, k0 : k0 + BLOCK, :]
            vb = v_s[h, k0 : k0 + BLOCK, :]
            dk = jnp.zeros((BLOCK, 128), F32)
            dv = jnp.zeros((BLOCK, 128), F32)
            q0 = k0
            while q0 < GLEN:
                n = BLOCK if q0 == k0 else min(CHUNK, GLEN - q0)
                qs = slice(q0, q0 + n)
                probs = jnp.exp2(dot(kb, qt_s[h, :, qs]))
                if q0 == k0 or k0 >= PROMPT:
                    keys = lax.broadcasted_iota(jnp.int32, (BLOCK, n), 0) + k0
                    queries = lax.broadcasted_iota(jnp.int32, (BLOCK, n), 1) + q0
                    probs = jnp.where(allowed_pairs(meta, queries, keys, q0, k0), probs, 0.0)
                dscore = (probs * dot(vb, dt_s[h, :, qs])).astype(BF)
                dv = dv + dot(probs.astype(BF), d_s[h, qs, :])
                dk = dk + dot(dscore, q_s[h, qs, :])
                dq = dot(kt_s[:, k0 : k0 + BLOCK], dscore)
                if j == 0:
                    dqt_s[:, qs] = dq
                else:
                    dqt_s[:, qs] += dq
                q0 += n
            dk_s[h, k0 : k0 + BLOCK, :] = (dk * LN2).astype(BF)
            dv_s[h, k0 : k0 + BLOCK, :] = dv.astype(BF)
        for i in range(GLEN // BLOCK):
            r = slice(i * BLOCK, (i + 1) * BLOCK)
            dq_s[h, r, :] = (dqt_s[:, r].T * factor[...]).astype(BF)
        return carry

    lax.fori_loop(0, local_heads, head, 0)
    for i in range(GLEN // BLOCK):
        r = slice(i * BLOCK, (i + 1) * BLOCK)
        out[r, :] = jnp.concatenate(
            [ref[h, r, :HD] for ref in (dq_s, dk_s, dv_s) for h in range(local_heads)], axis=1
        )


def attend_back(meta, factor, heads, mixed, grad_mixed, lse):
    width = heads[0].shape[1]
    local_heads = width // (3 * HD)
    rows = pltpu.VMEM((local_heads, GLEN, 128), BF)
    turned = pltpu.VMEM((local_heads, 128, GLEN), BF)
    return call(
        partial(attend_back_kernel, groups=len(heads), local_heads=local_heads),
        "attend_back",
        (shape((GLEN, width)),),
        [SMEM, VMEM] + [HBM] * len(heads) + [VMEM] * 3,
        [pltpu.VMEM((GLEN, width), BF)]
        + [rows] * 4
        + [turned] * 2
        + [pltpu.VMEM((128, GLEN), BF), pltpu.VMEM((128, GLEN), F32)]
        + [rows] * 3
        + [pltpu.SemaphoreType.DMA((len(heads),))],
        0.05,
    )(meta, factor, *heads, mixed, grad_mixed, lse)[0]


def rms_of(value):
    return lax.rsqrt(jnp.mean(value * value, axis=-1, keepdims=True) + 1e-06)


def feed_kernel(*refs, parts, pieces, block, last):
    meta, gain_mlp, gain_next, hidden_in = refs[:4]
    mixed = refs[4 : 4 + parts]
    weights = refs[4 + parts : 4 + parts + pieces]
    refs = refs[4 + parts + pieces :]
    middle_out, inner_out, low_out, result = refs[:4]
    normed_out = None if last else refs[4]
    hidden, middle_s, inner_s, r_s, mt_s, mx_s, sems, io_sems = refs[4 if last else 5 :]
    rows = hidden.shape[0]
    loads, slot = [], 0
    for p in range(parts):
        sources, group, _ = mixed[p].shape
        for source in range(sources):
            at = (source * parts + p) * group
            loads.append(
                pltpu.make_async_copy(
                    mixed[p].at[source], mt_s.at[at : at + group], io_sems.at[len(loads)]
                )
            )
    start_all(loads)
    load_hidden = pltpu.make_async_copy(hidden_in, hidden, io_sems.at[len(loads)])
    load_hidden.start()
    copies = [start_all(side_copies(meta, *weights, which, r_s, sems)) for which in range(3)]
    wait_all(loads)
    for i in range(0, rows, 128):
        n = min(128, rows - i)
        mx_s[i : i + n, :] = mt_s[:, i : i + n].T
    load_hidden.wait()

    def stage(which, body):
        wait_all(copies[which])

        def step(i, carry):
            r = pl.ds(pl.multiple_of(i * block, 64), block)
            mask = row_mask(meta, meta[4] * rows + i * block, block)

            def adapted(x):
                both = dot(x, r_s[:, which * PART : which * PART + WIDE])
                low = (both[:, D:] * mask).astype(BF)
                low_out[r, which * AR : (which + 1) * AR] = low
                return both[:, :D] + dot(low, r_s[:, which * PART + WIDE : (which + 1) * PART], NT)

            body(r, adapted)
            return carry

        lax.fori_loop(0, rows // block, step, 0)

    def out_stage(r, adapted):
        middle_s[r, :] = hidden[r, :] + adapted(mx_s[r, :])

    def in_stage(r, adapted):
        middle = middle_s[r, :]
        inner_s[r, :] = adapted((middle * rms_of(middle) * gain_mlp[...]).astype(BF))

    def down_stage(r, adapted):
        inner = inner_s[r, :]
        value = middle_s[r, :] + adapted((inner * sigmoid(inner)).astype(BF))
        result[r, :] = value.astype(result.dtype)
        if not last:
            normed_out[r, :] = (value * rms_of(value) * gain_next[...]).astype(BF)

    stage(0, out_stage)
    store_middle = pltpu.make_async_copy(middle_s, middle_out, io_sems.at[len(loads) + 1])
    store_middle.start()
    stage(1, in_stage)
    store_inner = pltpu.make_async_copy(inner_s, inner_out, io_sems.at[len(loads) + 2])
    store_inner.start()
    stage(2, down_stage)
    store_middle.wait()
    store_inner.wait()


def feed(meta, gain_mlp, gain_next, mixed, hidden, weights, last):
    rows = hidden.shape[0]
    row = pltpu.VMEM((rows, D), F32)
    outs = (shape((rows, D), F32), shape((rows, D), F32), shape((rows, 3 * AR)))
    outs += (shape((rows, D), BF),) if last else (shape((rows, D), F32), shape((rows, D), BF))
    return call(
        partial(
            feed_kernel,
            parts=len(mixed),
            pieces=2,
            block=math.gcd(rows, 320),
            last=last,
        ),
        "feed",
        outs,
        [SMEM] + [VMEM] * 2 + [HBM] * (1 + len(mixed) + 2),
        [
            row,
            row,
            row,
            pltpu.VMEM((D, SIDE), BF),
            pltpu.VMEM((D, rows), BF),
            pltpu.VMEM((rows, D), BF),
            pltpu.SemaphoreType.DMA((3, 2)),
            pltpu.SemaphoreType.DMA((sum(m.shape[0] for m in mixed) + 3,)),
        ],
        17,
        out_specs=(HBM, HBM) + (VMEM,) * (len(outs) - 2),
    )(meta, gain_mlp, gain_next, hidden, *mixed, *weights)


def rms_back(grad, value, gain, grad_normed):
    r = rms_of(value)
    e = gain * grad_normed
    return grad + r * e - value * (r * r * r) * jnp.mean(value * e, axis=-1, keepdims=True)


def feed_back_kernel(*refs, parts, pieces, block):
    meta, gain_mlp, grad_hbm, middle_hbm, inner_hbm = refs[:5]
    weights = refs[5 : 5 + pieces]
    refs = refs[5 + pieces :]
    grad_out, gi_s, gm_s, dl_s, il_s = refs[:5]
    mixed_grad = refs[5 : 5 + parts]
    grad_in, middle_s, inner_s, r_s, sems, io_sems = refs[5 + parts :]
    rows = grad_in.shape[0]
    loads = start_all(
        [
            pltpu.make_async_copy(source, target, io_sems.at[k])
            for k, (source, target) in enumerate(
                ((grad_hbm, grad_in), (inner_hbm, inner_s), (middle_hbm, middle_s))
            )
        ]
    )
    copies = {which: start_all(side_copies(meta, *weights, which, r_s, sems)) for which in (2, 1, 0)}

    def rows_of(i):
        return pl.ds(pl.multiple_of(i * block, 64), block)

    def narrow(g, which, i):
        mask = row_mask(meta, meta[4] * rows + i * block, block)
        return (dot(g, r_s[:, which * PART + WIDE : (which + 1) * PART]) * mask).astype(BF)

    def across(g, low, which):
        both = jnp.concatenate([g, low], axis=1)
        return dot(both, r_s[:, which * PART : which * PART + WIDE], NT)

    def down_stage(i, carry):
        r = rows_of(i)
        gl = grad_in[r, :].astype(BF)
        dl = narrow(gl, 2, i)
        dl_s[r, :] = dl
        inner = inner_s[r, :]
        s = sigmoid(inner)
        gi_s[r, :] = (across(gl, dl, 2) * (s * (1.0 + inner * (1.0 - s)))).astype(BF)
        return carry

    def in_stage(i, carry):
        r = rows_of(i)
        gi = gi_s[r, :]
        il = narrow(gi, 1, i)
        il_s[r, :] = il
        grad = rms_back(grad_in[r, :].astype(F32), middle_s[r, :], gain_mlp[...], across(gi, il, 1))
        grad_out[r, :] = grad
        gm_s[r, :D] = grad.astype(BF)
        return carry

    def out_stage(i, carry):
        r = rows_of(i)
        gm_s[r, D:] = narrow(gm_s[r, :D], 0, i)
        return carry

    wait_all(copies[2])
    loads[0].wait()
    loads[1].wait()
    lax.fori_loop(0, rows // block, down_stage, 0)
    wait_all(copies[1])
    loads[2].wait()
    lax.fori_loop(0, rows // block, in_stage, 0)
    wait_all(copies[0])
    lax.fori_loop(0, rows // block, out_stage, 0)
    sources, group, _ = mixed_grad[0].shape
    for source in range(sources):
        for p in range(parts):
            at = (source * parts + p) * group
            mixed_grad[p][source] = dot(r_s[at : at + group, :WIDE], gm_s[...], NT).astype(BF)


def feed_back(meta, gain_mlp, grad, middle, inner, weights, parts, sources):
    rows = grad.shape[0]
    narrow = shape((rows, AR))
    return call(
        partial(
            feed_back_kernel,
            parts=parts,
            pieces=2,
            block=math.gcd(rows, 320),
        ),
        "feed_back",
        (shape((rows, D), F32), shape((rows, D)), shape((rows, WIDE)), narrow, narrow)
        + (shape((sources, D // sources // parts, rows)),) * parts,
        [SMEM, VMEM] + [HBM] * (3 + 2),
        [
            pltpu.VMEM((rows, D), grad.dtype),
            pltpu.VMEM((rows, D), F32),
            pltpu.VMEM((rows, D), F32),
            pltpu.VMEM((D, SIDE), BF),
            pltpu.SemaphoreType.DMA((3, 2)),
            pltpu.SemaphoreType.DMA((3,)),
        ],
        0.05,
    )(meta, gain_mlp, grad, middle, inner, *weights)


def feed_sums_kernel(*refs, parts):
    gain_mlp, grad, middle_ref, inner_ref, gi, gm, dl, il, low = refs[:9]
    mixed = refs[9 : 9 + parts]
    sums = refs[9 + parts]
    for p in range(parts):
        sources, group, _ = mixed[p].shape
        for source in range(sources):
            at = (source * parts + p) * group
            sums[at : at + group, :AR] = dot(mixed[p][source], gm[:, D:]).astype(BF)
    inner = inner_ref[...]
    act = (inner * sigmoid(inner)).astype(BF)
    middle = middle_ref[...]
    nf = (middle * rms_of(middle) * gain_mlp[...]).astype(BF)
    pairs = (
        (1, low[:, :AR], gm[:, :D]),
        (2, il[...], nf),
        (3, low[:, AR : 2 * AR], gi[...]),
        (4, dl[...], act),
        (5, low[:, 2 * AR :], grad[...].astype(BF)),
    )
    for slot, few, wide in pairs:
        turned = few.T
        for i in range(0, D, BLOCK):
            part = dot(turned, wide[:, i : i + BLOCK])
            sums[i : i + BLOCK, slot * AR : (slot + 1) * AR] = part.T.astype(BF)


def feed_sums(gain_mlp, grad, middle, inner, gi, gm, dl, il, low, mixed):
    return call(
        partial(feed_sums_kernel, parts=len(mixed)),
        "feed_sums",
        (shape((D, 6 * AR)),),
        [VMEM] * (9 + len(mixed)),
        [],
        0.05,
    )(gain_mlp, grad, middle, inner, gi, gm, dl, il, low, *mixed)[0]


def norm_back_kernel(gain, grad, hidden, *refs, cut):
    total = refs[0][...].astype(F32)
    out = refs[-1]
    for ref in refs[1 : -3 if cut else -1]:
        total = total + ref[...].astype(F32)
    if cut:
        first = pl.program_id(0) < cut
        total = total + jnp.where(first, refs[-3][...], refs[-2][...]).astype(F32)
    out[...] = rms_back(grad[...], hidden[...], gain[...], total)


def norm_back(gain, grad, hidden, terms):
    rows = grad.shape[0]
    block = math.gcd(rows, 128)
    cut = terms[-2].shape[0] // block if terms[-1].shape[0] < rows else 0
    row = pl.BlockSpec((block, D), lambda i: (i, 0))
    specs = [row] * (2 + len(terms))
    if cut:
        specs[-2] = pl.BlockSpec((block, D), lambda i: (jnp.minimum(i, cut - 1), 0))
        specs[-1] = pl.BlockSpec((block, D), lambda i: (jnp.maximum(i - cut, 0), 0))
    return pl.pallas_call(
        partial(norm_back_kernel, cut=cut),
        grid=(rows // block,),
        out_shape=shape((rows, D), F32),
        in_specs=[pl.BlockSpec((1, D), lambda i: (0, 0))] + specs,
        out_specs=row,
        cost_estimate=pl.CostEstimate(flops=int(5e7), bytes_accessed=1024, transcendentals=0),
        name="norm_back",
    )(gain, grad, hidden, *terms)


def project_back_kernel(*refs, arrays, pieces, parts, block, mode):
    meta = refs[0]
    grads = refs[1 : 1 + parts]
    weights = refs[1 + parts : 1 + parts + pieces]
    refs = refs[1 + parts + pieces :]
    if mode == "own":
        lora_in, refs = refs[0], refs[1:]
    outs, refs = refs[:arrays], refs[arrays:]
    if mode != "own":
        lora_out, refs = refs[0], refs[1:]
    if mode == "far":
        lora_own, refs = refs[0], refs[1:]
    wq_s, cb_s, bd_s = refs[:3]
    g_s = refs[3 : 3 + parts]
    sems, row_sems = refs[3 + parts :]
    count = g_s[0].shape[0]
    rows_at = pl.ds(pl.multiple_of(meta[7], 256), count)
    loads = start_all(
        [
            pltpu.make_async_copy(
                grads[p] if count == GLEN else grads[p].at[rows_at], g_s[p], row_sems.at[p]
            )
            for p in range(parts)
        ]
    )
    copies = start_all(head_copies(meta, weights, wq_s, cb_s, sems))
    wait_all(copies)
    wait_all(loads)
    columns = wq_s.shape[1]
    each = columns // parts
    fill_second(meta, cb_s, bd_s, columns // 3, each // 3)
    base = meta[7] if mode == "far" else 0

    def rows_of(place):
        at = pl.ds(pl.multiple_of(base + place, 64), block)
        return jnp.concatenate([g_s[p][at, :] for p in range(parts)], axis=1)

    def narrow(g, place):
        mask = row_mask(meta, meta[7] + place, block)
        return (dot(g, bd_s[...]) * jnp.concatenate([mask] * 3, axis=1)).astype(BF)

    for k in range(arrays):
        rows = outs[k].shape[0]
        local = 0 if arrays == 1 else (meta[5] if k == 0 else 1 - meta[5]) * rows

        def step(i, carry, k=k, local=local):
            place = pl.multiple_of(local + i * block, 64)
            g = rows_of(place)
            if mode == "own":
                lora = lora_in[pl.ds(place, block), :]
            else:
                lora = narrow(g, place)
                lora_out[pl.ds(place, block), :] = lora
            outs[k][pl.ds(pl.multiple_of(i * block, 64), block), :] = (
                dot(g, wq_s[...], NT) + dot(lora, cb_s[:, : 3 * AR], NT)
            ).astype(BF)
            return carry

        lax.fori_loop(0, rows // block, step, 0)
    if mode == "far":
        half = GLEN // 2
        own = half - meta[7]

        def own_step(i, carry):
            place = pl.multiple_of(i * block, 64)
            at = pl.multiple_of(own + place, 64)
            g = jnp.concatenate([g_s[p][pl.ds(at, block), :] for p in range(parts)], axis=1)
            mask = row_mask(meta, at, block)
            lora_own[pl.ds(place, block), :] = (
                dot(g, bd_s[...]) * jnp.concatenate([mask] * 3, axis=1)
            ).astype(BF)
            return carry

        lax.fori_loop(0, half // block, own_step, 0)


def project_back(meta, grads, weights, base, arrays, rows, mode, lora=None):
    columns = sum(g.shape[1] for g in grads)
    count = rows * arrays
    low = (shape((count, 3 * AR)),)
    held = count if mode == "own" else GLEN
    return call(
        partial(
            project_back_kernel,
            arrays=arrays,
            pieces=len(weights),
            parts=len(grads),
            block=320,
            mode=mode,
        ),
        "project_back",
        tuple(shape((rows, D)) for _ in range(arrays)) + low * {"own": 0, "far": 2, "all": 1}[mode],
        [SMEM] + [HBM] * (len(grads) + len(weights)) + [VMEM] * (mode == "own"),
        [
            pltpu.VMEM((D, columns), BF),
            pltpu.VMEM((D, 6 * AR), BF),
            pltpu.VMEM((columns, 3 * AR), BF),
        ]
        + [pltpu.VMEM((held, g.shape[1]), BF) for g in grads]
        + [
            pltpu.SemaphoreType.DMA((3 * sum(w.shape[0] for w in weights),)),
            pltpu.SemaphoreType.DMA((len(grads),)),
        ],
        0.05,
    )(meta.at[7].set(base), *grads, *weights, *(() if lora is None else (lora,)))


def project_sums_kernel(*refs, parts, groups, arrays):
    meta = refs[0]
    grads = refs[1 : 1 + parts]
    lows = refs[1 + parts : 1 + parts + groups]
    loras = refs[1 + parts + groups : 1 + parts + 2 * groups]
    tokens = refs[1 + parts + 2 * groups : 1 + parts + 2 * groups + groups * arrays]
    sums, turned = refs[1 + parts + 2 * groups + groups * arrays :]
    sections = []
    for index in range(groups):
        for k in range(arrays):
            ref = tokens[index * arrays + k]
            rows = ref.shape[0]
            at = 0 if arrays == 1 else (meta[5] if k == 0 else 1 - meta[5]) * rows
            slot = index * arrays + k
            turned[slot] = loras[index][pl.ds(at if arrays == 1 else pl.multiple_of(at, 64), rows), :].T
            sections.append((slot, ref))
    for i in range(0, D, BLOCK):
        total = None
        for slot, ref in sections:
            piece = dot(turned[slot], ref[:, i : i + BLOCK])
            total = piece if total is None else total + piece
        sums[i : i + BLOCK, : 3 * AR] = total.T.astype(BF)
    sums[:, 3 * AR :] = jnp.zeros((D, 3 * AR), BF)
    each = grads[0].shape[1]
    group = each // 3
    for c in range(3):
        few = [low[:, c * AR : (c + 1) * AR].T for low in lows]
        for p in range(parts):
            total = None
            for index in range(groups):
                rows = lows[index].shape[0]
                if groups == 1:
                    at = pl.ds(0, rows)
                else:
                    chip = meta[6] if index == 0 else 1 - meta[6]
                    at = pl.ds(pl.multiple_of(chip * rows, 256), rows)
                piece = dot(few[index], grads[p][at, c * group : (c + 1) * group])
                total = piece if total is None else total + piece
            own = pl.multiple_of(meta[4] * group * parts + p * group, math.gcd(group, 256))
            sums[pl.ds(own, group), (3 + c) * AR : (4 + c) * AR] = total.T.astype(BF)


def project_sums(meta, grads, lows, loras, tokens):
    flat = [t for arrays in tokens for t in arrays]
    rows = flat[0].shape[0]
    return call(
        partial(
            project_sums_kernel, parts=len(grads), groups=len(lows), arrays=len(tokens[0])
        ),
        "project_sums",
        (shape((D, 6 * AR)),),
        [SMEM] + [VMEM] * (len(grads) + 2 * len(lows) + len(flat)),
        [pltpu.VMEM((len(flat), 3 * AR, rows), BF)],
        0.05,
    )(meta, *grads, *lows, *loras, *flat)[0]


def swap(value, axis, count, step):
    return lax.ppermute(value, axis, [(i, i ^ step) for i in range(count)])


def fence(*values):
    return lax.optimization_barrier(values)


def after(value, *earlier):
    return lax.optimization_barrier((value, *earlier))[0]


def reduce_quarter(value, core, chip, seq_count, fsdp_count):
    def halves(v, index, step):
        v = v.reshape(fsdp_count, 2, v.shape[1] // 2, v.shape[2])
        keep = jnp.where(index == 0, v[:, 0], v[:, 1])
        give = jnp.where(index == 0, v[:, 1], v[:, 0])
        return (keep.astype(F32) + swap(give, "seq", seq_count, step).astype(F32)).astype(BF)

    value = value.reshape(fsdp_count, value.shape[0] // fsdp_count, value.shape[1])
    return halves(halves(value, core, 1), chip, 2)


def owned(value):
    return lax.all_to_all(value, "fsdp", split_axis=0, concat_axis=0, tiled=True)


def reduce_owner(value, core, chip, seq_count):
    def join(v, index, step):
        far = swap(v, "seq", seq_count, step)
        return jnp.where(index == 0, jnp.concatenate([v, far]), jnp.concatenate([far, v]))

    value = jnp.sum(value.astype(F32), axis=0).astype(BF)
    return join(join(value, chip, 2), core, 1)


def reduce_rows(value):
    return lax.psum_scatter(value, "fsdp", scatter_dimension=0, tiled=True)


def local(
    tokens,
    cont_lengths,
    adapter_ids,
    attn_gain,
    mlp_gain,
    query_scale,
    w_qkv,
    output_weight,
    inward_weight,
    down_weight,
    projection_first_factor,
    b_qkv,
    output_first_factor,
    output_second_factor,
    inward_first_factor,
    inward_second_factor,
    down_first_factor,
    down_second_factor,
    cotangent,
    seq_count,
    fsdp_count,
):
    rows = tokens.shape[1]
    shard = w_qkv.shape[1]
    width = D // seq_count
    paired = seq_count == 4
    place = lax.axis_index("seq")
    core = place % 2
    chip = place // 2 if paired else place * 0
    span = rows if rows % 128 == 0 else GLEN
    meta = jnp.concatenate(
        [
            adapter_ids[0],
            PROMPT + cont_lengths[0, :1],
            jnp.stack([place, core, chip, place * 0]),
        ]
    ).astype(jnp.int32)

    parts = 2 if paired else 1
    group = width // parts

    def heads_part(layer):
        return jnp.concatenate(
            [
                lax.dynamic_slice(
                    w_qkv, (layer, 0, c * D + place * width + p * group), (1, shard, group)
                )[0]
                for p in range(parts)
                for c in range(3)
            ],
            axis=1,
        )

    def both_part(layer):
        turned = jnp.concatenate([b_qkv[layer, c].T for c in range(3)], axis=1)
        return jnp.where(core == 0, projection_first_factor[layer], turned)

    def side_part(layer):
        whole = jnp.concatenate(
            [
                output_weight[layer],
                output_first_factor[layer],
                output_second_factor[layer].T,
                inward_weight[layer],
                inward_first_factor[layer],
                inward_second_factor[layer].T,
                down_weight[layer],
                down_first_factor[layer],
                down_second_factor[layer].T,
            ],
            axis=1,
        )
        half = PART // 2
        return jnp.where(
            core == 0,
            jnp.concatenate([whole[:, k * PART : k * PART + half] for k in range(3)], axis=1),
            jnp.concatenate([whole[:, k * PART + half : (k + 1) * PART] for k in range(3)], axis=1),
        )

    def gathered(value):
        return lax.all_gather(value, "fsdp", axis=0, tiled=True)

    def other_core(own, columns):
        return swap(own[:, :columns], "seq", seq_count, 1)

    def to_rows(mixed):
        if span != rows:
            mixed = mixed[0].reshape(group, seq_count, rows).transpose(1, 0, 2)
        return lax.all_to_all(mixed, "seq", split_axis=0, concat_axis=0, tiled=True)

    def to_heads(value):
        value = lax.all_to_all(value, "seq", split_axis=0, concat_axis=0, tiled=True)
        if span != rows:
            value = value.transpose(1, 0, 2).reshape(1, group, GLEN)
        return value

    both = 3 * AR
    head_weights, side_weights, kept = [], [], []

    def gather_head(layer, *earlier):
        value = jnp.concatenate([both_part(layer), heads_part(layer)], axis=1)
        return gathered(after(value, *earlier) if earlier else value)

    head_gathered = gather_head(0)
    side_gathered = gathered(after(side_part(0), head_gathered))
    hidden = tokens[0].astype(F32)
    normed = (hidden * rms_of(hidden) * attn_gain[0]).astype(BF)
    if paired:
        far = swap(normed, "seq", seq_count, 2)
        head_gathered, far = fence(head_gathered, far)
    for layer in range(LAYERS):
        last = layer == LAYERS - 1
        factor = 1.442695041 / math.sqrt(HD) * jax.nn.softplus(query_scale[layer])
        tiled = jnp.concatenate([jnp.tile(factor * LOG2E, group // HD), jnp.ones((2 * group,), F32)])
        scale = jnp.tile(tiled, parts).reshape(1, 3 * width)
        if layer > 0 and paired:
            far = swap(normed, "seq", seq_count, 2)
            head_gathered, far = fence(head_gathered, far)
        head_weights.append((head_gathered[None], other_core(head_gathered, both)[None]))
        if layer > 0:
            side_gathered = gathered(after(side_part(layer), head_gathered))
        if paired:
            own = ([normed, swap(normed, "seq", seq_count, 1)], chip * 2 * rows)
            projected = [project(meta, scale, own[0], head_weights[layer], own[1], parts)]
            far = after(far, projected[0][-1])
            far = ([far, swap(far, "seq", seq_count, 1)], (1 - chip) * 2 * rows)
            projected.append(project(meta, scale, far[0], head_weights[layer], far[1], parts))
            groups = [own, far]
        else:
            groups = [([lax.all_gather(normed, "seq", axis=0, tiled=True)], place * 0)]
            projected = [project(meta, scale, groups[0][0], head_weights[layer], place * 0, parts)]
        heads = [[p[k] for p in projected] for k in range(parts)]
        attended, mixed = [], []
        for p in range(parts):
            inputs = heads[p] if p == 0 else [after(h, attended[-1][1]) for h in heads[p]]
            attended.append(attend(meta, inputs, span))
            if p < parts - 1:
                mixed.append(to_rows(attended[-1][0]))
        attended, mixed = fence(attended, mixed)
        side_gathered = after(side_gathered, attended[-1][1])
        mixed = mixed + [to_rows(attended[-1][0])]
        side_weights.append((side_gathered, other_core(side_gathered, SIDE // 2)))
        if not last:
            head_gathered = gather_head(layer + 1, attended[-1][1], side_gathered)
        results = feed(
            meta,
            mlp_gain[layer][None],
            attn_gain[(layer + 1) % LAYERS][None],
            mixed,
            hidden,
            side_weights[layer],
            last,
        )
        kept.append(
            (hidden, groups, heads, [p[-1] for p in projected], attended, mixed, factor)
            + tuple(results[:3])
        )
        if last:
            layer_output = results[3]
        else:
            hidden, normed = results[3:]

    grad = cotangent[0]
    sums = [None] * LAYERS
    for layer in reversed(range(LAYERS)):
        hidden, groups, heads, lows, attended, mixed, factor, middle, inner, low = kept[layer]
        gain = mlp_gain[layer][None]
        grad_in = grad
        results = feed_back(
            meta, gain, grad_in, middle, inner, side_weights[layer], parts, seq_count
        )
        results = fence(*results)
        grad, gi, gm, dl, il = results[:5]
        mixed_grads = [to_heads(results[5])]
        side_sum = feed_sums(gain, grad_in, middle, inner, gi, gm, dl, il, low, mixed)
        mixed_grads, side_sum = fence(mixed_grads, side_sum)
        side_total = reduce_rows(side_sum)
        if layer == 0 and paired:
            side_reduced = after(side_total, sums[1][1])
            side_reduced = lax.psum(side_reduced, "seq")
            sums[1] = tuple(lax.psum(v, "seq") for v in sums[1])
        factor_row = jnp.pad(factor, (0, 128 - HD)).reshape(1, 128)
        head_grads = []
        for p in range(parts):
            if p < parts - 1:
                mixed_grads.append(to_heads(after(results[6 + p], side_sum)))
            head_grads.append(
                attend_back(meta, factor_row, heads[p], attended[p][0], mixed_grads[p], attended[p][1])
            )
            head_grads, mixed_grads = fence(head_grads, mixed_grads)
        if paired:
            own, far = groups
            far_back = project_back(
                meta, head_grads, head_weights[layer], far[1], 2, rows, "far"
            )
            far_sum = (
                far_back[0].astype(F32) + swap(far_back[1], "seq", seq_count, 1).astype(F32)
            ).astype(BF)
            if layer > 0:
                far_sum, head_grads, side_total = fence(far_sum, head_grads, side_total)
            else:
                far_sum, head_grads = fence(far_sum, head_grads)
            loras = [far_back[3], far_back[2]]
            cut = rows * 3 // 5
            crossed = swap(far_sum[:cut], "seq", seq_count, 2)
            head_sum = project_sums(meta, head_grads, lows, loras, [g[0] for g in groups])
            if layer == 0:
                side_total = side_reduced
            head_sum, crossed, head_grads, rest, sums[1], side_total = fence(
                head_sum, crossed, head_grads, far_sum[cut:], sums[1], side_total
            )
            if layer > 0:
                head_total = reduce_rows(head_sum)
                rest = swap(rest, "seq", seq_count, 2)
            else:
                head_total = reduce_quarter(head_sum, core, chip, seq_count, fsdp_count)
            own_back = project_back(
                meta, head_grads, head_weights[layer], own[1], 2, rows, "own", loras[0]
            )
            if layer > 0:
                own_back, rest = fence(own_back, rest)
            else:
                own_back, head_total, rest = fence(own_back, head_total, rest)
                rest = swap(rest, "seq", seq_count, 2)
                head_total = owned(head_total)
                head_total, rest = fence(head_total, rest)
                head_total = reduce_owner(head_total, core, chip, seq_count)
            near = swap(own_back[1], "seq", seq_count, 1)
            sums[layer] = (side_total, head_total)
            terms = [own_back[0], near, crossed, rest]
        else:
            back = project_back(
                meta, head_grads, head_weights[layer], place * 0, 1, GLEN, "all"
            )
            terms = [lax.psum_scatter(back[0], "seq", scatter_dimension=0, tiled=True)]
            head_sum = project_sums(meta, head_grads, lows, [back[1]], [g[0] for g in groups])
            sums[layer] = tuple(lax.psum(v, "seq") for v in (side_total, reduce_rows(head_sum)))
        grad = norm_back(attn_gain[layer][None], grad, hidden, terms)

    side = jnp.stack([s[0] for s in sums]).astype(F32)
    head = jnp.stack([s[1] for s in sums]).astype(F32)

    def columns(slot):
        return side[:, :, slot * AR : (slot + 1) * AR]

    return (
        layer_output[None],
        grad[None],
        head[:, :, : 3 * AR],
        head[:, :, 3 * AR :].reshape(LAYERS, shard, 3, AR).transpose(0, 2, 3, 1),
        columns(0),
        columns(1).transpose(0, 2, 1),
        columns(2),
        columns(3).transpose(0, 2, 1),
        columns(4),
        columns(5).transpose(0, 2, 1),
    )


def solution(mesh):
    rows = P("fsdp", "seq", None)
    first = P(None, "fsdp", None)
    second = P(None, None, "fsdp")
    return jax.shard_map(
        partial(local, seq_count=mesh.shape["seq"], fsdp_count=mesh.shape["fsdp"]),
        mesh=mesh,
        in_specs=(
            rows,
            P("fsdp", None),
            P("fsdp", None),
            P(),
            P(),
            P(),
            first,
            first,
            first,
            first,
            first,
            P(None, None, None, "fsdp"),
            first,
            second,
            first,
            second,
            first,
            second,
            rows,
        ),
        out_specs=(
            rows,
            rows,
            first,
            P(None, None, None, "fsdp"),
            first,
            second,
            first,
            second,
            first,
            second,
        ),
        check_vma=False,
    )
```

time: 2830 us -> 793 us (0.28)
  matrix products: 815 us -> 0 us
  blocking collectives: 548 us -> 16.7 us
  Pallas kernels: 0 us -> 442 us
  local copies, waits for them, and re-layouts: 436 us -> 36.6 us
  waiting for transfers between devices: 571 us -> 213 us
  other arithmetic: 352 us -> 15.9 us
  loops' own time: 41 us -> 0 us
    dot_general x134 -> x0, matrix products: 815 us -> none  [the longest x10 146 us: one_block(): jnp.einsum('qhd,khd->hqk', grad_block, value_heads, preferred_element_typ...]
    all_gather x16 -> x0, blocking collectives: 548 us -> none  [the longest x2 76 us: local(): lax.all_gather(projection_first_factor[layer_index], 'fsdp', axis=0, tile...]
    pallas_call x0 -> x26, Pallas kernels: none -> 442 us  [the longest x4 115 us: attend_back(): call(partial(attend_back_kernel, groups=len(heads), local_heads=local_hea...]
    reduce_scatter x16 -> x3, waiting for transfers between devices: 354 us -> 0.02 us  [reduce_rows(): return lax.psum_scatter(value, 'fsdp', scatter_dimension=0, tiled=True)]
    convert_element_type x18 -> x8, other arithmetic: 210 us -> 9.81 us  [the longest x2 3.76 us: local(): far_sum = (far_back[0].astype(F32) + swap(far_back[1], 'seq', seq_count,...]
    while x124 -> x0, local copies, waits for them, and re-layouts: 100 us -> none
    all_to_all x8, waiting for transfers between devices: 103 us -> 15.3 us  [the longest x3 10 us: to_rows(): return lax.all_to_all(mixed, 'seq', split_axis=0, concat_axis=0, tiled=True)]
    ppermute x0 -> x22, waiting for transfers between devices: none -> 82.2 us  [swap(): return lax.ppermute(value, axis, [(i, i ^ step) for i in range(count)])]
  transfers between devices with their start and end apart: 34 -> 38, of which waited for: 12 -> 24; matrix products, arithmetic and copies ran while one was open for 36% -> 4% of each run, Pallas kernels for 0% -> 51%
where the time goes in v2:
time: 793 us; the launch traced here: 784 us
  Pallas kernels  442 us (56%)
  waiting for transfers between devices  213 us (27%)
  starting transfers between devices  44.6 us (6%)
  local copies, waits for them, and re-layouts  36.6 us (5%)
  blocking collectives  16.7 us (2%)
  other arithmetic  15.9 us (2%)
  between operations  15.3 us (2%)
    pallas_call x4, Pallas kernels, attend_back(): call(partial(attend_back_kernel, groups=len(heads), local_heads=local_hea...  115 us
    all_gather x4, waiting for transfers between devices, gathered(): return lax.all_gather(value, 'fsdp', axis=0, tiled=True)  109 us
    ppermute x22, waiting for transfers between devices, swap(): return lax.ppermute(value, axis, [(i, i ^ step) for i in range(count)])  82.2 us
    pallas_call x4, Pallas kernels, attend(): call(partial(attend_kernel, groups=len(heads), local_heads=local_heads),...  78.2 us
    pallas_call x4, Pallas kernels, project_back(): call(partial(project_back_kernel, arrays=arrays, pieces=len(weights), par...  58.5 us
    pallas_call x4, Pallas kernels, project(): call(partial(project_kernel, arrays=arrays, pieces=len(weights), parts=pa...  55.5 us
    pallas_call x2, Pallas kernels, feed(): call(partial(feed_kernel, parts=len(mixed), pieces=2, block=math.gcd(rows...  39.2 us
    pallas_call x2, Pallas kernels, feed_back(): call(partial(feed_back_kernel, parts=parts, pieces=2, block=math.gcd(rows...  38.5 us
  transfers between devices with their start and end apart: 38, of which 24 were waited for; matrix products, arithmetic and copies ran while one was open for 4% of the time, Pallas kernels for 51%

profile of v2, /device:TPU:0, one launch (start us, length us, event | category | flops | bytes accessed | tf_op | source)
XLA Modules:
  0.0 783.8 jit_solution(2797625934043504334)
XLA Ops:
  22.8 58.7 %all-gather.5.cloned.1.call-done = bf16[1280,1344]{1,0:T(8,128)(2,1)} async-done(((bf16[160,1344]{1,0:T(8,128)(2,1)}), bf16[1280,1344]{1,0:T(8,128)(2,1)}) %all-gather.5.cloned.1.call-update) | async-done | bytes 3440656 | tf_op jit(solution)/shard_map/all_gather | solution.py:937
  86.9 14.2 %project.4 = (bf16[1280,480]{1,0:T(8,128)(2,1)}, bf16[1280,480]{1,0:T(8,128)(2,1)}, bf16[1280,384]{1,0:T(8,128)(2,1)}) custom-call(s32[8]{0:T(128)} %copy-done.54, f32[1,960]{1,0:T(1,128)} %reshape_tile.6.refs_1_, bf16[640,1280]{1,0:T(8,128)(2,1)} %copy-done.2, bf16[640,1280]{1,0:T(8,128)(2,1)} %collective-permute-done.refs_3_.refs_8_, ...), custom_call_target="tpu_custom_call" | custom-call | flops 14949999616 | bytes 1024 | tf_op jit(solution)/shard_map/project/pallas_call | solution.py:168
  106.1 13.7 %project.5 = (bf16[1280,480]{1,0:T(8,128)(2,1)}, bf16[1280,480]{1,0:T(8,128)(2,1)}, bf16[1280,384]{1,0:T(8,128)(2,1)}) custom-call(s32[8]{0:T(128)} %copy-done.55, f32[1,960]{1,0:T(1,128)} %reshape_tile.6.refs_1_, bf16[640,1280]{1,0:T(8,128)(2,1)} %collective-permute-done.1.refs_2_.refs_9_, bf16[640,1280]{1,0:T(8,128)(2,1)} %copy-done.14, ...), custom_call_target="tpu_custom_call" | custom-call | flops 14949999616 | bytes 1024 | tf_op jit(solution)/shard_map/project/pallas_call | solution.py:168
  119.9 27.2 %attend.4 = (bf16[4,160,640]{2,1,0:T(8,128)(2,1)}, f32[8,2560]{1,0:T(8,128)}) custom-call(s32[8]{0:T(128)} %copy-done.49, bf16[1280,480]{1,0:T(8,128)(2,1)} %get-tuple-element.208.refs_1_.refs_2_, bf16[1280,480]{1,0:T(8,128)(2,1)} %get-tuple-element.212.refs_2_.refs_3_), custom_call_target="tpu_custom_call" | custom-call | flops 18400000000 | bytes 1024 | tf_op jit(solution)/shard_map/attend/pallas_call | solution.py:255
  150.7 17.1 %attend.5 = (bf16[4,160,640]{2,1,0:T(8,128)(2,1)}, f32[8,2560]{1,0:T(8,128)}) custom-call(s32[8]{0:T(128)} %copy-done.49, bf16[1280,480]{1,0:T(8,128)(2,1)} %get-tuple-element.216.refs_1_.refs_2_, bf16[1280,480]{1,0:T(8,128)(2,1)} %get-tuple-element.218.refs_2_.refs_3_), custom_call_target="tpu_custom_call" | custom-call | flops 18400000000 | bytes 1024 | tf_op jit(solution)/shard_map/attend/pallas_call | solution.py:255
  195.2 20.6 %feed.2 = (f32[640,1280]{1,0:T(8,128)}, f32[640,1280]{1,0:T(8,128)}, bf16[640,384]{1,0:T(8,128)(2,1)}, f32[640,1280]{1,0:T(8,128)}, bf16[640,1280]{1,0:T(8,128)(2,1)}) custom-call(s32[8]{0:T(128)} %copy-done.49, f32[1,1280]{1,0:T(1,128)} %get-tuple-element.394.refs_1_.refs_0_, f32[1,1280]{1,0:T(1,128)} %get-tuple-element.392.refs_2_.gain, ...), custom_call_target="tpu_custom_call" | custom-call | flops 19549999104 | bytes 1024 | tf_op jit(solution)/shard_map/feed/pallas_call | solution.py:455
  217.5 26.6 %all-gather.9.cloned.1.call-done = bf16[1280,1344]{1,0:T(8,128)(2,1)} async-done(((bf16[160,1344]{1,0:T(8,128)(2,1)}), bf16[1280,1344]{1,0:T(8,128)(2,1)}) %all-gather.9.cloned.1.call-update) | async-done | bytes 3440656 | tf_op jit(solution)/shard_map/all_gather | solution.py:937
  260.7 13.8 %project.6 = (bf16[1280,480]{1,0:T(8,128)(2,1)}, bf16[1280,480]{1,0:T(8,128)(2,1)}, bf16[1280,384]{1,0:T(8,128)(2,1)}) custom-call(s32[8]{0:T(128)} %copy-done.54, f32[1,960]{1,0:T(1,128)} %reshape_tile.7.refs_1_, bf16[640,1280]{1,0:T(8,128)(2,1)} %get-tuple-element.227.refs_2_.refs_7_, bf16[640,1280]{1,0:T(8,128)(2,1)} %collective-permute-done.5.refs_3_.refs_8_, ...), custom_call_target="tpu_custom_call" | custom-call | flops 14949999616 | bytes 1024 | tf_op jit(solution)/shard_map/project/pallas_call | solution.py:168
  279.3 13.8 %project.7 = (bf16[1280,480]{1,0:T(8,128)(2,1)}, bf16[1280,480]{1,0:T(8,128)(2,1)}, bf16[1280,384]{1,0:T(8,128)(2,1)}) custom-call(s32[8]{0:T(128)} %copy-done.55, f32[1,960]{1,0:T(1,128)} %reshape_tile.7.refs_1_, bf16[640,1280]{1,0:T(8,128)(2,1)} %copy-done.15, bf16[640,1280]{1,0:T(8,128)(2,1)} %copy-done.17, bf16[1,1280,1344]{2,1,0:T(8,128)(2,1)} %bitcast.221, ...), custom_call_target="tpu_custom_call" | custom-call | flops 14949999616 | bytes 1024 | tf_op jit(solution)/shard_map/project/pallas_call | solution.py:168
  293.0 17.1 %attend.6 = (bf16[4,160,640]{2,1,0:T(8,128)(2,1)}, f32[8,2560]{1,0:T(8,128)}) custom-call(s32[8]{0:T(128)} %copy-done.49, bf16[1280,480]{1,0:T(8,128)(2,1)} %get-tuple-element.230.refs_1_.refs_2_, bf16[1280,480]{1,0:T(8,128)(2,1)} %get-tuple-element.234.refs_2_.refs_3_), custom_call_target="tpu_custom_call" | custom-call | flops 18400000000 | bytes 1024 | tf_op jit(solution)/shard_map/attend/pallas_call | solution.py:255
  313.6 16.9 %attend.7 = (bf16[4,160,640]{2,1,0:T(8,128)(2,1)}, f32[8,2560]{1,0:T(8,128)}) custom-call(s32[8]{0:T(128)} %copy-done.49, bf16[1280,480]{1,0:T(8,128)(2,1)} %get-tuple-element.238.refs_1_.refs_2_, bf16[1280,480]{1,0:T(8,128)(2,1)} %get-tuple-element.240.refs_2_.refs_3_), custom_call_target="tpu_custom_call" | custom-call | flops 18400000000 | bytes 1024 | tf_op jit(solution)/shard_map/attend/pallas_call | solution.py:255
  330.6 14.8 %all-gather.11.cloned.1.call-done.refs_6_.refs_5_ = bf16[1280,2304]{1,0:T(8,128)(2,1)} async-done(((bf16[160,2304]{1,0:T(8,128)(2,1)}), bf16[1280,2304]{1,0:T(8,128)(2,1)}) %all-gather.11.cloned.1.call-update) | async-done | bytes 5898256 | tf_op jit(solution)/shard_map/all_gather | solution.py:937
  345.3 16.7 %all_to_all.45.refs_5_.refs_10_ = bf16[4,160,640]{2,1,0:T(8,128)(2,1)} all-to-all(bf16[4,160,640]{2,1,0:T(8,128)(2,1)} %get-tuple-element.244.refs_4_), channel_id=1, replica_groups=mesh['seq'=4,'fsdp'=8] {'seq'}, dimensions={0} | all-to-all | bytes 1638400 | tf_op jit(solution)/shard_map/all_to_all | solution.py:945
  362.0 18.6 %feed.3 = (f32[640,1280]{1,0:T(8,128)}, f32[640,1280]{1,0:T(8,128)}, bf16[640,384]{1,0:T(8,128)(2,1)}, bf16[640,1280]{1,0:T(8,128)(2,1)}) custom-call(s32[8]{0:T(128)} %copy-done.49, f32[1,1280]{1,0:T(1,128)} %get-tuple-element.395.refs_1_.refs_0_, f32[1,1280]{1,0:T(1,128)} %get-tuple-element.393.refs_2_.gain, ...), custom_call_target="tpu_custom_call" | custom-call | flops 19549999104 | bytes 1024 | tf_op jit(solution)/shard_map/feed/pallas_call | solution.py:455
  380.6 18.8 %feed_back.2 = (f32[640,1280]{1,0:T(8,128)}, bf16[640,1280]{1,0:T(8,128)(2,1)}, bf16[640,1408]{1,0:T(8,128)(2,1)}, bf16[640,128]{1,0:T(8,128)(2,1)}, bf16[640,12...) custom-call(s32[8]{0:T(128)} %copy-done.49, ...), custom_call_target="tpu_custom_call" | custom-call | flops 57500000 | bytes 1024 | tf_op jit(solution)/shard_map/feed_back/pallas_call | solution.py:560
  419.9 28.4 %attend_back.4.refs_1_ = bf16[2560,480]{1,0:T(8,128)(2,1)} custom-call(s32[8]{0:T(128)} %copy-done.49, f32[1,128]{1,0:T(1,128)} %pad_bitcast_fusion.1.refs_1_, bf16[1280,480]{1,0:T(8,128)(2,1)} %get-tuple-element.230.refs_1_.refs_2_, bf16[1280,480]{1,0:T(8,128)(2,1)} %get-tuple-element.234.refs_2_.refs_3_, bf16[4,160,640]{2,1,0:T(8,128)(2,1)} %get-tuple-element.252.refs_4_, ...), custom_call_target="tpu_custom_call" | custom-call | flops 57500000 | bytes 1024 | tf_op jit(solution)/shard_map/attend_back/pallas_call | solution.py:359
  449.2 28.9 %attend_back.5.refs_2_ = bf16[2560,480]{1,0:T(8,128)(2,1)} custom-call(s32[8]{0:T(128)} %copy-done.49, f32[1,128]{1,0:T(1,128)} %pad_bitcast_fusion.1.refs_1_, bf16[1280,480]{1,0:T(8,128)(2,1)} %get-tuple-element.238.refs_1_.refs_2_, bf16[1280,480]{1,0:T(8,128)(2,1)} %get-tuple-element.240.refs_2_.refs_3_, bf16[4,160,640]{2,1,0:T(8,128)(2,1)} %get-tuple-element.244.refs_4_, ...), custom_call_target="tpu_custom_call" | custom-call | flops 57500000 | bytes 1024 | tf_op jit(solution)/shard_map/attend_back/pallas_call | solution.py:359
  478.1 17.8 %project_back.4 = (bf16[640,1280]{1,0:T(8,128)(2,1)}, bf16[640,1280]{1,0:T(8,128)(2,1)}, bf16[1280,384]{1,0:T(8,128)(2,1)}, bf16[1280,384]{1,0:T(8,128)(2,1)}) custom-call(s32[8]{0:T(128)} %copy-done.55, bf16[2560,480]{1,0:T(8,128)(2,1)} %attend_back.4.refs_1_, bf16[2560,480]{1,0:T(8,128)(2,1)} %attend_back.5.refs_2_, bf16[1,1280,1344]{2,1,0:T(8,128)(2,1)} %bitcast.222, ...), custom_call_target="tpu_custom_call" | custom-call | flops 57500000 | bytes 1024 | tf_op jit(solution)/shard_map/project_back/pallas_call | solution.py:733
  556.2 19.7 %feed_back.3 = (f32[640,1280]{1,0:T(8,128)}, bf16[640,1280]{1,0:T(8,128)(2,1)}, bf16[640,1408]{1,0:T(8,128)(2,1)}, bf16[640,128]{1,0:T(8,128)(2,1)}, bf16[640,12...) custom-call(s32[8]{0:T(128)} %copy-done.49, ...), custom_call_target="tpu_custom_call" | custom-call | flops 57500000 | bytes 1024 | tf_op jit(solution)/shard_map/feed_back/pallas_call | solution.py:560
  596.3 28.6 %attend_back.6.refs_1_ = bf16[2560,480]{1,0:T(8,128)(2,1)} custom-call(s32[8]{0:T(128)} %copy-done.49, f32[1,128]{1,0:T(1,128)} %pad_bitcast_fusion.refs_1_, bf16[1280,480]{1,0:T(8,128)(2,1)} %get-tuple-element.208.refs_1_.refs_2_, bf16[1280,480]{1,0:T(8,128)(2,1)} %get-tuple-element.212.refs_2_.refs_3_, bf16[4,160,640]{2,1,0:T(8,128)(2,1)} %get-tuple-element.289.refs_4_, ...), custom_call_target="tpu_custom_call" | custom-call | flops 57500000 | bytes 1024 | tf_op jit(solution)/shard_map/attend_back/pallas_call | solution.py:359
  625.8 28.9 %attend_back.7.refs_2_ = bf16[2560,480]{1,0:T(8,128)(2,1)} custom-call(s32[8]{0:T(128)} %copy-done.49, f32[1,128]{1,0:T(1,128)} %pad_bitcast_fusion.refs_1_, bf16[1280,480]{1,0:T(8,128)(2,1)} %get-tuple-element.216.refs_1_.refs_2_, bf16[1280,480]{1,0:T(8,128)(2,1)} %get-tuple-element.218.refs_2_.refs_3_, bf16[4,160,640]{2,1,0:T(8,128)(2,1)} %get-tuple-element.222.refs_4_, ...), custom_call_target="tpu_custom_call" | custom-call | flops 57500000 | bytes 1024 | tf_op jit(solution)/shard_map/attend_back/pallas_call | solution.py:359
  654.7 17.8 %project_back.6 = (bf16[640,1280]{1,0:T(8,128)(2,1)}, bf16[640,1280]{1,0:T(8,128)(2,1)}, bf16[1280,384]{1,0:T(8,128)(2,1)}, bf16[1280,384]{1,0:T(8,128)(2,1)}) custom-call(s32[8]{0:T(128)} %copy-done.55, bf16[2560,480]{1,0:T(8,128)(2,1)} %attend_back.6.refs_1_, bf16[2560,480]{1,0:T(8,128)(2,1)} %attend_back.7.refs_2_, bf16[1,1280,1344]{2,1,0:T(8,128)(2,1)} %bitcast.218, ...), custom_call_target="tpu_custom_call" | custom-call | flops 57500000 | bytes 1024 | tf_op jit(solution)/shard_map/project_back/pallas_call | solution.py:733
  693.4 18.3 %collective-permute-done.15.refs_2_ = bf16[384,1280]{1,0:T(8,128)(2,1)S(1)} collective-permute-done((bf16[384,1280]{1,0:T(8,128)(2,1)}, bf16[384,1280]{1,0:T(8,128)(2,1)S(1)}, u32[]{:S(2)}, u32[]{:S(2)}) %collective-permute-start.15) | collective-permute-done | bytes 983072 | tf_op jit(solution)/shard_map/ppermute | solution.py:817
  745.3 14.6 %collective-permute-done.19.refs_3_ = bf16[256,1280]{1,0:T(8,128)(2,1)S(1)} collective-permute-done((bf16[256,1280]{1,0:T(8,128)(2,1)S(1)}, bf16[256,1280]{1,0:T(8,128)(2,1)S(1)}, u32[]{:S(2)}, u32[]{:S(2)}) %collective-permute-start.19) | collective-permute-done | bytes 655392 | tf_op jit(solution)/shard_map/ppermute | solution.py:817
  (268 shorter events, 257.2 us)
Async XLA Ops:
  7.2 74.4 %all-gather.5.cloned.1.call-start = ((), (), s32[]{:S(2)}) async-start(), calls=%async_computation.12 | async-start | bytes 4055040 | tf_op jit(solution)/shard_map/all_gather | solution.py:937
  12.7 164.3 %all-gather.7.cloned.1.call-start = ((), (), s32[]{:S(2)}) async-start(), calls=%async_computation.13 | async-start | bytes 6635520 | tf_op jit(solution)/shard_map/all_gather | solution.py:937
  14.2 67.4 %collective-permute-start.1 = (bf16[640,1280]{1,0:T(8,128)(2,1)S(1)}, bf16[640,1280]{1,0:T(8,128)(2,1)}, u32[]{:S(2)}, u32[]{:S(2)}) collective-permute-start(bf16[640,1280]{1,0:T(8,128)(2,1)S(1)} %multiply_convert_fusion.refs_2_.refs_7_), channel_id=1, source_target_pairs={{0,16},{8,24},{16,0},{24,8},{1,17},{9,25},{17,1},{25,9},{2,18},{10... | collective-permute-start | bytes 4915208 | tf_op jit(solution)/shard_map/ppermute | solution.py:817
  147.0 20.7 %all-to-all-start = ((bf16[4,160,640]{2,1,0:T(8,128)(2,1)}), bf16[4,160,640]{2,1,0:T(8,128)(2,1)S(1)}, u32[]{:S(2)}, u32[]{:S(2)}) async-start(bf16[4,160,640]{2,1,0:T(8,128)(2,1)} %get-tuple-element.289.refs_4_), calls=%async_computation | async-start | bytes 1638400 | tf_op jit(solution)/shard_map/all_to_all | solution.py:945
  150.6 93.4 %all-gather.9.cloned.1.call-start = ((), (), s32[]{:S(2)}) async-start(), calls=%async_computation.14 | async-start | bytes 4055040 | tf_op jit(solution)/shard_map/all_gather | solution.py:937
  177.0 17.2 %collective-permute-start.4 = (bf16[1280,2304]{1,0:T(8,128)(2,1)}, bf16[1280,2304]{1,0:T(8,128)(2,1)}, u32[]{:S(2)}, u32[]{:S(2)}) collective-permute-start(bf16[1280,2304]{1,0:T(8,128)(2,1)} %all-gather.7.cloned.1.call-done.refs_6_.refs_5_), channel_id=1, source_target_pairs={{0,8},{8,0},{16,24},{24,16},{1,9},{9,1},{17,25},{25,17},{2,10},{10... | collective-permute-start | bytes 17694728 | tf_op jit(solution)/shard_map/ppermute | solution.py:817
  182.3 163.1 %all-gather.11.cloned.1.call-start = ((), (), s32[]{:S(2)}) async-start(), calls=%async_computation.15 | async-start | bytes 6635520 | tf_op jit(solution)/shard_map/all_gather | solution.py:937
  215.8 37.7 %collective-permute-start.6 = (bf16[640,1280]{1,0:T(8,128)(2,1)}, bf16[640,1280]{1,0:T(8,128)(2,1)S(1)}, u32[]{:S(2)}, u32[]{:S(2)}) collective-permute-start(bf16[640,1280]{1,0:T(8,128)(2,1)} %get-tuple-element.227.refs_2_.refs_7_), channel_id=1, source_target_pairs={{0,16},{8,24},{16,0},{24,8},{1,17},{9,25},{17,1},{25,9},{2,18},{10... | collective-permute-start | bytes 4915208 | tf_op jit(solution)/shard_map/ppermute | solution.py:817
  310.1 20.4 %all-to-all-start.2 = ((bf16[4,160,640]{2,1,0:T(8,128)(2,1)}), bf16[4,160,640]{2,1,0:T(8,128)(2,1)S(1)}, u32[]{:S(2)}, u32[]{:S(2)}) async-start(bf16[4,160,640]{2,1,0:T(8,128)(2,1)} %get-tuple-element.252.refs_4_), calls=%async_computation.2 | async-start | bytes 1638400 | tf_op jit(solution)/shard_map/all_to_all | solution.py:945
  345.3 16.7 %collective-permute-start.9 = (bf16[1280,2304]{1,0:T(8,128)(2,1)}, bf16[1280,2304]{1,0:T(8,128)(2,1)}, u32[]{:S(2)}, u32[]{:S(2)}) collective-permute-start(bf16[1280,2304]{1,0:T(8,128)(2,1)} %all-gather.11.cloned.1.call-done.refs_6_.refs_5_), channel_id=1, source_target_pairs={{0,8},{8,0},{16,24},{24,16},{1,9},{9,1},{17,25},{25,17},{2,10},{10... | collective-permute-start | bytes 17694728 | tf_op jit(solution)/shard_map/ppermute | solution.py:817
  399.4 15.5 %all-to-all-start.4 = ((bf16[4,160,640]{2,1,0:T(8,128)(2,1)}), bf16[4,160,640]{2,1,0:T(8,128)(2,1)S(1)}, u32[]{:S(2)}, u32[]{:S(2)}) async-start(bf16[4,160,640]{2,1,0:T(8,128)(2,1)} %get-tuple-element.253), calls=%async_computation.4 | async-start | bytes 1638400 | tf_op jit(solution)/shard_map/all_to_all | solution.py:948
  402.9 98.7 %reduce-scatter.4.cloned.1.call-start = ((), (), s32[]{:S(2)}) async-start(), calls=%async_computation.16 | async-start | bytes 2211840 | tf_op jit(solution)/shard_map/reduce_scatter | solution.py:853
  415.8 32.5 %all-to-all-start.5 = ((bf16[4,160,640]{2,1,0:T(8,128)(2,1)}), bf16[4,160,640]{2,1,0:T(8,128)(2,1)S(1)}, u32[]{:S(2)}, u32[]{:S(2)}) async-start(bf16[4,160,640]{2,1,0:T(8,128)(2,1)} %get-tuple-element.263), calls=%async_computation.5 | async-start | bytes 1638400 | tf_op jit(solution)/shard_map/all_to_all | solution.py:948
  419.3 261.8 %reduce-scatter.6.cloned.1.call-start = ((), (), s32[]{:S(2)}) async-start(), calls=%async_computation.17 | async-start | bytes 2211840 | tf_op jit(solution)/shard_map/reduce_scatter | solution.py:853
  502.7 24.2 %collective-permute-start.11 = (bf16[384,1280]{1,0:T(8,128)(2,1)}, bf16[384,1280]{1,0:T(8,128)(2,1)S(1)}, u32[]{:S(2)}, u32[]{:S(2)}) collective-permute-start(bf16[384,1280]{1,0:T(8,128)(2,1)} %slice.300), channel_id=1, source_target_pairs={{0,16},{8,24},{16,0},{24,8},{1,17},{9,25},{17,1},{25,9},{2,18},{10... | collective-permute-start | bytes 2949128 | tf_op jit(solution)/shard_map/ppermute | solution.py:817
  527.0 16.3 %collective-permute-start.12 = (bf16[256,1280]{1,0:T(8,128)(2,1)S(1)}, bf16[256,1280]{1,0:T(8,128)(2,1)S(1)}, u32[]{:S(2)}, u32[]{:S(2)}) collective-permute-start(bf16[256,1280]{1,0:T(8,128)(2,1)S(1)} %copy-done.28), channel_id=1, source_target_pairs={{0,16},{8,24},{16,0},{24,8},{1,17},{9,25},{17,1},{25,9},{2,18},{10... | collective-permute-start | bytes 1966088 | tf_op jit(solution)/shard_map/ppermute | solution.py:817
  575.9 15.5 %all-to-all-start.6 = ((bf16[4,160,640]{2,1,0:T(8,128)(2,1)}), bf16[4,160,640]{2,1,0:T(8,128)(2,1)S(1)}, u32[]{:S(2)}, u32[]{:S(2)}) async-start(bf16[4,160,640]{2,1,0:T(8,128)(2,1)} %get-tuple-element.290), calls=%async_computation.7 | async-start | bytes 1638400 | tf_op jit(solution)/shard_map/all_to_all | solution.py:948
  579.4 101.7 %reduce-scatter.8.cloned.1.call-start = ((), (), s32[]{:S(2)}) async-start(), calls=%async_computation.18 | async-start | bytes 2211840 | tf_op jit(solution)/shard_map/reduce_scatter | solution.py:853
  592.3 32.7 %all-to-all-start.7 = ((bf16[4,160,640]{2,1,0:T(8,128)(2,1)}), bf16[4,160,640]{2,1,0:T(8,128)(2,1)S(1)}, u32[]{:S(2)}, u32[]{:S(2)}) async-start(bf16[4,160,640]{2,1,0:T(8,128)(2,1)} %get-tuple-element.300), calls=%async_computation.8 | async-start | bytes 1638400 | tf_op jit(solution)/shard_map/all_to_all | solution.py:948
  595.8 122.0 %all-reduce.7.cloned.1.call-start = ((), (), s32[]{:S(2)}) async-start(), calls=%async_computation.19 | async-start | bytes 1474560 | tf_op jit(solution)/shard_map/psum | solution.py:1037
  679.2 32.5 %collective-permute-start.15 = (bf16[384,1280]{1,0:T(8,128)(2,1)}, bf16[384,1280]{1,0:T(8,128)(2,1)S(1)}, u32[]{:S(2)}, u32[]{:S(2)}) collective-permute-start(bf16[384,1280]{1,0:T(8,128)(2,1)} %slice.302), channel_id=1, source_target_pairs={{0,16},{8,24},{16,0},{24,8},{1,17},{9,25},{17,1},{25,9},{2,18},{10... | collective-permute-start | bytes 2949128 | tf_op jit(solution)/shard_map/ppermute | solution.py:817
  739.2 20.7 %all-to-all-start.8 = ((bf16[8,40,768]{2,1,0:T(8,128)(2,1)}), bf16[8,40,768]{2,1,0:T(8,128)(2,1)S(1)}, u32[]{:S(2)}, u32[]{:S(2)}) async-start(bf16[8,40,768]{2,1,0:T(8,128)(2,1)} %fusion.8), calls=%async_computation.11 | async-start | bytes 983040 | tf_op jit(solution)/shard_map/all_to_all | solution.py:840
  744.1 15.7 %collective-permute-start.19 = (bf16[256,1280]{1,0:T(8,128)(2,1)S(1)}, bf16[256,1280]{1,0:T(8,128)(2,1)S(1)}, u32[]{:S(2)}, u32[]{:S(2)}) collective-permute-start(bf16[256,1280]{1,0:T(8,128)(2,1)S(1)} %copy-done.27), channel_id=1, source_target_pairs={{0,16},{8,24},{16,0},{24,8},{1,17},{9,25},{17,1},{25,9},{2,18},{10... | collective-permute-start | bytes 1966088 | tf_op jit(solution)/shard_map/ppermute | solution.py:817
  745.3 22.4 %collective-permute-start.18 = (bf16[640,1280]{1,0:T(8,128)(2,1)}, bf16[640,1280]{1,0:T(8,128)(2,1)S(1)}, u32[]{:S(2)}, u32[]{:S(2)}) collective-permute-start(bf16[640,1280]{1,0:T(8,128)(2,1)} %get-tuple-element.323), channel_id=1, source_target_pairs={{0,8},{8,0},{16,24},{24,16},{1,9},{9,1},{17,25},{25,17},{2,10},{10... | collective-permute-start | bytes 4915208 | tf_op jit(solution)/shard_map/ppermute | solution.py:817
  (72 other events, 916.2 us)
Sparse Core Ops, SparseCore 0:
  12.8 68.6 all-gather.4
  84.3 92.6 all-gather.6
  179.8 64.1 all-gather.8
  253.6 91.6 all-gather.10
  415.1 64.0 reduce-scatter.3
  527.1 65.3 reduce-scatter.5
  596.0 65.5 reduce-scatter.7
  681.2 36.4 all-reduce.6

commit v3 on v2

--- a/solution.py
+++ b/solution.py
@@ -86,9 +86,10 @@
             for source, target in (
                 (own.at[block, :, :both], cb_s.at[into, pl.ds(pl.multiple_of(core * both, both), both)]),
                 (other.at[block], cb_s.at[into, pl.ds(pl.multiple_of((1 - core) * both, both), both)]),
-                (own.at[block, :, both:], wq_s.at[into]),
+                (own.at[block, :, both:], None if wq_s is None else wq_s.at[into]),
             ):
-                copies.append(pltpu.make_async_copy(source, target, sems.at[len(copies)]))
+                if target is not None:
+                    copies.append(pltpu.make_async_copy(source, target, sems.at[len(copies)]))
             block_at += 1
     return copies
 
@@ -200,10 +201,22 @@
     return causal & same if key_at >= PROMPT else causal
 
 
+def three_parts(x):
+    high = x.astype(BF).astype(F32)
+    rest = x - high
+    middle = rest.astype(BF).astype(F32)
+    return high, middle, (rest - middle).astype(BF).astype(F32)
+
+
+def with_parts(base, place, value):
+    a, b, c = three_parts(value)
+    return jnp.where(place == 0, a, jnp.where(place == 1, b, jnp.where(place == 2, c, base)))
+
+
 def attend_kernel(*refs, groups, local_heads):
     meta = refs[0]
     sources = refs[1 : 1 + groups]
-    out, lse, hs, q_s, k_s, v_s, sems = refs[1 + groups :]
+    out, saved, hs, q_s, k_s, v_s, sems, out_sems = refs[1 + groups :]
     load_rows(meta, sources, hs, sems)
     width = local_heads * HD
     span = out.shape[2]
@@ -213,8 +226,14 @@
             r = slice(i * BLOCK, (i + 1) * BLOCK)
             for c, ref in ((0, q_s), (1, k_s), (2, v_s)):
                 x = hs[r, c * width + h * HD : c * width + (h + 1) * HD]
-                fill = jnp.ones if c == 2 else jnp.zeros
+                fill = jnp.ones if c > 0 else jnp.zeros
                 ref[h, r, :] = jnp.concatenate([x, fill((BLOCK, 128 - HD), BF)], axis=1)
+    stores = [
+        pltpu.make_async_copy(ref, saved.at[c], out_sems.at[c])
+        for c, ref in ((0, q_s), (1, k_s), (2, v_s))
+    ]
+    stores[1].start()
+    stores[2].start()
 
     def head(h, carry):
         place = pl.multiple_of(h * HD, 16)
@@ -235,10 +254,10 @@
             total = dot(jnp.exp2(sd - peak).astype(BF), v_s[h, d0:nk, :])
             if d0 > 0:
                 total = total + dot(jnp.exp2(sp - peak).astype(BF), v_s[h, 0:d0, :])
-            turned = jnp.where(lane == HD + 1, peak, total).T
-            rowsum = turned[HD : HD + 1, :]
-            lse[pl.ds(h, 1), q0 : q0 + BLOCK] = turned[HD + 1 : HD + 2, :] + jnp.log2(rowsum)
-            result = (turned[:HD, :] * (1.0 / rowsum)).astype(BF)
+            lse = peak + jnp.log2(total[:, HD : HD + 1])
+            q_s[h, q0 : q0 + BLOCK, :] = with_parts(qb.astype(F32), lane - HD, -lse).astype(BF)
+            turned = total.T
+            result = (turned[:HD, :] * (1.0 / turned[HD : HD + 1, :])).astype(BF)
             for part in range(BLOCK // 128):
                 t = q0 + part * 128
                 out[t // span, pl.ds(place, HD), t % span : t % span + 128] = result[
@@ -247,6 +266,8 @@
         return carry
 
     lax.fori_loop(0, local_heads, head, 0)
+    stores[0].start()
+    wait_all(stores)
 
 
 def attend(meta, heads, span):
@@ -255,61 +276,40 @@
     return call(
         partial(attend_kernel, groups=len(heads), local_heads=local_heads),
         "attend",
-        (shape((GLEN // span, local_heads * HD, span)), shape((8, GLEN), F32)),
+        (shape((GLEN // span, local_heads * HD, span)), shape((3, local_heads, GLEN, 128))),
         [SMEM] + [HBM] * len(heads),
         [pltpu.VMEM((GLEN, width), BF)]
         + [pltpu.VMEM((local_heads, GLEN, 128), BF)] * 3
-        + [pltpu.SemaphoreType.DMA((len(heads),))],
+        + [pltpu.SemaphoreType.DMA((len(heads),)), pltpu.SemaphoreType.DMA((3,))],
         16,
+        out_specs=(VMEM, HBM),
     )(meta, *heads)
 
 
-def three_parts(x):
-    high = x.astype(BF).astype(F32)
-    rest = x - high
-    middle = rest.astype(BF).astype(F32)
-    return high, middle, (rest - middle).astype(BF).astype(F32)
-
-
-def attend_back_kernel(*refs, groups, local_heads):
-    meta, factor = refs[:2]
-    sources = refs[2 : 2 + groups]
-    o_ref, do_ref, lse = refs[2 + groups : 5 + groups]
-    out, hs, q_s, k_s, v_s, d_s, qt_s, dt_s, kt_s, dqt_s, dq_s, dk_s, dv_s, sems = refs[5 + groups :]
-    load_rows(meta, sources, hs, sems)
+def attend_back_kernel(meta, factor, saved, o_ref, do_ref, out, q_s, k_s, v_s, dt_s, kt_s, dqt_s, sems):
+    local_heads = saved.shape[1]
     width = local_heads * HD
     span = o_ref.shape[2]
-    zero_row = lax.broadcasted_iota(jnp.int32, (128 - HD, 128), 0)
-
-    def extra_rows(value):
-        a, b, c = three_parts(value)
-        return jnp.where(
-            zero_row == 0, a, jnp.where(zero_row == 1, b, jnp.where(zero_row == 2, c, 0.0))
-        ).astype(BF)
-
+    loads = [
+        start_all(
+            [
+                pltpu.make_async_copy(saved.at[c, h], ref.at[h], sems.at[c, h])
+                for c, ref in ((0, q_s), (1, k_s), (2, v_s))
+            ]
+        )
+        for h in range(local_heads)
+    ]
+    extra = lax.broadcasted_iota(jnp.int32, (128 - HD, 128), 0)
     for h in range(local_heads):
         cs = slice(h * HD, (h + 1) * HD)
         for i in range(GLEN // 128):
-            r = slice(i * 128, (i + 1) * 128)
             t, inner = (i * 128) // span, slice((i * 128) % span, (i * 128) % span + 128)
-            ones = jnp.ones((128, 128 - HD), BF)
-            q = jnp.concatenate([hs[r, h * HD : (h + 1) * HD], jnp.zeros_like(ones)], axis=1)
-            q_s[h, r, :] = q
-            k_s[h, r, :] = jnp.concatenate(
-                [hs[r, width + h * HD : width + (h + 1) * HD], ones], axis=1
-            )
-            v_s[h, r, :] = jnp.concatenate(
-                [hs[r, 2 * width + h * HD : 2 * width + (h + 1) * HD], ones], axis=1
-            )
-            qt_s[h, :HD, r] = q.T[:HD, :]
-            qt_s[h, HD:, r] = extra_rows(-lse[h : h + 1, r])
             do = do_ref[t, cs, inner]
             delta = jnp.sum(do.astype(F32) * o_ref[t, cs, inner].astype(F32), axis=0, keepdims=True)
-            dt = jnp.concatenate([do, extra_rows(-delta)], axis=0)
-            dt_s[h, :, r] = dt
-            d_s[h, r, :] = dt.T
-
-    def head(h, carry):
+            dt_s[h, :HD, i * 128 : (i + 1) * 128] = do
+            dt_s[h, HD:, i * 128 : (i + 1) * 128] = with_parts(0.0, extra, -delta).astype(BF)
+    for h in range(local_heads):
+        wait_all(loads[h])
         for i in range(GLEN // BLOCK):
             kt_s[:, i * BLOCK : (i + 1) * BLOCK] = k_s[h, i * BLOCK : (i + 1) * BLOCK, :].T
         for j in range(GLEN // BLOCK):
@@ -322,13 +322,13 @@
             while q0 < GLEN:
                 n = BLOCK if q0 == k0 else min(CHUNK, GLEN - q0)
                 qs = slice(q0, q0 + n)
-                probs = jnp.exp2(dot(kb, qt_s[h, :, qs]))
+                probs = jnp.exp2(dot(kb, q_s[h, qs, :], NT))
                 if q0 == k0 or k0 >= PROMPT:
                     keys = lax.broadcasted_iota(jnp.int32, (BLOCK, n), 0) + k0
                     queries = lax.broadcasted_iota(jnp.int32, (BLOCK, n), 1) + q0
                     probs = jnp.where(allowed_pairs(meta, queries, keys, q0, k0), probs, 0.0)
                 dscore = (probs * dot(vb, dt_s[h, :, qs])).astype(BF)
-                dv = dv + dot(probs.astype(BF), d_s[h, qs, :])
+                dv = dv + dot(probs.astype(BF), dt_s[h, :, qs], NT)
                 dk = dk + dot(dscore, q_s[h, qs, :])
                 dq = dot(kt_s[:, k0 : k0 + BLOCK], dscore)
                 if j == 0:
@@ -336,39 +336,29 @@
                 else:
                     dqt_s[:, qs] += dq
                 q0 += n
-            dk_s[h, k0 : k0 + BLOCK, :] = (dk * LN2).astype(BF)
-            dv_s[h, k0 : k0 + BLOCK, :] = dv.astype(BF)
-        for i in range(GLEN // BLOCK):
-            r = slice(i * BLOCK, (i + 1) * BLOCK)
-            dq_s[h, r, :] = (dqt_s[:, r].T * factor[...]).astype(BF)
-        return carry
-
-    lax.fori_loop(0, local_heads, head, 0)
-    for i in range(GLEN // BLOCK):
-        r = slice(i * BLOCK, (i + 1) * BLOCK)
-        out[r, :] = jnp.concatenate(
-            [ref[h, r, :HD] for ref in (dq_s, dk_s, dv_s) for h in range(local_heads)], axis=1
-        )
-
-
-def attend_back(meta, factor, heads, mixed, grad_mixed, lse):
-    width = heads[0].shape[1]
-    local_heads = width // (3 * HD)
+            r = slice(k0, k0 + BLOCK)
+            out[r, width + h * HD : width + (h + 1) * HD] = (dk[:, :HD] * LN2).astype(BF)
+            out[r, 2 * width + h * HD : 2 * width + (h + 1) * HD] = dv[:, :HD].astype(BF)
+            out[r, h * HD : (h + 1) * HD] = (dqt_s[:, r].T * factor[...]).astype(BF)[:, :HD]
+
+
+def attend_back(meta, factor, saved, mixed, grad_mixed):
+    local_heads = saved.shape[1]
     rows = pltpu.VMEM((local_heads, GLEN, 128), BF)
-    turned = pltpu.VMEM((local_heads, 128, GLEN), BF)
     return call(
-        partial(attend_back_kernel, groups=len(heads), local_heads=local_heads),
+        attend_back_kernel,
         "attend_back",
-        (shape((GLEN, width)),),
-        [SMEM, VMEM] + [HBM] * len(heads) + [VMEM] * 3,
-        [pltpu.VMEM((GLEN, width), BF)]
-        + [rows] * 4
-        + [turned] * 2
-        + [pltpu.VMEM((128, GLEN), BF), pltpu.VMEM((128, GLEN), F32)]
-        + [rows] * 3
-        + [pltpu.SemaphoreType.DMA((len(heads),))],
+        (shape((GLEN, 3 * local_heads * HD)),),
+        [SMEM, VMEM, HBM] + [VMEM] * 2,
+        [rows] * 3
+        + [
+            pltpu.VMEM((local_heads, 128, GLEN), BF),
+            pltpu.VMEM((128, GLEN), BF),
+            pltpu.VMEM((128, GLEN), F32),
+            pltpu.SemaphoreType.DMA((3, local_heads)),
+        ],
         0.05,
-    )(meta, factor, *heads, mixed, grad_mixed, lse)[0]
+    )(meta, factor, saved, mixed, grad_mixed)[0]
 
 
 def rms_of(value):
@@ -484,14 +474,34 @@
     return grad + r * e - value * (r * r * r) * jnp.mean(value * e, axis=-1, keepdims=True)
 
 
-def feed_back_kernel(*refs, parts, pieces, block):
+def feed_back_kernel(*refs, parts, pieces, block, terms):
     meta, gain_mlp, grad_hbm, middle_hbm, inner_hbm = refs[:5]
     weights = refs[5 : 5 + pieces]
     refs = refs[5 + pieces :]
+    if terms:
+        gain_next, hidden_hbm, term_hbm = refs[0], refs[1], refs[2 : 2 + terms]
+        refs = refs[2 + terms :]
     grad_out, gi_s, gm_s, dl_s, il_s = refs[:5]
     mixed_grad = refs[5 : 5 + parts]
-    grad_in, middle_s, inner_s, r_s, sems, io_sems = refs[5 + parts :]
+    refs = refs[5 + parts :]
+    if terms:
+        gl_out, refs = refs[0], refs[1:]
+    grad_in, middle_s, inner_s, r_s, sems, io_sems = refs[:6]
     rows = grad_in.shape[0]
+    early = []
+    if terms:
+        hidden_s, term_s, term_sems = refs[6], refs[7 : 7 + terms - 1], refs[7 + terms - 1]
+        early.append(pltpu.make_async_copy(hidden_hbm, hidden_s, term_sems.at[terms]))
+        for k in range(terms - 2):
+            early.append(pltpu.make_async_copy(term_hbm[k], term_s[k], term_sems.at[k]))
+        cut = term_hbm[-2].shape[0]
+        early.append(
+            pltpu.make_async_copy(term_hbm[-2], term_s[-1].at[:cut], term_sems.at[terms - 2])
+        )
+        early.append(
+            pltpu.make_async_copy(term_hbm[-1], term_s[-1].at[cut:], term_sems.at[terms - 1])
+        )
+        start_all(early)
     loads = start_all(
         [
             pltpu.make_async_copy(source, target, io_sems.at[k])
@@ -538,8 +548,22 @@
         gm_s[r, D:] = narrow(gm_s[r, :D], 0, i)
         return carry
 
+    loads[0].wait()
+    if terms:
+        wait_all(early)
+
+        def norm_stage(i, carry):
+            r = rows_of(i)
+            total = term_s[0][r, :].astype(F32)
+            for ref in term_s[1:]:
+                total = total + ref[r, :].astype(F32)
+            grad = rms_back(grad_in[r, :], hidden_s[r, :], gain_next[...], total)
+            grad_in[r, :] = grad
+            gl_out[r, :] = grad.astype(BF)
+            return carry
+
+        lax.fori_loop(0, rows // block, norm_stage, 0)
     wait_all(copies[2])
-    loads[0].wait()
     loads[1].wait()
     lax.fori_loop(0, rows // block, down_stage, 0)
     wait_all(copies[1])
@@ -554,7 +578,7 @@
             mixed_grad[p][source] = dot(r_s[at : at + group, :WIDE], gm_s[...], NT).astype(BF)
 
 
-def feed_back(meta, gain_mlp, grad, middle, inner, weights, parts, sources):
+def feed_back(meta, gain_mlp, grad, middle, inner, weights, parts, sources, norm=None):
     rows = grad.shape[0]
     narrow = shape((rows, AR))
     return call(
@@ -563,11 +587,15 @@
             parts=parts,
             pieces=2,
             block=math.gcd(rows, 320),
+            terms=0 if norm is None else len(norm[2]),
         ),
         "feed_back",
         (shape((rows, D), F32), shape((rows, D)), shape((rows, WIDE)), narrow, narrow)
-        + (shape((sources, D // sources // parts, rows)),) * parts,
-        [SMEM, VMEM] + [HBM] * (3 + 2),
+        + (shape((sources, D // sources // parts, rows)),) * parts
+        + (() if norm is None else (shape((rows, D)),)),
+        [SMEM, VMEM]
+        + [HBM] * (3 + 2)
+        + ([] if norm is None else [VMEM] + [HBM] * (1 + len(norm[2]))),
         [
             pltpu.VMEM((rows, D), grad.dtype),
             pltpu.VMEM((rows, D), F32),
@@ -575,9 +603,24 @@
             pltpu.VMEM((D, SIDE), BF),
             pltpu.SemaphoreType.DMA((3, 2)),
             pltpu.SemaphoreType.DMA((3,)),
-        ],
+        ]
+        + (
+            []
+            if norm is None
+            else [pltpu.VMEM((rows, D), F32)]
+            + [pltpu.VMEM((rows, D), BF)] * (len(norm[2]) - 1)
+            + [pltpu.SemaphoreType.DMA((len(norm[2]) + 1,))]
+        ),
         0.05,
-    )(meta, gain_mlp, grad, middle, inner, *weights)
+    )(
+        meta,
+        gain_mlp,
+        grad,
+        middle,
+        inner,
+        *weights,
+        *(() if norm is None else (norm[0], norm[1], *norm[2])),
+    )
 
 
 def feed_sums_kernel(*refs, parts):
@@ -659,8 +702,6 @@
     outs, refs = refs[:arrays], refs[arrays:]
     if mode != "own":
         lora_out, refs = refs[0], refs[1:]
-    if mode == "far":
-        lora_own, refs = refs[0], refs[1:]
     wq_s, cb_s, bd_s = refs[:3]
     g_s = refs[3 : 3 + parts]
     sems, row_sems = refs[3 + parts :]
@@ -680,10 +721,9 @@
     columns = wq_s.shape[1]
     each = columns // parts
     fill_second(meta, cb_s, bd_s, columns // 3, each // 3)
-    base = meta[7] if mode == "far" else 0
 
     def rows_of(place):
-        at = pl.ds(pl.multiple_of(base + place, 64), block)
+        at = pl.ds(pl.multiple_of(place, 64), block)
         return jnp.concatenate([g_s[p][at, :] for p in range(parts)], axis=1)
 
     def narrow(g, place):
@@ -708,28 +748,12 @@
             return carry
 
         lax.fori_loop(0, rows // block, step, 0)
-    if mode == "far":
-        half = GLEN // 2
-        own = half - meta[7]
-
-        def own_step(i, carry):
-            place = pl.multiple_of(i * block, 64)
-            at = pl.multiple_of(own + place, 64)
-            g = jnp.concatenate([g_s[p][pl.ds(at, block), :] for p in range(parts)], axis=1)
-            mask = row_mask(meta, at, block)
-            lora_own[pl.ds(place, block), :] = (
-                dot(g, bd_s[...]) * jnp.concatenate([mask] * 3, axis=1)
-            ).astype(BF)
-            return carry
-
-        lax.fori_loop(0, half // block, own_step, 0)
 
 
 def project_back(meta, grads, weights, base, arrays, rows, mode, lora=None):
     columns = sum(g.shape[1] for g in grads)
     count = rows * arrays
     low = (shape((count, 3 * AR)),)
-    held = count if mode == "own" else GLEN
     return call(
         partial(
             project_back_kernel,
@@ -740,14 +764,14 @@
             mode=mode,
         ),
         "project_back",
-        tuple(shape((rows, D)) for _ in range(arrays)) + low * {"own": 0, "far": 2, "all": 1}[mode],
+        tuple(shape((rows, D)) for _ in range(arrays)) + low * (mode != "own"),
         [SMEM] + [HBM] * (len(grads) + len(weights)) + [VMEM] * (mode == "own"),
         [
             pltpu.VMEM((D, columns), BF),
             pltpu.VMEM((D, 6 * AR), BF),
             pltpu.VMEM((columns, 3 * AR), BF),
         ]
-        + [pltpu.VMEM((held, g.shape[1]), BF) for g in grads]
+        + [pltpu.VMEM((count, g.shape[1]), BF) for g in grads]
         + [
             pltpu.SemaphoreType.DMA((3 * sum(w.shape[0] for w in weights),)),
             pltpu.SemaphoreType.DMA((len(grads),)),
@@ -756,13 +780,35 @@
     )(meta.at[7].set(base), *grads, *weights, *(() if lora is None else (lora,)))
 
 
-def project_sums_kernel(*refs, parts, groups, arrays):
+def project_sums_kernel(*refs, parts, groups, arrays, block):
     meta = refs[0]
-    grads = refs[1 : 1 + parts]
-    lows = refs[1 + parts : 1 + parts + groups]
-    loras = refs[1 + parts + groups : 1 + parts + 2 * groups]
-    tokens = refs[1 + parts + 2 * groups : 1 + parts + 2 * groups + groups * arrays]
-    sums, turned = refs[1 + parts + 2 * groups + groups * arrays :]
+    grads, refs = refs[1 : 1 + parts], refs[1 + parts :]
+    lows, refs = refs[:groups], refs[groups:]
+    lora_far, refs = refs[0], refs[1:]
+    tokens, refs = refs[: groups * arrays], refs[groups * arrays :]
+    if groups == 1:
+        loras = [lora_far]
+        sums, turned = refs
+    else:
+        weights, refs = refs[:2], refs[2:]
+        sums, lora_own, turned, cb_s, bd_s, sems = refs
+        loras = [lora_own, lora_far]
+        run_copies(head_copies(meta, weights, None, cb_s, sems))
+        each = grads[0].shape[1]
+        fill_second(meta, cb_s, bd_s, each * parts // 3, each // 3)
+        count = lora_own.shape[0]
+
+        def step(i, carry):
+            place = pl.multiple_of(i * block, 64)
+            at = pl.multiple_of(meta[6] * count + place, 64)
+            g = jnp.concatenate([ref[pl.ds(at, block), :] for ref in grads], axis=1)
+            mask = row_mask(meta, at, block)
+            lora_own[pl.ds(place, block), :] = (
+                dot(g, bd_s[...]) * jnp.concatenate([mask] * 3, axis=1)
+            ).astype(BF)
+            return carry
+
+        lax.fori_loop(0, count // block, step, 0)
     sections = []
     for index in range(groups):
         for k in range(arrays):
@@ -798,19 +844,35 @@
             sums[pl.ds(own, group), (3 + c) * AR : (4 + c) * AR] = total.T.astype(BF)
 
 
-def project_sums(meta, grads, lows, loras, tokens):
+def project_sums(meta, grads, lows, lora_far, tokens, weights):
     flat = [t for arrays in tokens for t in arrays]
     rows = flat[0].shape[0]
+    columns = sum(g.shape[1] for g in grads)
+    outs = (shape((D, 6 * AR)),)
+    scratch = [pltpu.VMEM((len(flat), 3 * AR, rows), BF)]
+    if len(lows) > 1:
+        outs += (shape(lows[0].shape),)
+        scratch += [
+            pltpu.VMEM((D, 6 * AR), BF),
+            pltpu.VMEM((columns, 3 * AR), BF),
+            pltpu.SemaphoreType.DMA((3,)),
+        ]
+    else:
+        weights = ()
     return call(
         partial(
-            project_sums_kernel, parts=len(grads), groups=len(lows), arrays=len(tokens[0])
+            project_sums_kernel,
+            parts=len(grads),
+            groups=len(lows),
+            arrays=len(tokens[0]),
+            block=320,
         ),
         "project_sums",
-        (shape((D, 6 * AR)),),
-        [SMEM] + [VMEM] * (len(grads) + 2 * len(lows) + len(flat)),
-        [pltpu.VMEM((len(flat), 3 * AR, rows), BF)],
+        outs,
+        [SMEM] + [VMEM] * (len(grads) + len(lows) + 1 + len(flat)) + [HBM] * len(weights),
+        scratch,
         0.05,
-    )(meta, *grads, *lows, *loras, *flat)[0]
+    )(meta, *grads, *lows, lora_far, *flat, *weights)
 
 
 def swap(value, axis, count, step):
@@ -823,6 +885,12 @@
 
 def after(value, *earlier):
     return lax.optimization_barrier((value, *earlier))[0]
+
+
+def sum_over_seq(value, seq_count):
+    for step in (1, 2):
+        value = (value.astype(F32) + swap(value, "seq", seq_count, step).astype(F32)).astype(BF)
+    return value
 
 
 def reduce_quarter(value, core, chip, seq_count, fsdp_count):
@@ -840,13 +908,9 @@
     return lax.all_to_all(value, "fsdp", split_axis=0, concat_axis=0, tiled=True)
 
 
-def reduce_owner(value, core, chip, seq_count):
-    def join(v, index, step):
-        far = swap(v, "seq", seq_count, step)
-        return jnp.where(index == 0, jnp.concatenate([v, far]), jnp.concatenate([far, v]))
-
-    value = jnp.sum(value.astype(F32), axis=0).astype(BF)
-    return join(join(value, chip, 2), core, 1)
+def joined(value, index, seq_count, step):
+    far = swap(value, "seq", seq_count, step)
+    return jnp.where(index == 0, jnp.concatenate([value, far]), jnp.concatenate([far, value]))
 
 
 def reduce_rows(value):
@@ -970,15 +1034,24 @@
         tiled = jnp.concatenate([jnp.tile(factor * LOG2E, group // HD), jnp.ones((2 * group,), F32)])
         scale = jnp.tile(tiled, parts).reshape(1, 3 * width)
         if layer > 0 and paired:
-            far = swap(normed, "seq", seq_count, 2)
-            head_gathered, far = fence(head_gathered, far)
+            cut = rows * 3 // 5
+            far = swap(normed[:cut], "seq", seq_count, 2)
+            head_gathered, far, rest = fence(head_gathered, far, normed[cut:])
+            next_side = gathered(after(side_part(layer), head_gathered))
+            far = [far, swap(rest, "seq", seq_count, 2)]
         head_weights.append((head_gathered[None], other_core(head_gathered, both)[None]))
         if layer > 0:
-            side_gathered = gathered(after(side_part(layer), head_gathered))
+            side_gathered = (
+                next_side if paired else gathered(after(side_part(layer), head_gathered))
+            )
         if paired:
             own = ([normed, swap(normed, "seq", seq_count, 1)], chip * 2 * rows)
             projected = [project(meta, scale, own[0], head_weights[layer], own[1], parts)]
-            far = after(far, projected[0][-1])
+            if layer > 0:
+                far[0], far[1], projected[0] = fence(far[0], far[1], projected[0])
+                far = jnp.concatenate(far)
+            else:
+                far = after(far, projected[0][-1])
             far = ([far, swap(far, "seq", seq_count, 1)], (1 - chip) * 2 * rows)
             projected.append(project(meta, scale, far[0], head_weights[layer], far[1], parts))
             groups = [own, far]
@@ -1017,33 +1090,35 @@
             hidden, normed = results[3:]
 
     grad = cotangent[0]
+    pending = None
     sums = [None] * LAYERS
     for layer in reversed(range(LAYERS)):
         hidden, groups, heads, lows, attended, mixed, factor, middle, inner, low = kept[layer]
         gain = mlp_gain[layer][None]
-        grad_in = grad
         results = feed_back(
-            meta, gain, grad_in, middle, inner, side_weights[layer], parts, seq_count
+            meta, gain, grad, middle, inner, side_weights[layer], parts, seq_count, pending
         )
         results = fence(*results)
+        grad_in = grad if pending is None else results[5 + parts]
         grad, gi, gm, dl, il = results[:5]
         mixed_grads = [to_heads(results[5])]
         side_sum = feed_sums(gain, grad_in, middle, inner, gi, gm, dl, il, low, mixed)
         mixed_grads, side_sum = fence(mixed_grads, side_sum)
         side_total = reduce_rows(side_sum)
-        if layer == 0 and paired:
-            side_reduced = after(side_total, sums[1][1])
-            side_reduced = lax.psum(side_reduced, "seq")
-            sums[1] = tuple(lax.psum(v, "seq") for v in sums[1])
         factor_row = jnp.pad(factor, (0, 128 - HD)).reshape(1, 128)
         head_grads = []
         for p in range(parts):
             if p < parts - 1:
                 mixed_grads.append(to_heads(after(results[6 + p], side_sum)))
             head_grads.append(
-                attend_back(meta, factor_row, heads[p], attended[p][0], mixed_grads[p], attended[p][1])
+                attend_back(meta, factor_row, attended[p][1], attended[p][0], mixed_grads[p])
             )
-            head_grads, mixed_grads = fence(head_grads, mixed_grads)
+            if p == parts - 1 and layer < LAYERS - 1 and paired:
+                whole = sum_over_seq(jnp.stack(sums[layer + 1]), seq_count)
+                head_grads, mixed_grads, whole = fence(head_grads, mixed_grads, whole)
+                sums[layer + 1] = (whole[0], whole[1])
+            else:
+                head_grads, mixed_grads = fence(head_grads, mixed_grads)
         if paired:
             own, far = groups
             far_back = project_back(
@@ -1052,26 +1127,25 @@
             far_sum = (
                 far_back[0].astype(F32) + swap(far_back[1], "seq", seq_count, 1).astype(F32)
             ).astype(BF)
-            if layer > 0:
-                far_sum, head_grads, side_total = fence(far_sum, head_grads, side_total)
-            else:
-                far_sum, head_grads = fence(far_sum, head_grads)
-            loras = [far_back[3], far_back[2]]
-            cut = rows * 3 // 5
+            far_sum, head_grads, side_total = fence(far_sum, head_grads, side_total)
+            cut = rows * (3 if layer > 0 else 2) // 5
             crossed = swap(far_sum[:cut], "seq", seq_count, 2)
-            head_sum = project_sums(meta, head_grads, lows, loras, [g[0] for g in groups])
+            head_sum, lora_own = project_sums(
+                meta, head_grads, lows, far_back[2], [g[0] for g in groups], head_weights[layer]
+            )
             if layer == 0:
-                side_total = side_reduced
-            head_sum, crossed, head_grads, rest, sums[1], side_total = fence(
-                head_sum, crossed, head_grads, far_sum[cut:], sums[1], side_total
+                side_total = sum_over_seq(side_total, seq_count)
+            head_sum, lora_own, crossed, head_grads, rest, side_total = fence(
+                head_sum, lora_own, crossed, head_grads, far_sum[cut:], side_total
             )
             if layer > 0:
                 head_total = reduce_rows(head_sum)
-                rest = swap(rest, "seq", seq_count, 2)
             else:
                 head_total = reduce_quarter(head_sum, core, chip, seq_count, fsdp_count)
+            if layer > 0:
+                rest = swap(rest, "seq", seq_count, 2)
             own_back = project_back(
-                meta, head_grads, head_weights[layer], own[1], 2, rows, "own", loras[0]
+                meta, head_grads, head_weights[layer], own[1], 2, rows, "own", lora_own
             )
             if layer > 0:
                 own_back, rest = fence(own_back, rest)
@@ -1080,7 +1154,6 @@
                 rest = swap(rest, "seq", seq_count, 2)
                 head_total = owned(head_total)
                 head_total, rest = fence(head_total, rest)
-                head_total = reduce_owner(head_total, core, chip, seq_count)
             near = swap(own_back[1], "seq", seq_count, 1)
             sums[layer] = (side_total, head_total)
             terms = [own_back[0], near, crossed, rest]
@@ -1089,9 +1162,18 @@
                 meta, head_grads, head_weights[layer], place * 0, 1, GLEN, "all"
             )
             terms = [lax.psum_scatter(back[0], "seq", scatter_dimension=0, tiled=True)]
-            head_sum = project_sums(meta, head_grads, lows, [back[1]], [g[0] for g in groups])
+            head_sum = project_sums(
+                meta, head_grads, lows, back[1], [g[0] for g in groups], head_weights[layer]
+            )[0]
             sums[layer] = tuple(lax.psum(v, "seq") for v in (side_total, reduce_rows(head_sum)))
-        grad = norm_back(attn_gain[layer][None], grad, hidden, terms)
+        if layer > 0 and paired:
+            pending = (attn_gain[layer][None], hidden, terms)
+        else:
+            grad = norm_back(attn_gain[layer][None], grad, hidden, terms)
+            if paired:
+                head_total = joined(jnp.sum(head_total.astype(F32), axis=0).astype(BF), chip, seq_count, 2)
+                grad, head_total = fence(grad, head_total)
+                sums[0] = (sums[0][0], joined(head_total, core, seq_count, 1))
 
     side = jnp.stack([s[0] for s in sums]).astype(F32)
     head = jnp.stack([s[1] for s in sums]).astype(F32)

time: 793 us -> 762 us (0.961)
  waiting for transfers between devices: 213 us -> 188 us
  Pallas kernels: 442 us -> 427 us
    ppermute x22 -> x27, waiting for transfers between devices: 82.2 us -> 48.1 us  [swap(): return lax.ppermute(value, axis, [(i, i ^ step) for i in range(count)])]
    all_to_all x1, waiting for transfers between devices: 0.01 us -> 13.6 us  [owned(): lax.all_to_all(value, 'fsdp', split_axis=0, concat_axis=0, tiled=True)]
    pallas_call x4, Pallas kernels: 115 us -> 105 us  [attend_back(): call(attend_back_kernel, 'attend_back', (shape((GLEN, 3 * local_heads * H...]
    pallas_call x2 -> x1, Pallas kernels: 16 us -> 7.98 us  [norm_back(): pl.pallas_call(partial(norm_back_kernel, cut=cut), grid=(rows // block,),...]
  transfers between devices with their start and end apart: 38 -> 42, of which waited for: 24 -> 25; matrix products, arithmetic and copies ran while one was open for 4% -> 5% of each run, Pallas kernels for 51% -> 51%
where the time goes in v3:
time: 762 us; the launch traced here: 753 us
  Pallas kernels  427 us (56%)
  waiting for transfers between devices  188 us (25%)
  starting transfers between devices  44.2 us (6%)
  local copies, waits for them, and re-layouts  42.9 us (6%)
  other arithmetic  19.5 us (3%)
  blocking collectives  16.5 us (2%)
  between operations  15.4 us (2%)
    all_gather x4, waiting for transfers between devices, gathered(): return lax.all_gather(value, 'fsdp', axis=0, tiled=True)  107 us
    pallas_call x4, Pallas kernels, attend_back(): call(attend_back_kernel, 'attend_back', (shape((GLEN, 3 * local_heads * H...  105 us
    pallas_call x4, Pallas kernels, attend(): call(partial(attend_kernel, groups=len(heads), local_heads=local_heads),...  75.9 us
    pallas_call x4, Pallas kernels, project(): call(partial(project_kernel, arrays=arrays, pieces=len(weights), parts=pa...  56.4 us
    pallas_call x4, Pallas kernels, project_back(): call(partial(project_back_kernel, arrays=arrays, pieces=len(weights), par...  51.8 us
    ppermute x27, waiting for transfers between devices, swap(): return lax.ppermute(value, axis, [(i, i ^ step) for i in range(count)])  48.1 us
    pallas_call x2, Pallas kernels, feed_back(): call(partial(feed_back_kernel, parts=parts, pieces=2, block=math.gcd(rows...  43.3 us
    pallas_call x2, Pallas kernels, feed(): call(partial(feed_kernel, parts=len(mixed), pieces=2, block=math.gcd(rows...  38.9 us
  transfers between devices with their start and end apart: 42, of which 25 were waited for; matrix products, arithmetic and copies ran while one was open for 5% of the time, Pallas kernels for 51%

profile of v3, /device:TPU:0, one launch (start us, length us, event | category | flops | bytes accessed | tf_op | source)
XLA Modules:
  0.0 752.7 jit_solution(3974331171729702158)
XLA Ops:
  22.7 58.2 %all-gather.5.cloned.1.call-done = bf16[1280,1344]{1,0:T(8,128)(2,1)} async-done(((bf16[160,1344]{1,0:T(8,128)(2,1)}), bf16[1280,1344]{1,0:T(8,128)(2,1)}) %all-gather.5.cloned.1.call-update) | async-done | bytes 3440656 | tf_op jit(solution)/shard_map/all_gather | solution.py:1001
  88.4 14.1 %project.4 = (bf16[1280,480]{1,0:T(8,128)(2,1)}, bf16[1280,480]{1,0:T(8,128)(2,1)}, bf16[1280,384]{1,0:T(8,128)(2,1)}) custom-call(s32[8]{0:T(128)} %copy-done.55, f32[1,960]{1,0:T(1,128)} %reshape_tile.6.refs_1_, bf16[640,1280]{1,0:T(8,128)(2,1)} %multiply_convert_fusion.refs_2_.refs_6_, bf16[640,1280]{1,0:T(8,128)(2,1)} %collective-permute-done.refs_3_.refs_7_, ...), custom_call_target="tpu_custom_call" | custom-call | flops 14949999616 | bytes 1024 | tf_op jit(solution)/shard_map/project/pallas_call | solution.py:169
  107.5 13.7 %project.5 = (bf16[1280,480]{1,0:T(8,128)(2,1)}, bf16[1280,480]{1,0:T(8,128)(2,1)}, bf16[1280,384]{1,0:T(8,128)(2,1)}) custom-call(s32[8]{0:T(128)} %copy-done.56, f32[1,960]{1,0:T(1,128)} %reshape_tile.6.refs_1_, bf16[640,1280]{1,0:T(8,128)(2,1)} %copy-done.19, bf16[640,1280]{1,0:T(8,128)(2,1)} %copy-done.20, bf16[1,1280,1344]{2,1,0:T(8,128)(2,1)} %bitcast.217, ...), custom_call_target="tpu_custom_call" | custom-call | flops 14949999616 | bytes 1024 | tf_op jit(solution)/shard_map/project/pallas_call | solution.py:169
  121.3 19.4 %attend.4 = (bf16[4,160,640]{2,1,0:T(8,128)(2,1)}, bf16[3,2,2560,128]{3,2,1,0:T(8,128)(2,1)}) custom-call(s32[8]{0:T(128)} %copy-done.50, bf16[1280,480]{1,0:T(8,128)(2,1)} %get-tuple-element.219.refs_1_, bf16[1280,480]{1,0:T(8,128)(2,1)} %get-tuple-element.223.refs_2_), custom_call_target="tpu_custom_call" | custom-call | flops 18400000000 | bytes 1024 | tf_op jit(solution)/shard_map/attend/pallas_call | solution.py:276
  144.3 19.0 %attend.5 = (bf16[4,160,640]{2,1,0:T(8,128)(2,1)}, bf16[3,2,2560,128]{3,2,1,0:T(8,128)(2,1)}) custom-call(s32[8]{0:T(128)} %copy-done.50, bf16[1280,480]{1,0:T(8,128)(2,1)} %get-tuple-element.227.refs_1_, bf16[1280,480]{1,0:T(8,128)(2,1)} %get-tuple-element.229.refs_2_), custom_call_target="tpu_custom_call" | custom-call | flops 18400000000 | bytes 1024 | tf_op jit(solution)/shard_map/attend/pallas_call | solution.py:276
  194.0 20.4 %feed.2 = (f32[640,1280]{1,0:T(8,128)}, f32[640,1280]{1,0:T(8,128)}, bf16[640,384]{1,0:T(8,128)(2,1)}, f32[640,1280]{1,0:T(8,128)}, bf16[640,1280]{1,0:T(8,128)(2,1)}) custom-call(s32[8]{0:T(128)} %copy-done.50, f32[1,1280]{1,0:T(1,128)} %get-tuple-element.415.refs_1_.refs_0_, f32[1,1280]{1,0:T(1,128)} %get-tuple-element.413.refs_2_.refs_7_, ...), custom_call_target="tpu_custom_call" | custom-call | flops 19549999104 | bytes 1024 | tf_op jit(solution)/shard_map/feed/pallas_call | solution.py:445
  218.9 24.0 %all-gather.9.cloned.1.call-done = bf16[1280,1344]{1,0:T(8,128)(2,1)} async-done(((bf16[160,1344]{1,0:T(8,128)(2,1)}), bf16[1280,1344]{1,0:T(8,128)(2,1)}) %all-gather.9.cloned.1.call-update) | async-done | bytes 3440656 | tf_op jit(solution)/shard_map/all_gather | solution.py:1001
  249.8 14.3 %project.6 = (bf16[1280,480]{1,0:T(8,128)(2,1)}, bf16[1280,480]{1,0:T(8,128)(2,1)}, bf16[1280,384]{1,0:T(8,128)(2,1)}) custom-call(s32[8]{0:T(128)} %copy-done.55, f32[1,960]{1,0:T(1,128)} %reshape_tile.7.refs_1_, bf16[640,1280]{1,0:T(8,128)(2,1)} %get-tuple-element.239.refs_2_.refs_6_, bf16[640,1280]{1,0:T(8,128)(2,1)} %collective-permute-done.7.refs_3_.refs_7_, ...), custom_call_target="tpu_custom_call" | custom-call | flops 14949999616 | bytes 1024 | tf_op jit(solution)/shard_map/project/pallas_call | solution.py:169
  270.1 14.3 %project.7 = (bf16[1280,480]{1,0:T(8,128)(2,1)}, bf16[1280,480]{1,0:T(8,128)(2,1)}, bf16[1280,384]{1,0:T(8,128)(2,1)}) custom-call(s32[8]{0:T(128)} %copy-done.56, f32[1,960]{1,0:T(1,128)} %reshape_tile.7.refs_1_, bf16[640,1280]{1,0:T(8,128)(2,1)} %copy-done.5, bf16[640,1280]{1,0:T(8,128)(2,1)} %copy-done.21, bf16[1,1280,1344]{2,1,0:T(8,128)(2,1)} %bitcast.222, ...), custom_call_target="tpu_custom_call" | custom-call | flops 14949999616 | bytes 1024 | tf_op jit(solution)/shard_map/project/pallas_call | solution.py:169
  284.4 18.8 %attend.6 = (bf16[4,160,640]{2,1,0:T(8,128)(2,1)}, bf16[3,2,2560,128]{3,2,1,0:T(8,128)(2,1)}) custom-call(s32[8]{0:T(128)} %copy-done.50, bf16[1280,480]{1,0:T(8,128)(2,1)} %get-tuple-element.246.refs_1_, bf16[1280,480]{1,0:T(8,128)(2,1)} %get-tuple-element.249.refs_2_), custom_call_target="tpu_custom_call" | custom-call | flops 18400000000 | bytes 1024 | tf_op jit(solution)/shard_map/attend/pallas_call | solution.py:276
  306.8 18.7 %attend.7 = (bf16[4,160,640]{2,1,0:T(8,128)(2,1)}, bf16[3,2,2560,128]{3,2,1,0:T(8,128)(2,1)}) custom-call(s32[8]{0:T(128)} %copy-done.50, bf16[1280,480]{1,0:T(8,128)(2,1)} %get-tuple-element.253.refs_1_, bf16[1280,480]{1,0:T(8,128)(2,1)} %get-tuple-element.255.refs_2_), custom_call_target="tpu_custom_call" | custom-call | flops 18400000000 | bytes 1024 | tf_op jit(solution)/shard_map/attend/pallas_call | solution.py:276
  337.6 16.5 %all_to_all.45.refs_5_.refs_10_ = bf16[4,160,640]{2,1,0:T(8,128)(2,1)} all-to-all(bf16[4,160,640]{2,1,0:T(8,128)(2,1)} %get-tuple-element.259.o_ref), channel_id=1, replica_groups=mesh['seq'=4,'fsdp'=8] {'seq'}, dimensions={0} | all-to-all | bytes 1638400 | tf_op jit(solution)/shard_map/all_to_all | solution.py:1009
  354.1 18.6 %feed.3 = (f32[640,1280]{1,0:T(8,128)}, f32[640,1280]{1,0:T(8,128)}, bf16[640,384]{1,0:T(8,128)(2,1)}, bf16[640,1280]{1,0:T(8,128)(2,1)}) custom-call(s32[8]{0:T(128)} %copy-done.50, f32[1,1280]{1,0:T(1,128)} %get-tuple-element.416.refs_1_.refs_0_, f32[1,1280]{1,0:T(1,128)} %get-tuple-element.414.refs_2_.gain, ...), custom_call_target="tpu_custom_call" | custom-call | flops 19549999104 | bytes 1024 | tf_op jit(solution)/shard_map/feed/pallas_call | solution.py:445
  372.7 18.7 %feed_back.2 = (f32[640,1280]{1,0:T(8,128)}, bf16[640,1280]{1,0:T(8,128)(2,1)}, bf16[640,1408]{1,0:T(8,128)(2,1)}, bf16[640,128]{1,0:T(8,128)(2,1)}, bf16[640,12...) custom-call(s32[8]{0:T(128)} %copy-done.50, ...), custom_call_target="tpu_custom_call" | custom-call | flops 57500000 | bytes 1024 | tf_op jit(solution)/shard_map/feed_back/pallas_call | solution.py:584
  412.4 25.9 %attend_back.4.refs_1_ = bf16[2560,480]{1,0:T(8,128)(2,1)} custom-call(s32[8]{0:T(128)} %copy-done.50, f32[1,128]{1,0:T(1,128)} %pad_bitcast_fusion.1.factor, bf16[3,2,2560,128]{3,2,1,0:T(8,128)(2,1)} %get-tuple-element.269.saved, bf16[4,160,640]{2,1,0:T(8,128)(2,1)} %get-tuple-element.270.o_ref, bf16[4,160,640]{2,1,0:T(8,128)(2,1)} %copy-done.7), custom_call_target="tpu_custom_call" | custom-call | flops 57500000 | bytes 1024 | tf_op jit(solution)/shard_map/attend_back/pallas_call | solution.py:348
  439.2 26.3 %attend_back.5.refs_2_ = bf16[2560,480]{1,0:T(8,128)(2,1)} custom-call(s32[8]{0:T(128)} %copy-done.50, f32[1,128]{1,0:T(1,128)} %pad_bitcast_fusion.1.factor, bf16[3,2,2560,128]{3,2,1,0:T(8,128)(2,1)} %get-tuple-element.261.saved, bf16[4,160,640]{2,1,0:T(8,128)(2,1)} %get-tuple-element.259.o_ref, bf16[4,160,640]{2,1,0:T(8,128)(2,1)} %copy-done.9), custom_call_target="tpu_custom_call" | custom-call | flops 57500000 | bytes 1024 | tf_op jit(solution)/shard_map/attend_back/pallas_call | solution.py:348
  465.6 14.4 %project_back.4 = (bf16[640,1280]{1,0:T(8,128)(2,1)}, bf16[640,1280]{1,0:T(8,128)(2,1)}, bf16[1280,384]{1,0:T(8,128)(2,1)}) custom-call(s32[8]{0:T(128)} %copy-done.56, bf16[2560,480]{1,0:T(8,128)(2,1)} %attend_back.4.refs_1_, bf16[2560,480]{1,0:T(8,128)(2,1)} %attend_back.5.refs_2_, bf16[1,1280,1344]{2,1,0:T(8,128)(2,1)} %bitcast.223, ...), custom_call_target="tpu_custom_call" | custom-call | flops 57500000 | bytes 1024 | tf_op jit(solution)/shard_map/project_back/pallas_call | solution.py:757
  488.7 14.6 %project_sums.2 = (bf16[1280,768]{1,0:T(8,128)(2,1)}, bf16[1280,384]{1,0:T(8,128)(2,1)}) custom-call(s32[8]{0:T(128)} %copy-done.50, bf16[2560,480]{1,0:T(8,128)(2,1)} %attend_back.4.refs_1_, bf16[2560,480]{1,0:T(8,128)(2,1)} %attend_back.5.refs_2_, bf16[1280,384]{1,0:T(8,128)(2,1)} %get-tuple-element.289.refs_3_, ...), custom_call_target="tpu_custom_call" | custom-call | flops 57500000 | bytes 1024 | tf_op jit(solution)/shard_map/project_sums/pallas_call | solution.py:862
  533.1 24.6 %feed_back.3 = (f32[640,1280]{1,0:T(8,128)}, bf16[640,1280]{1,0:T(8,128)(2,1)}, bf16[640,1408]{1,0:T(8,128)(2,1)}, bf16[640,128]{1,0:T(8,128)(2,1)}, bf16[640,12...) custom-call(s32[8]{0:T(128)} %copy-done.50, ...), custom_call_target="tpu_custom_call" | custom-call | flops 57500000 | bytes 1024 | tf_op jit(solution)/shard_map/feed_back/pallas_call | solution.py:584
  584.1 26.0 %attend_back.6.refs_1_ = bf16[2560,480]{1,0:T(8,128)(2,1)} custom-call(s32[8]{0:T(128)} %copy-done.50, f32[1,128]{1,0:T(1,128)} %pad_bitcast_fusion.factor, bf16[3,2,2560,128]{3,2,1,0:T(8,128)(2,1)} %get-tuple-element.307.saved, bf16[4,160,640]{2,1,0:T(8,128)(2,1)} %get-tuple-element.308.o_ref, bf16[4,160,640]{2,1,0:T(8,128)(2,1)} %copy-done.6), custom_call_target="tpu_custom_call" | custom-call | flops 57500000 | bytes 1024 | tf_op jit(solution)/shard_map/attend_back/pallas_call | solution.py:348
  611.0 26.4 %attend_back.7.refs_2_ = bf16[2560,480]{1,0:T(8,128)(2,1)} custom-call(s32[8]{0:T(128)} %copy-done.50, f32[1,128]{1,0:T(1,128)} %pad_bitcast_fusion.factor, bf16[3,2,2560,128]{3,2,1,0:T(8,128)(2,1)} %get-tuple-element.235.saved, bf16[4,160,640]{2,1,0:T(8,128)(2,1)} %get-tuple-element.233.o_ref, bf16[4,160,640]{2,1,0:T(8,128)(2,1)} %copy-done.8), custom_call_target="tpu_custom_call" | custom-call | flops 57500000 | bytes 1024 | tf_op jit(solution)/shard_map/attend_back/pallas_call | solution.py:348
  638.6 14.5 %project_back.6 = (bf16[640,1280]{1,0:T(8,128)(2,1)}, bf16[640,1280]{1,0:T(8,128)(2,1)}, bf16[1280,384]{1,0:T(8,128)(2,1)}) custom-call(s32[8]{0:T(128)} %copy-done.56, bf16[2560,480]{1,0:T(8,128)(2,1)} %attend_back.6.refs_1_, bf16[2560,480]{1,0:T(8,128)(2,1)} %attend_back.7.refs_2_, bf16[1,1280,1344]{2,1,0:T(8,128)(2,1)} %bitcast.218, ...), custom_call_target="tpu_custom_call" | custom-call | flops 57500000 | bytes 1024 | tf_op jit(solution)/shard_map/project_back/pallas_call | solution.py:757
  664.0 14.9 %project_sums.3 = (bf16[1280,768]{1,0:T(8,128)(2,1)}, bf16[1280,384]{1,0:T(8,128)(2,1)}) custom-call(s32[8]{0:T(128)} %copy-done.50, bf16[2560,480]{1,0:T(8,128)(2,1)} %attend_back.6.refs_1_, bf16[2560,480]{1,0:T(8,128)(2,1)} %attend_back.7.refs_2_, bf16[1280,384]{1,0:T(8,128)(2,1)} %get-tuple-element.221.refs_3_, ...), custom_call_target="tpu_custom_call" | custom-call | flops 57500000 | bytes 1024 | tf_op jit(solution)/shard_map/project_sums/pallas_call | solution.py:862
  708.9 13.6 %all-to-all-done.8 = bf16[8,40,768]{2,1,0:T(8,128)(2,1)S(1)} async-done(((bf16[8,40,768]{2,1,0:T(8,128)(2,1)}), bf16[8,40,768]{2,1,0:T(8,128)(2,1)S(1)}, u32[]{:S(2)}, u32[]{:S(2)}) %all-to-all-start.8) | async-done | bytes 491552 | tf_op jit(solution)/shard_map/all_to_all | solution.py:908
  (286 shorter events, 247.5 us)
Async XLA Ops:
  7.2 73.7 %all-gather.5.cloned.1.call-start = ((), (), s32[]{:S(2)}) async-start(), calls=%async_computation.12 | async-start | bytes 4055040 | tf_op jit(solution)/shard_map/all_gather | solution.py:1001
  12.1 163.8 %all-gather.7.cloned.1.call-start = ((), (), s32[]{:S(2)}) async-start(), calls=%async_computation.13 | async-start | bytes 6635520 | tf_op jit(solution)/shard_map/all_gather | solution.py:1001
  14.8 66.2 %collective-permute-start.1 = (bf16[640,1280]{1,0:T(8,128)(2,1)}, bf16[640,1280]{1,0:T(8,128)(2,1)S(1)}, u32[]{:S(2)}, u32[]{:S(2)}) collective-permute-start(bf16[640,1280]{1,0:T(8,128)(2,1)} %multiply_convert_fusion.refs_2_.refs_6_), channel_id=1, source_target_pairs={{0,16},{8,24},{16,0},{24,8},{1,17},{9,25},{17,1},{25,9},{2,18},{10... | collective-permute-start | bytes 4915208 | tf_op jit(solution)/shard_map/ppermute | solution.py:879
  140.7 22.7 %all-to-all-start = ((bf16[4,160,640]{2,1,0:T(8,128)(2,1)}), bf16[4,160,640]{2,1,0:T(8,128)(2,1)S(1)}, u32[]{:S(2)}, u32[]{:S(2)}) async-start(bf16[4,160,640]{2,1,0:T(8,128)(2,1)} %get-tuple-element.308.o_ref), calls=%async_computation | async-start | bytes 1638400 | tf_op jit(solution)/shard_map/all_to_all | solution.py:1009
  144.2 98.6 %all-gather.9.cloned.1.call-start = ((), (), s32[]{:S(2)}) async-start(), calls=%async_computation.14 | async-start | bytes 4055040 | tf_op jit(solution)/shard_map/all_gather | solution.py:1001
  175.9 17.2 %collective-permute-start.4 = (bf16[1280,2304]{1,0:T(8,128)(2,1)}, bf16[1280,2304]{1,0:T(8,128)(2,1)}, u32[]{:S(2)}, u32[]{:S(2)}) collective-permute-start(bf16[1280,2304]{1,0:T(8,128)(2,1)} %all-gather.7.cloned.1.call-done.refs_6_.refs_5_), channel_id=1, source_target_pairs={{0,8},{8,0},{16,24},{24,16},{1,9},{9,1},{17,25},{25,17},{2,10},{10... | collective-permute-start | bytes 17694728 | tf_op jit(solution)/shard_map/ppermute | solution.py:879
  181.1 156.5 %all-gather.11.cloned.1.call-start = ((), (), s32[]{:S(2)}) async-start(), calls=%async_computation.15 | async-start | bytes 6635520 | tf_op jit(solution)/shard_map/all_gather | solution.py:1001
  216.7 26.1 %collective-permute-start.5 = (bf16[384,1280]{1,0:T(8,128)(2,1)}, bf16[384,1280]{1,0:T(8,128)(2,1)S(1)}, u32[]{:S(2)}, u32[]{:S(2)}) collective-permute-start(bf16[384,1280]{1,0:T(8,128)(2,1)} %slice.295), channel_id=1, source_target_pairs={{0,16},{8,24},{16,0},{24,8},{1,17},{9,25},{17,1},{25,9},{2,18},{10... | collective-permute-start | bytes 2949128 | tf_op jit(solution)/shard_map/ppermute | solution.py:879
  246.8 17.3 %collective-permute-start.6 = (bf16[256,1280]{1,0:T(8,128)(2,1)S(1)}, bf16[256,1280]{1,0:T(8,128)(2,1)}, u32[]{:S(2)}, u32[]{:S(2)}) collective-permute-start(bf16[256,1280]{1,0:T(8,128)(2,1)S(1)} %slice.296), channel_id=1, source_target_pairs={{0,16},{8,24},{16,0},{24,8},{1,17},{9,25},{17,1},{25,9},{2,18},{10... | collective-permute-start | bytes 1966088 | tf_op jit(solution)/shard_map/ppermute | solution.py:879
  303.1 22.4 %all-to-all-start.2 = ((bf16[4,160,640]{2,1,0:T(8,128)(2,1)}), bf16[4,160,640]{2,1,0:T(8,128)(2,1)S(1)}, u32[]{:S(2)}, u32[]{:S(2)}) async-start(bf16[4,160,640]{2,1,0:T(8,128)(2,1)} %get-tuple-element.270.o_ref), calls=%async_computation.2 | async-start | bytes 1638400 | tf_op jit(solution)/shard_map/all_to_all | solution.py:1009
  337.6 16.5 %collective-permute-start.10 = (bf16[1280,2304]{1,0:T(8,128)(2,1)}, bf16[1280,2304]{1,0:T(8,128)(2,1)}, u32[]{:S(2)}, u32[]{:S(2)}) collective-permute-start(bf16[1280,2304]{1,0:T(8,128)(2,1)} %all-gather.11.cloned.1.call-done.refs_6_.refs_5_), channel_id=1, source_target_pairs={{0,8},{8,0},{16,24},{24,16},{1,9},{9,1},{17,25},{25,17},{2,10},{10... | collective-permute-start | bytes 17694728 | tf_op jit(solution)/shard_map/ppermute | solution.py:879
  394.9 90.8 %reduce-scatter.4.cloned.1.call-start = ((), (), s32[]{:S(2)}) async-start(), calls=%async_computation.16 | async-start | bytes 2211840 | tf_op jit(solution)/shard_map/reduce_scatter | solution.py:917
  407.8 30.5 %all-to-all-start.5 = ((bf16[4,160,640]{2,1,0:T(8,128)(2,1)}), bf16[4,160,640]{2,1,0:T(8,128)(2,1)S(1)}, u32[]{:S(2)}, u32[]{:S(2)}) async-start(bf16[4,160,640]{2,1,0:T(8,128)(2,1)} %get-tuple-element.280), calls=%async_computation.5 | async-start | bytes 1638400 | tf_op jit(solution)/shard_map/all_to_all | solution.py:1012
  411.3 165.2 %reduce-scatter.6.cloned.1.call-start = ((), (), s32[]{:S(2)}) async-start(), calls=%async_computation.17 | async-start | bytes 2211840 | tf_op jit(solution)/shard_map/reduce_scatter | solution.py:917
  486.8 24.2 %collective-permute-start.12 = (bf16[384,1280]{1,0:T(8,128)(2,1)}, bf16[384,1280]{1,0:T(8,128)(2,1)S(1)}, u32[]{:S(2)}, u32[]{:S(2)}) collective-permute-start(bf16[384,1280]{1,0:T(8,128)(2,1)} %slice.314), channel_id=1, source_target_pairs={{0,16},{8,24},{16,0},{24,8},{1,17},{9,25},{17,1},{25,9},{2,18},{10... | collective-permute-start | bytes 2949128 | tf_op jit(solution)/shard_map/ppermute | solution.py:879
  511.1 16.3 %collective-permute-start.13 = (bf16[256,1280]{1,0:T(8,128)(2,1)S(1)}, bf16[256,1280]{1,0:T(8,128)(2,1)S(1)}, u32[]{:S(2)}, u32[]{:S(2)}) collective-permute-start(bf16[256,1280]{1,0:T(8,128)(2,1)S(1)} %slice.315), channel_id=1, source_target_pairs={{0,16},{8,24},{16,0},{24,8},{1,17},{9,25},{17,1},{25,9},{2,18},{10... | collective-permute-start | bytes 1966088 | tf_op jit(solution)/shard_map/ppermute | solution.py:879
  561.2 97.6 %reduce-scatter.8.cloned.1.call-start = ((), (), s32[]{:S(2)}) async-start(), calls=%async_computation.18 | async-start | bytes 2211840 | tf_op jit(solution)/shard_map/reduce_scatter | solution.py:917
  577.7 32.4 %all-to-all-start.7 = ((bf16[4,160,640]{2,1,0:T(8,128)(2,1)}), bf16[4,160,640]{2,1,0:T(8,128)(2,1)S(1)}, u32[]{:S(2)}, u32[]{:S(2)}) async-start(bf16[4,160,640]{2,1,0:T(8,128)(2,1)} %get-tuple-element.319), calls=%async_computation.8 | async-start | bytes 1638400 | tf_op jit(solution)/shard_map/all_to_all | solution.py:1012
  581.6 55.8 %collective-permute-start.16 = (bf16[2,160,768]{2,1,0:T(8,128)(2,1)S(1)}, bf16[2,160,768]{2,1,0:T(8,128)(2,1)}, u32[]{:S(2)}, u32[]{:S(2)}) collective-permute-start(bf16[2,160,768]{2,1,0:T(8,128)(2,1)S(1)} %add_convert_fusion.3), channel_id=1, source_target_pairs={{0,16},{8,24},{16,0},{24,8},{1,17},{9,25},{17,1},{25,9},{2,18},{10... | collective-permute-start | bytes 1474568 | tf_op jit(solution)/shard_map/ppermute | solution.py:879
  659.9 23.3 %collective-permute-start.18 = (bf16[256,1280]{1,0:T(8,128)(2,1)}, bf16[256,1280]{1,0:T(8,128)(2,1)S(1)}, u32[]{:S(2)}, u32[]{:S(2)}) collective-permute-start(bf16[256,1280]{1,0:T(8,128)(2,1)} %slice.316), channel_id=1, source_target_pairs={{0,16},{8,24},{16,0},{24,8},{1,17},{9,25},{17,1},{25,9},{2,18},{10... | collective-permute-start | bytes 1966088 | tf_op jit(solution)/shard_map/ppermute | solution.py:879
  661.6 20.8 %collective-permute-start.20 = (bf16[160,768]{1,0:T(8,128)(2,1)S(1)}, bf16[160,768]{1,0:T(8,128)(2,1)S(1)}, u32[]{:S(2)}, u32[]{:S(2)}) collective-permute-start(bf16[160,768]{1,0:T(8,128)(2,1)S(1)} %add_convert_fusion.5), channel_id=1, source_target_pairs={{0,16},{8,24},{16,0},{24,8},{1,17},{9,25},{17,1},{25,9},{2,18},{10... | collective-permute-start | bytes 737288 | tf_op jit(solution)/shard_map/ppermute | solution.py:879
  704.3 28.9 %collective-permute-start.23 = (bf16[640,1280]{1,0:T(8,128)(2,1)}, bf16[640,1280]{1,0:T(8,128)(2,1)S(1)}, u32[]{:S(2)}, u32[]{:S(2)}) collective-permute-start(bf16[640,1280]{1,0:T(8,128)(2,1)} %get-tuple-element.344), channel_id=1, source_target_pairs={{0,8},{8,0},{16,24},{24,16},{1,9},{9,1},{17,25},{25,17},{2,10},{10... | collective-permute-start | bytes 4915208 | tf_op jit(solution)/shard_map/ppermute | solution.py:879
  704.3 24.5 %collective-permute-start.24 = (bf16[384,1280]{1,0:T(8,128)(2,1)}, bf16[384,1280]{1,0:T(8,128)(2,1)}, u32[]{:S(2)}, u32[]{:S(2)}) collective-permute-start(bf16[384,1280]{1,0:T(8,128)(2,1)} %slice.317), channel_id=1, source_target_pairs={{0,16},{8,24},{16,0},{24,8},{1,17},{9,25},{17,1},{25,9},{2,18},{10... | collective-permute-start | bytes 2949128 | tf_op jit(solution)/shard_map/ppermute | solution.py:879
  704.6 17.9 %all-to-all-start.8 = ((bf16[8,40,768]{2,1,0:T(8,128)(2,1)}), bf16[8,40,768]{2,1,0:T(8,128)(2,1)S(1)}, u32[]{:S(2)}, u32[]{:S(2)}) async-start(bf16[8,40,768]{2,1,0:T(8,128)(2,1)} %fusion.8), calls=%async_computation.11 | async-start | bytes 983040 | tf_op jit(solution)/shard_map/all_to_all | solution.py:908
  (77 other events, 714.0 us)
Sparse Core Ops, SparseCore 0:
  12.2 68.6 all-gather.4
  83.1 92.7 all-gather.6
  178.6 64.1 all-gather.8
  244.9 92.7 all-gather.10
  407.1 63.9 reduce-scatter.3
  511.2 65.3 reduce-scatter.5
  580.0 65.5 reduce-scatter.7

commit v4 on v3

--- a/solution.py
+++ b/solution.py
@@ -21,7 +21,8 @@
 ROFF = 8
 NEG = -1e30
 BLOCK = 256
-CHUNK = 512
+KEYS = 512
+CHUNK = 1024
 WIDE = D + AR
 PART = D + 2 * AR
 SIDE = 3 * PART
@@ -310,33 +311,33 @@
             dt_s[h, HD:, i * 128 : (i + 1) * 128] = with_parts(0.0, extra, -delta).astype(BF)
     for h in range(local_heads):
         wait_all(loads[h])
-        for i in range(GLEN // BLOCK):
-            kt_s[:, i * BLOCK : (i + 1) * BLOCK] = k_s[h, i * BLOCK : (i + 1) * BLOCK, :].T
-        for j in range(GLEN // BLOCK):
-            k0 = j * BLOCK
-            kb = k_s[h, k0 : k0 + BLOCK, :]
-            vb = v_s[h, k0 : k0 + BLOCK, :]
-            dk = jnp.zeros((BLOCK, 128), F32)
-            dv = jnp.zeros((BLOCK, 128), F32)
+        for i in range(GLEN // KEYS):
+            kt_s[:, i * KEYS : (i + 1) * KEYS] = k_s[h, i * KEYS : (i + 1) * KEYS, :].T
+        for j in range(GLEN // KEYS):
+            k0 = j * KEYS
+            kb = k_s[h, k0 : k0 + KEYS, :]
+            vb = v_s[h, k0 : k0 + KEYS, :]
+            dk = jnp.zeros((KEYS, 128), F32)
+            dv = jnp.zeros((KEYS, 128), F32)
             q0 = k0
             while q0 < GLEN:
-                n = BLOCK if q0 == k0 else min(CHUNK, GLEN - q0)
+                n = KEYS if q0 == k0 else min(CHUNK, GLEN - q0)
                 qs = slice(q0, q0 + n)
                 probs = jnp.exp2(dot(kb, q_s[h, qs, :], NT))
                 if q0 == k0 or k0 >= PROMPT:
-                    keys = lax.broadcasted_iota(jnp.int32, (BLOCK, n), 0) + k0
-                    queries = lax.broadcasted_iota(jnp.int32, (BLOCK, n), 1) + q0
+                    keys = lax.broadcasted_iota(jnp.int32, (KEYS, n), 0) + k0
+                    queries = lax.broadcasted_iota(jnp.int32, (KEYS, n), 1) + q0
                     probs = jnp.where(allowed_pairs(meta, queries, keys, q0, k0), probs, 0.0)
                 dscore = (probs * dot(vb, dt_s[h, :, qs])).astype(BF)
                 dv = dv + dot(probs.astype(BF), dt_s[h, :, qs], NT)
                 dk = dk + dot(dscore, q_s[h, qs, :])
-                dq = dot(kt_s[:, k0 : k0 + BLOCK], dscore)
+                dq = dot(kt_s[:, k0 : k0 + KEYS], dscore)
                 if j == 0:
                     dqt_s[:, qs] = dq
                 else:
                     dqt_s[:, qs] += dq
                 q0 += n
-            r = slice(k0, k0 + BLOCK)
+            r = slice(k0, k0 + KEYS)
             out[r, width + h * HD : width + (h + 1) * HD] = (dk[:, :HD] * LN2).astype(BF)
             out[r, 2 * width + h * HD : 2 * width + (h + 1) * HD] = dv[:, :HD].astype(BF)
             out[r, h * HD : (h + 1) * HD] = (dqt_s[:, r].T * factor[...]).astype(BF)[:, :HD]

time: 762 us -> 757 us (level)
  transfers between devices with their start and end apart: 42 -> 42, of which waited for: 25 -> 25; matrix products, arithmetic and copies ran while one was open for 5% -> 5% of each run, Pallas kernels for 51% -> 50%
where the time goes in v4:
time: 757 us; the launch traced here: 748 us
  Pallas kernels  421 us (56%)
  waiting for transfers between devices  188 us (25%)
  starting transfers between devices  44.5 us (6%)
  local copies, waits for them, and re-layouts  42.9 us (6%)
  other arithmetic  19.5 us (3%)
  blocking collectives  16.5 us (2%)
  between operations  15.5 us (2%)
    all_gather x4, waiting for transfers between devices, gathered(): return lax.all_gather(value, 'fsdp', axis=0, tiled=True)  107 us
    pallas_call x4, Pallas kernels, attend_back(): call(attend_back_kernel, 'attend_back', (shape((GLEN, 3 * local_heads * H...  99.1 us
    pallas_call x4, Pallas kernels, attend(): call(partial(attend_kernel, groups=len(heads), local_heads=local_heads),...  75.9 us
    pallas_call x4, Pallas kernels, project(): call(partial(project_kernel, arrays=arrays, pieces=len(weights), parts=pa...  56.4 us
    pallas_call x4, Pallas kernels, project_back(): call(partial(project_back_kernel, arrays=arrays, pieces=len(weights), par...  52.6 us
    ppermute x27, waiting for transfers between devices, swap(): return lax.ppermute(value, axis, [(i, i ^ step) for i in range(count)])  47.8 us
    pallas_call x2, Pallas kernels, feed_back(): call(partial(feed_back_kernel, parts=parts, pieces=2, block=math.gcd(rows...  43.1 us
    pallas_call x2, Pallas kernels, feed(): call(partial(feed_kernel, parts=len(mixed), pieces=2, block=math.gcd(rows...  38.9 us
  transfers between devices with their start and end apart: 42, of which 25 were waited for; matrix products, arithmetic and copies ran while one was open for 5% of the time, Pallas kernels for 50%

profile of v4, /device:TPU:0, one launch (start us, length us, event | category | flops | bytes accessed | tf_op | source)
XLA Modules:
  0.0 748.0 jit_solution(541570032684902824)
XLA Ops:
  22.7 58.2 %all-gather.5.cloned.1.call-done = bf16[1280,1344]{1,0:T(8,128)(2,1)} async-done(((bf16[160,1344]{1,0:T(8,128)(2,1)}), bf16[1280,1344]{1,0:T(8,128)(2,1)}) %all-gather.5.cloned.1.call-update) | async-done | bytes 3440656 | tf_op jit(solution)/shard_map/all_gather | solution.py:1002
  88.4 14.2 %project.4 = (bf16[1280,480]{1,0:T(8,128)(2,1)}, bf16[1280,480]{1,0:T(8,128)(2,1)}, bf16[1280,384]{1,0:T(8,128)(2,1)}) custom-call(s32[8]{0:T(128)} %copy-done.55, f32[1,960]{1,0:T(1,128)} %reshape_tile.6.refs_1_, bf16[640,1280]{1,0:T(8,128)(2,1)} %multiply_convert_fusion.refs_2_.refs_6_, bf16[640,1280]{1,0:T(8,128)(2,1)} %collective-permute-done.refs_3_.refs_7_, ...), custom_call_target="tpu_custom_call" | custom-call | flops 14949999616 | bytes 1024 | tf_op jit(solution)/shard_map/project/pallas_call | solution.py:170
  107.5 13.7 %project.5 = (bf16[1280,480]{1,0:T(8,128)(2,1)}, bf16[1280,480]{1,0:T(8,128)(2,1)}, bf16[1280,384]{1,0:T(8,128)(2,1)}) custom-call(s32[8]{0:T(128)} %copy-done.56, f32[1,960]{1,0:T(1,128)} %reshape_tile.6.refs_1_, bf16[640,1280]{1,0:T(8,128)(2,1)} %copy-done.19, bf16[640,1280]{1,0:T(8,128)(2,1)} %copy-done.20, bf16[1,1280,1344]{2,1,0:T(8,128)(2,1)} %bitcast.217, ...), custom_call_target="tpu_custom_call" | custom-call | flops 14949999616 | bytes 1024 | tf_op jit(solution)/shard_map/project/pallas_call | solution.py:170
  121.3 19.4 %attend.4 = (bf16[4,160,640]{2,1,0:T(8,128)(2,1)}, bf16[3,2,2560,128]{3,2,1,0:T(8,128)(2,1)}) custom-call(s32[8]{0:T(128)} %copy-done.50, bf16[1280,480]{1,0:T(8,128)(2,1)} %get-tuple-element.219.refs_1_, bf16[1280,480]{1,0:T(8,128)(2,1)} %get-tuple-element.223.refs_2_), custom_call_target="tpu_custom_call" | custom-call | flops 18400000000 | bytes 1024 | tf_op jit(solution)/shard_map/attend/pallas_call | solution.py:277
  144.3 19.0 %attend.5 = (bf16[4,160,640]{2,1,0:T(8,128)(2,1)}, bf16[3,2,2560,128]{3,2,1,0:T(8,128)(2,1)}) custom-call(s32[8]{0:T(128)} %copy-done.50, bf16[1280,480]{1,0:T(8,128)(2,1)} %get-tuple-element.227.refs_1_, bf16[1280,480]{1,0:T(8,128)(2,1)} %get-tuple-element.229.refs_2_), custom_call_target="tpu_custom_call" | custom-call | flops 18400000000 | bytes 1024 | tf_op jit(solution)/shard_map/attend/pallas_call | solution.py:277
  194.0 20.3 %feed.2 = (f32[640,1280]{1,0:T(8,128)}, f32[640,1280]{1,0:T(8,128)}, bf16[640,384]{1,0:T(8,128)(2,1)}, f32[640,1280]{1,0:T(8,128)}, bf16[640,1280]{1,0:T(8,128)(2,1)}) custom-call(s32[8]{0:T(128)} %copy-done.50, f32[1,1280]{1,0:T(1,128)} %get-tuple-element.415.refs_1_.refs_0_, f32[1,1280]{1,0:T(1,128)} %get-tuple-element.413.refs_2_.refs_7_, ...), custom_call_target="tpu_custom_call" | custom-call | flops 19549999104 | bytes 1024 | tf_op jit(solution)/shard_map/feed/pallas_call | solution.py:446
  218.9 24.0 %all-gather.9.cloned.1.call-done = bf16[1280,1344]{1,0:T(8,128)(2,1)} async-done(((bf16[160,1344]{1,0:T(8,128)(2,1)}), bf16[1280,1344]{1,0:T(8,128)(2,1)}) %all-gather.9.cloned.1.call-update) | async-done | bytes 3440656 | tf_op jit(solution)/shard_map/all_gather | solution.py:1002
  249.8 14.3 %project.6 = (bf16[1280,480]{1,0:T(8,128)(2,1)}, bf16[1280,480]{1,0:T(8,128)(2,1)}, bf16[1280,384]{1,0:T(8,128)(2,1)}) custom-call(s32[8]{0:T(128)} %copy-done.55, f32[1,960]{1,0:T(1,128)} %reshape_tile.7.refs_1_, bf16[640,1280]{1,0:T(8,128)(2,1)} %get-tuple-element.239.refs_2_.refs_6_, bf16[640,1280]{1,0:T(8,128)(2,1)} %collective-permute-done.7.refs_3_.refs_7_, ...), custom_call_target="tpu_custom_call" | custom-call | flops 14949999616 | bytes 1024 | tf_op jit(solution)/shard_map/project/pallas_call | solution.py:170
  270.1 14.3 %project.7 = (bf16[1280,480]{1,0:T(8,128)(2,1)}, bf16[1280,480]{1,0:T(8,128)(2,1)}, bf16[1280,384]{1,0:T(8,128)(2,1)}) custom-call(s32[8]{0:T(128)} %copy-done.56, f32[1,960]{1,0:T(1,128)} %reshape_tile.7.refs_1_, bf16[640,1280]{1,0:T(8,128)(2,1)} %copy-done.5, bf16[640,1280]{1,0:T(8,128)(2,1)} %copy-done.21, bf16[1,1280,1344]{2,1,0:T(8,128)(2,1)} %bitcast.222, ...), custom_call_target="tpu_custom_call" | custom-call | flops 14949999616 | bytes 1024 | tf_op jit(solution)/shard_map/project/pallas_call | solution.py:170
  284.3 18.8 %attend.6 = (bf16[4,160,640]{2,1,0:T(8,128)(2,1)}, bf16[3,2,2560,128]{3,2,1,0:T(8,128)(2,1)}) custom-call(s32[8]{0:T(128)} %copy-done.50, bf16[1280,480]{1,0:T(8,128)(2,1)} %get-tuple-element.246.refs_1_, bf16[1280,480]{1,0:T(8,128)(2,1)} %get-tuple-element.249.refs_2_), custom_call_target="tpu_custom_call" | custom-call | flops 18400000000 | bytes 1024 | tf_op jit(solution)/shard_map/attend/pallas_call | solution.py:277
  306.8 18.7 %attend.7 = (bf16[4,160,640]{2,1,0:T(8,128)(2,1)}, bf16[3,2,2560,128]{3,2,1,0:T(8,128)(2,1)}) custom-call(s32[8]{0:T(128)} %copy-done.50, bf16[1280,480]{1,0:T(8,128)(2,1)} %get-tuple-element.253.refs_1_, bf16[1280,480]{1,0:T(8,128)(2,1)} %get-tuple-element.255.refs_2_), custom_call_target="tpu_custom_call" | custom-call | flops 18400000000 | bytes 1024 | tf_op jit(solution)/shard_map/attend/pallas_call | solution.py:277
  337.6 16.5 %all_to_all.45.refs_5_.refs_10_ = bf16[4,160,640]{2,1,0:T(8,128)(2,1)} all-to-all(bf16[4,160,640]{2,1,0:T(8,128)(2,1)} %get-tuple-element.259.o_ref), channel_id=1, replica_groups=mesh['seq'=4,'fsdp'=8] {'seq'}, dimensions={0} | all-to-all | bytes 1638400 | tf_op jit(solution)/shard_map/all_to_all | solution.py:1010
  354.1 18.6 %feed.3 = (f32[640,1280]{1,0:T(8,128)}, f32[640,1280]{1,0:T(8,128)}, bf16[640,384]{1,0:T(8,128)(2,1)}, bf16[640,1280]{1,0:T(8,128)(2,1)}) custom-call(s32[8]{0:T(128)} %copy-done.50, f32[1,1280]{1,0:T(1,128)} %get-tuple-element.416.refs_1_.refs_0_, f32[1,1280]{1,0:T(1,128)} %get-tuple-element.414.refs_2_.gain, ...), custom_call_target="tpu_custom_call" | custom-call | flops 19549999104 | bytes 1024 | tf_op jit(solution)/shard_map/feed/pallas_call | solution.py:446
  372.7 18.7 %feed_back.2 = (f32[640,1280]{1,0:T(8,128)}, bf16[640,1280]{1,0:T(8,128)(2,1)}, bf16[640,1408]{1,0:T(8,128)(2,1)}, bf16[640,128]{1,0:T(8,128)(2,1)}, bf16[640,12...) custom-call(s32[8]{0:T(128)} %copy-done.50, ...), custom_call_target="tpu_custom_call" | custom-call | flops 57500000 | bytes 1024 | tf_op jit(solution)/shard_map/feed_back/pallas_call | solution.py:585
  412.4 24.7 %attend_back.4.refs_1_ = bf16[2560,480]{1,0:T(8,128)(2,1)} custom-call(s32[8]{0:T(128)} %copy-done.50, f32[1,128]{1,0:T(1,128)} %pad_bitcast_fusion.1.factor, bf16[3,2,2560,128]{3,2,1,0:T(8,128)(2,1)} %get-tuple-element.269.saved, bf16[4,160,640]{2,1,0:T(8,128)(2,1)} %get-tuple-element.270.o_ref, bf16[4,160,640]{2,1,0:T(8,128)(2,1)} %copy-done.7), custom_call_target="tpu_custom_call" | custom-call | flops 57500000 | bytes 1024 | tf_op jit(solution)/shard_map/attend_back/pallas_call | solution.py:349
  438.0 24.7 %attend_back.5.refs_2_ = bf16[2560,480]{1,0:T(8,128)(2,1)} custom-call(s32[8]{0:T(128)} %copy-done.50, f32[1,128]{1,0:T(1,128)} %pad_bitcast_fusion.1.factor, bf16[3,2,2560,128]{3,2,1,0:T(8,128)(2,1)} %get-tuple-element.261.saved, bf16[4,160,640]{2,1,0:T(8,128)(2,1)} %get-tuple-element.259.o_ref, bf16[4,160,640]{2,1,0:T(8,128)(2,1)} %copy-done.9), custom_call_target="tpu_custom_call" | custom-call | flops 57500000 | bytes 1024 | tf_op jit(solution)/shard_map/attend_back/pallas_call | solution.py:349
  462.7 14.8 %project_back.4 = (bf16[640,1280]{1,0:T(8,128)(2,1)}, bf16[640,1280]{1,0:T(8,128)(2,1)}, bf16[1280,384]{1,0:T(8,128)(2,1)}) custom-call(s32[8]{0:T(128)} %copy-done.56, bf16[2560,480]{1,0:T(8,128)(2,1)} %attend_back.4.refs_1_, bf16[2560,480]{1,0:T(8,128)(2,1)} %attend_back.5.refs_2_, bf16[1,1280,1344]{2,1,0:T(8,128)(2,1)} %bitcast.223, ...), custom_call_target="tpu_custom_call" | custom-call | flops 57500000 | bytes 1024 | tf_op jit(solution)/shard_map/project_back/pallas_call | solution.py:758
  486.3 14.6 %project_sums.2 = (bf16[1280,768]{1,0:T(8,128)(2,1)}, bf16[1280,384]{1,0:T(8,128)(2,1)}) custom-call(s32[8]{0:T(128)} %copy-done.50, bf16[2560,480]{1,0:T(8,128)(2,1)} %attend_back.4.refs_1_, bf16[2560,480]{1,0:T(8,128)(2,1)} %attend_back.5.refs_2_, bf16[1280,384]{1,0:T(8,128)(2,1)} %get-tuple-element.289.refs_3_, ...), custom_call_target="tpu_custom_call" | custom-call | flops 57500000 | bytes 1024 | tf_op jit(solution)/shard_map/project_sums/pallas_call | solution.py:863
  530.7 24.3 %feed_back.3 = (f32[640,1280]{1,0:T(8,128)}, bf16[640,1280]{1,0:T(8,128)(2,1)}, bf16[640,1408]{1,0:T(8,128)(2,1)}, bf16[640,128]{1,0:T(8,128)(2,1)}, bf16[640,12...) custom-call(s32[8]{0:T(128)} %copy-done.50, ...), custom_call_target="tpu_custom_call" | custom-call | flops 57500000 | bytes 1024 | tf_op jit(solution)/shard_map/feed_back/pallas_call | solution.py:585
  581.8 25.0 %attend_back.6.refs_1_ = bf16[2560,480]{1,0:T(8,128)(2,1)} custom-call(s32[8]{0:T(128)} %copy-done.50, f32[1,128]{1,0:T(1,128)} %pad_bitcast_fusion.factor, bf16[3,2,2560,128]{3,2,1,0:T(8,128)(2,1)} %get-tuple-element.307.saved, bf16[4,160,640]{2,1,0:T(8,128)(2,1)} %get-tuple-element.308.o_ref, bf16[4,160,640]{2,1,0:T(8,128)(2,1)} %copy-done.6), custom_call_target="tpu_custom_call" | custom-call | flops 57500000 | bytes 1024 | tf_op jit(solution)/shard_map/attend_back/pallas_call | solution.py:349
  607.7 24.7 %attend_back.7.refs_2_ = bf16[2560,480]{1,0:T(8,128)(2,1)} custom-call(s32[8]{0:T(128)} %copy-done.50, f32[1,128]{1,0:T(1,128)} %pad_bitcast_fusion.factor, bf16[3,2,2560,128]{3,2,1,0:T(8,128)(2,1)} %get-tuple-element.235.saved, bf16[4,160,640]{2,1,0:T(8,128)(2,1)} %get-tuple-element.233.o_ref, bf16[4,160,640]{2,1,0:T(8,128)(2,1)} %copy-done.8), custom_call_target="tpu_custom_call" | custom-call | flops 57500000 | bytes 1024 | tf_op jit(solution)/shard_map/attend_back/pallas_call | solution.py:349
  633.7 14.6 %project_back.6 = (bf16[640,1280]{1,0:T(8,128)(2,1)}, bf16[640,1280]{1,0:T(8,128)(2,1)}, bf16[1280,384]{1,0:T(8,128)(2,1)}) custom-call(s32[8]{0:T(128)} %copy-done.56, bf16[2560,480]{1,0:T(8,128)(2,1)} %attend_back.6.refs_1_, bf16[2560,480]{1,0:T(8,128)(2,1)} %attend_back.7.refs_2_, bf16[1,1280,1344]{2,1,0:T(8,128)(2,1)} %bitcast.218, ...), custom_call_target="tpu_custom_call" | custom-call | flops 57500000 | bytes 1024 | tf_op jit(solution)/shard_map/project_back/pallas_call | solution.py:758
  659.2 14.7 %project_sums.3 = (bf16[1280,768]{1,0:T(8,128)(2,1)}, bf16[1280,384]{1,0:T(8,128)(2,1)}) custom-call(s32[8]{0:T(128)} %copy-done.50, bf16[2560,480]{1,0:T(8,128)(2,1)} %attend_back.6.refs_1_, bf16[2560,480]{1,0:T(8,128)(2,1)} %attend_back.7.refs_2_, bf16[1280,384]{1,0:T(8,128)(2,1)} %get-tuple-element.221.refs_3_, ...), custom_call_target="tpu_custom_call" | custom-call | flops 57500000 | bytes 1024 | tf_op jit(solution)/shard_map/project_sums/pallas_call | solution.py:863
  704.2 13.6 %all-to-all-done.8 = bf16[8,40,768]{2,1,0:T(8,128)(2,1)S(1)} async-done(((bf16[8,40,768]{2,1,0:T(8,128)(2,1)}), bf16[8,40,768]{2,1,0:T(8,128)(2,1)S(1)}, u32[]{:S(2)}, u32[]{:S(2)}) %all-to-all-start.8) | async-done | bytes 491552 | tf_op jit(solution)/shard_map/all_to_all | solution.py:909
  (286 shorter events, 248.1 us)
Async XLA Ops:
  7.2 73.7 %all-gather.5.cloned.1.call-start = ((), (), s32[]{:S(2)}) async-start(), calls=%async_computation.12 | async-start | bytes 4055040 | tf_op jit(solution)/shard_map/all_gather | solution.py:1002
  12.1 163.8 %all-gather.7.cloned.1.call-start = ((), (), s32[]{:S(2)}) async-start(), calls=%async_computation.13 | async-start | bytes 6635520 | tf_op jit(solution)/shard_map/all_gather | solution.py:1002
  14.8 66.2 %collective-permute-start.1 = (bf16[640,1280]{1,0:T(8,128)(2,1)}, bf16[640,1280]{1,0:T(8,128)(2,1)S(1)}, u32[]{:S(2)}, u32[]{:S(2)}) collective-permute-start(bf16[640,1280]{1,0:T(8,128)(2,1)} %multiply_convert_fusion.refs_2_.refs_6_), channel_id=1, source_target_pairs={{0,16},{8,24},{16,0},{24,8},{1,17},{9,25},{17,1},{25,9},{2,18},{10... | collective-permute-start | bytes 4915208 | tf_op jit(solution)/shard_map/ppermute | solution.py:880
  140.7 22.7 %all-to-all-start = ((bf16[4,160,640]{2,1,0:T(8,128)(2,1)}), bf16[4,160,640]{2,1,0:T(8,128)(2,1)S(1)}, u32[]{:S(2)}, u32[]{:S(2)}) async-start(bf16[4,160,640]{2,1,0:T(8,128)(2,1)} %get-tuple-element.308.o_ref), calls=%async_computation | async-start | bytes 1638400 | tf_op jit(solution)/shard_map/all_to_all | solution.py:1010
  144.3 98.6 %all-gather.9.cloned.1.call-start = ((), (), s32[]{:S(2)}) async-start(), calls=%async_computation.14 | async-start | bytes 4055040 | tf_op jit(solution)/shard_map/all_gather | solution.py:1002
  175.9 17.2 %collective-permute-start.4 = (bf16[1280,2304]{1,0:T(8,128)(2,1)}, bf16[1280,2304]{1,0:T(8,128)(2,1)}, u32[]{:S(2)}, u32[]{:S(2)}) collective-permute-start(bf16[1280,2304]{1,0:T(8,128)(2,1)} %all-gather.7.cloned.1.call-done.refs_6_.refs_5_), channel_id=1, source_target_pairs={{0,8},{8,0},{16,24},{24,16},{1,9},{9,1},{17,25},{25,17},{2,10},{10... | collective-permute-start | bytes 17694728 | tf_op jit(solution)/shard_map/ppermute | solution.py:880
  181.1 156.5 %all-gather.11.cloned.1.call-start = ((), (), s32[]{:S(2)}) async-start(), calls=%async_computation.15 | async-start | bytes 6635520 | tf_op jit(solution)/shard_map/all_gather | solution.py:1002
  216.7 26.1 %collective-permute-start.5 = (bf16[384,1280]{1,0:T(8,128)(2,1)}, bf16[384,1280]{1,0:T(8,128)(2,1)S(1)}, u32[]{:S(2)}, u32[]{:S(2)}) collective-permute-start(bf16[384,1280]{1,0:T(8,128)(2,1)} %slice.295), channel_id=1, source_target_pairs={{0,16},{8,24},{16,0},{24,8},{1,17},{9,25},{17,1},{25,9},{2,18},{10... | collective-permute-start | bytes 2949128 | tf_op jit(solution)/shard_map/ppermute | solution.py:880
  246.8 17.3 %collective-permute-start.6 = (bf16[256,1280]{1,0:T(8,128)(2,1)S(1)}, bf16[256,1280]{1,0:T(8,128)(2,1)}, u32[]{:S(2)}, u32[]{:S(2)}) collective-permute-start(bf16[256,1280]{1,0:T(8,128)(2,1)S(1)} %slice.296), channel_id=1, source_target_pairs={{0,16},{8,24},{16,0},{24,8},{1,17},{9,25},{17,1},{25,9},{2,18},{10... | collective-permute-start | bytes 1966088 | tf_op jit(solution)/shard_map/ppermute | solution.py:880
  303.1 22.4 %all-to-all-start.2 = ((bf16[4,160,640]{2,1,0:T(8,128)(2,1)}), bf16[4,160,640]{2,1,0:T(8,128)(2,1)S(1)}, u32[]{:S(2)}, u32[]{:S(2)}) async-start(bf16[4,160,640]{2,1,0:T(8,128)(2,1)} %get-tuple-element.270.o_ref), calls=%async_computation.2 | async-start | bytes 1638400 | tf_op jit(solution)/shard_map/all_to_all | solution.py:1010
  337.6 16.5 %collective-permute-start.10 = (bf16[1280,2304]{1,0:T(8,128)(2,1)}, bf16[1280,2304]{1,0:T(8,128)(2,1)}, u32[]{:S(2)}, u32[]{:S(2)}) collective-permute-start(bf16[1280,2304]{1,0:T(8,128)(2,1)} %all-gather.11.cloned.1.call-done.refs_6_.refs_5_), channel_id=1, source_target_pairs={{0,8},{8,0},{16,24},{24,16},{1,9},{9,1},{17,25},{25,17},{2,10},{10... | collective-permute-start | bytes 17694728 | tf_op jit(solution)/shard_map/ppermute | solution.py:880
  394.9 88.4 %reduce-scatter.4.cloned.1.call-start = ((), (), s32[]{:S(2)}) async-start(), calls=%async_computation.16 | async-start | bytes 2211840 | tf_op jit(solution)/shard_map/reduce_scatter | solution.py:918
  407.8 29.3 %all-to-all-start.5 = ((bf16[4,160,640]{2,1,0:T(8,128)(2,1)}), bf16[4,160,640]{2,1,0:T(8,128)(2,1)S(1)}, u32[]{:S(2)}, u32[]{:S(2)}) async-start(bf16[4,160,640]{2,1,0:T(8,128)(2,1)} %get-tuple-element.280), calls=%async_computation.5 | async-start | bytes 1638400 | tf_op jit(solution)/shard_map/all_to_all | solution.py:1013
  411.3 162.9 %reduce-scatter.6.cloned.1.call-start = ((), (), s32[]{:S(2)}) async-start(), calls=%async_computation.17 | async-start | bytes 2211840 | tf_op jit(solution)/shard_map/reduce_scatter | solution.py:918
  484.4 24.2 %collective-permute-start.12 = (bf16[384,1280]{1,0:T(8,128)(2,1)}, bf16[384,1280]{1,0:T(8,128)(2,1)S(1)}, u32[]{:S(2)}, u32[]{:S(2)}) collective-permute-start(bf16[384,1280]{1,0:T(8,128)(2,1)} %slice.314), channel_id=1, source_target_pairs={{0,16},{8,24},{16,0},{24,8},{1,17},{9,25},{17,1},{25,9},{2,18},{10... | collective-permute-start | bytes 2949128 | tf_op jit(solution)/shard_map/ppermute | solution.py:880
  508.7 16.3 %collective-permute-start.13 = (bf16[256,1280]{1,0:T(8,128)(2,1)S(1)}, bf16[256,1280]{1,0:T(8,128)(2,1)S(1)}, u32[]{:S(2)}, u32[]{:S(2)}) collective-permute-start(bf16[256,1280]{1,0:T(8,128)(2,1)S(1)} %slice.315), channel_id=1, source_target_pairs={{0,16},{8,24},{16,0},{24,8},{1,17},{9,25},{17,1},{25,9},{2,18},{10... | collective-permute-start | bytes 1966088 | tf_op jit(solution)/shard_map/ppermute | solution.py:880
  558.6 95.4 %reduce-scatter.8.cloned.1.call-start = ((), (), s32[]{:S(2)}) async-start(), calls=%async_computation.18 | async-start | bytes 2211840 | tf_op jit(solution)/shard_map/reduce_scatter | solution.py:918
  575.4 31.4 %all-to-all-start.7 = ((bf16[4,160,640]{2,1,0:T(8,128)(2,1)}), bf16[4,160,640]{2,1,0:T(8,128)(2,1)S(1)}, u32[]{:S(2)}, u32[]{:S(2)}) async-start(bf16[4,160,640]{2,1,0:T(8,128)(2,1)} %get-tuple-element.319), calls=%async_computation.8 | async-start | bytes 1638400 | tf_op jit(solution)/shard_map/all_to_all | solution.py:1013
  579.3 53.1 %collective-permute-start.16 = (bf16[2,160,768]{2,1,0:T(8,128)(2,1)S(1)}, bf16[2,160,768]{2,1,0:T(8,128)(2,1)}, u32[]{:S(2)}, u32[]{:S(2)}) collective-permute-start(bf16[2,160,768]{2,1,0:T(8,128)(2,1)S(1)} %add_convert_fusion.3), channel_id=1, source_target_pairs={{0,16},{8,24},{16,0},{24,8},{1,17},{9,25},{17,1},{25,9},{2,18},{10... | collective-permute-start | bytes 1474568 | tf_op jit(solution)/shard_map/ppermute | solution.py:880
  655.1 23.3 %collective-permute-start.18 = (bf16[256,1280]{1,0:T(8,128)(2,1)}, bf16[256,1280]{1,0:T(8,128)(2,1)S(1)}, u32[]{:S(2)}, u32[]{:S(2)}) collective-permute-start(bf16[256,1280]{1,0:T(8,128)(2,1)} %slice.316), channel_id=1, source_target_pairs={{0,16},{8,24},{16,0},{24,8},{1,17},{9,25},{17,1},{25,9},{2,18},{10... | collective-permute-start | bytes 1966088 | tf_op jit(solution)/shard_map/ppermute | solution.py:880
  656.8 20.8 %collective-permute-start.20 = (bf16[160,768]{1,0:T(8,128)(2,1)S(1)}, bf16[160,768]{1,0:T(8,128)(2,1)S(1)}, u32[]{:S(2)}, u32[]{:S(2)}) collective-permute-start(bf16[160,768]{1,0:T(8,128)(2,1)S(1)} %add_convert_fusion.5), channel_id=1, source_target_pairs={{0,16},{8,24},{16,0},{24,8},{1,17},{9,25},{17,1},{25,9},{2,18},{10... | collective-permute-start | bytes 737288 | tf_op jit(solution)/shard_map/ppermute | solution.py:880
  699.5 28.9 %collective-permute-start.23 = (bf16[640,1280]{1,0:T(8,128)(2,1)}, bf16[640,1280]{1,0:T(8,128)(2,1)S(1)}, u32[]{:S(2)}, u32[]{:S(2)}) collective-permute-start(bf16[640,1280]{1,0:T(8,128)(2,1)} %get-tuple-element.344), channel_id=1, source_target_pairs={{0,8},{8,0},{16,24},{24,16},{1,9},{9,1},{17,25},{25,17},{2,10},{10... | collective-permute-start | bytes 4915208 | tf_op jit(solution)/shard_map/ppermute | solution.py:880
  699.5 24.5 %collective-permute-start.24 = (bf16[384,1280]{1,0:T(8,128)(2,1)}, bf16[384,1280]{1,0:T(8,128)(2,1)}, u32[]{:S(2)}, u32[]{:S(2)}) collective-permute-start(bf16[384,1280]{1,0:T(8,128)(2,1)} %slice.317), channel_id=1, source_target_pairs={{0,16},{8,24},{16,0},{24,8},{1,17},{9,25},{17,1},{25,9},{2,18},{10... | collective-permute-start | bytes 2949128 | tf_op jit(solution)/shard_map/ppermute | solution.py:880
  699.9 17.9 %all-to-all-start.8 = ((bf16[8,40,768]{2,1,0:T(8,128)(2,1)}), bf16[8,40,768]{2,1,0:T(8,128)(2,1)S(1)}, u32[]{:S(2)}, u32[]{:S(2)}) async-start(bf16[8,40,768]{2,1,0:T(8,128)(2,1)} %fusion.8), calls=%async_computation.11 | async-start | bytes 983040 | tf_op jit(solution)/shard_map/all_to_all | solution.py:909
  (77 other events, 714.7 us)
Sparse Core Ops, SparseCore 0:
  12.2 68.6 all-gather.4
  83.1 92.7 all-gather.6
  178.6 64.1 all-gather.8
  244.9 92.7 all-gather.10
  407.0 63.9 reduce-scatter.3
  508.8 65.4 reduce-scatter.5
  577.7 65.6 reduce-scatter.7

commit v5 on v4

--- a/solution.py
+++ b/solution.py
@@ -1067,8 +1067,8 @@
             if p < parts - 1:
                 mixed.append(to_rows(attended[-1][0]))
         attended, mixed = fence(attended, mixed)
-        side_gathered = after(side_gathered, attended[-1][1])
         mixed = mixed + [to_rows(attended[-1][0])]
+        side_gathered = after(side_gathered, attended[-1][1], mixed[-1])
         side_weights.append((side_gathered, other_core(side_gathered, SIDE // 2)))
         if not last:
             head_gathered = gather_head(layer + 1, attended[-1][1], side_gathered)

time: 757 us -> 756 us (level)
  blocking collectives: 16.5 us -> 32.9 us
  waiting for transfers between devices: 188 us -> 178 us
    all_gather x4, waiting for transfers between devices: 107 us -> 89.9 us  [gathered(): return lax.all_gather(value, 'fsdp', axis=0, tiled=True)]
    all_to_all x1 -> x2, blocking collectives: 16.5 us -> 32.9 us  [to_rows(): return lax.all_to_all(mixed, 'seq', split_axis=0, concat_axis=0, tiled=True)]
    ppermute x27, waiting for transfers between devices: 47.8 us -> 63.9 us  [swap(): return lax.ppermute(value, axis, [(i, i ^ step) for i in range(count)])]
    all_to_all x3 -> x2, waiting for transfers between devices: 10 us -> 0.01 us  [to_rows(): return lax.all_to_all(mixed, 'seq', split_axis=0, concat_axis=0, tiled=True)]
    unnamed x122 -> x102, local copies, waits for them, and re-layouts: 15.6 us -> 12.2 us
  transfers between devices with their start and end apart: 42 -> 41, of which waited for: 25 -> 26; matrix products, arithmetic and copies ran while one was open for 5% -> 5% of each run, Pallas kernels for 50% -> 50%
where the time goes in v5:
time: 756 us; the launch traced here: 747 us
  Pallas kernels  420 us (56%)
  waiting for transfers between devices  178 us (24%)
  starting transfers between devices  40.7 us (5%)
  local copies, waits for them, and re-layouts  40.2 us (5%)
  blocking collectives  32.9 us (4%)
  other arithmetic  20.1 us (3%)
  between operations  15.4 us (2%)
    pallas_call x4, Pallas kernels, attend_back(): call(attend_back_kernel, 'attend_back', (shape((GLEN, 3 * local_heads * H...  99.1 us
    all_gather x4, waiting for transfers between devices, gathered(): return lax.all_gather(value, 'fsdp', axis=0, tiled=True)  89.9 us
    pallas_call x4, Pallas kernels, attend(): call(partial(attend_kernel, groups=len(heads), local_heads=local_heads),...  75.2 us
    ppermute x27, waiting for transfers between devices, swap(): return lax.ppermute(value, axis, [(i, i ^ step) for i in range(count)])  63.9 us
    pallas_call x4, Pallas kernels, project(): call(partial(project_kernel, arrays=arrays, pieces=len(weights), parts=pa...  56.3 us
    pallas_call x4, Pallas kernels, project_back(): call(partial(project_back_kernel, arrays=arrays, pieces=len(weights), par...  52.4 us
    pallas_call x2, Pallas kernels, feed_back(): call(partial(feed_back_kernel, parts=parts, pieces=2, block=math.gcd(rows...  43.1 us
    pallas_call x2, Pallas kernels, feed(): call(partial(feed_kernel, parts=len(mixed), pieces=2, block=math.gcd(rows...  38.9 us
  transfers between devices with their start and end apart: 41, of which 26 were waited for; matrix products, arithmetic and copies ran while one was open for 5% of the time, Pallas kernels for 50%

profile of v5, /device:TPU:0, one launch (start us, length us, event | category | flops | bytes accessed | tf_op | source)
XLA Modules:
  0.0 747.3 jit_solution(7269056899854840972)
XLA Ops:
  23.1 58.5 %all-gather.5.cloned.1.call-done = bf16[1280,1344]{1,0:T(8,128)(2,1)} async-done(((bf16[160,1344]{1,0:T(8,128)(2,1)}), bf16[1280,1344]{1,0:T(8,128)(2,1)}) %all-gather.5.cloned.1.call-update) | async-done | bytes 3440656 | tf_op jit(solution)/shard_map/all_gather | solution.py:1002
  87.8 14.2 %project.4 = (bf16[1280,480]{1,0:T(8,128)(2,1)}, bf16[1280,480]{1,0:T(8,128)(2,1)}, bf16[1280,384]{1,0:T(8,128)(2,1)}) custom-call(s32[8]{0:T(128)} %copy-done.45, f32[1,960]{1,0:T(1,128)} %reshape_tile.6.refs_1_, bf16[640,1280]{1,0:T(8,128)(2,1)} %multiply_convert_fusion.refs_2_.refs_6_, bf16[640,1280]{1,0:T(8,128)(2,1)} %collective-permute-done.refs_3_.refs_7_, ...), custom_call_target="tpu_custom_call" | custom-call | flops 14949999616 | bytes 1024 | tf_op jit(solution)/shard_map/project/pallas_call | solution.py:170
  105.9 13.7 %project.5 = (bf16[1280,480]{1,0:T(8,128)(2,1)}, bf16[1280,480]{1,0:T(8,128)(2,1)}, bf16[1280,384]{1,0:T(8,128)(2,1)}) custom-call(s32[8]{0:T(128)} %copy-done.46, f32[1,960]{1,0:T(1,128)} %reshape_tile.6.refs_1_, bf16[640,1280]{1,0:T(8,128)(2,1)} %collective-permute-done.1.refs_2_.refs_8_, bf16[640,1280]{1,0:T(8,128)(2,1)} %collective-permute-done.3.refs_3_.refs_9_, ...), custom_call_target="tpu_custom_call" | custom-call | flops 14949999616 | bytes 1024 | tf_op jit(solution)/shard_map/project/pallas_call | solution.py:170
  119.6 18.9 %attend.4 = (bf16[4,160,640]{2,1,0:T(8,128)(2,1)}, bf16[3,2,2560,128]{3,2,1,0:T(8,128)(2,1)}) custom-call(s32[8]{0:T(128)} %copy-done.40, bf16[1280,480]{1,0:T(8,128)(2,1)} %get-tuple-element.219.refs_1_, bf16[1280,480]{1,0:T(8,128)(2,1)} %get-tuple-element.223.refs_2_), custom_call_target="tpu_custom_call" | custom-call | flops 18400000000 | bytes 1024 | tf_op jit(solution)/shard_map/attend/pallas_call | solution.py:277
  142.1 18.9 %attend.5 = (bf16[4,160,640]{2,1,0:T(8,128)(2,1)}, bf16[3,2,2560,128]{3,2,1,0:T(8,128)(2,1)}) custom-call(s32[8]{0:T(128)} %copy-done.40, bf16[1280,480]{1,0:T(8,128)(2,1)} %get-tuple-element.227.refs_1_, bf16[1280,480]{1,0:T(8,128)(2,1)} %get-tuple-element.229.refs_2_), custom_call_target="tpu_custom_call" | custom-call | flops 18400000000 | bytes 1024 | tf_op jit(solution)/shard_map/attend/pallas_call | solution.py:277
  161.1 16.4 %all_to_all.45.refs_5_.refs_10_ = bf16[4,160,640]{2,1,0:T(8,128)(2,1)} all-to-all(bf16[4,160,640]{2,1,0:T(8,128)(2,1)} %get-tuple-element.233.o_ref), channel_id=1, replica_groups=mesh['seq'=4,'fsdp'=8] {'seq'}, dimensions={0} | all-to-all | bytes 1638400 | tf_op jit(solution)/shard_map/all_to_all | solution.py:1010
  187.4 20.3 %feed.2 = (f32[640,1280]{1,0:T(8,128)}, f32[640,1280]{1,0:T(8,128)}, bf16[640,384]{1,0:T(8,128)(2,1)}, f32[640,1280]{1,0:T(8,128)}, bf16[640,1280]{1,0:T(8,128)(2,1)}) custom-call(s32[8]{0:T(128)} %copy-done.40, f32[1,1280]{1,0:T(1,128)} %get-tuple-element.415.refs_1_.refs_0_, f32[1,1280]{1,0:T(1,128)} %get-tuple-element.413.refs_2_.refs_7_, ...), custom_call_target="tpu_custom_call" | custom-call | flops 19549999104 | bytes 1024 | tf_op jit(solution)/shard_map/feed/pallas_call | solution.py:446
  212.0 31.4 %all-gather.9.cloned.1.call-done = bf16[1280,1344]{1,0:T(8,128)(2,1)} async-done(((bf16[160,1344]{1,0:T(8,128)(2,1)}), bf16[1280,1344]{1,0:T(8,128)(2,1)}) %all-gather.9.cloned.1.call-update) | async-done | bytes 3440656 | tf_op jit(solution)/shard_map/all_gather | solution.py:1002
  249.4 14.2 %project.6 = (bf16[1280,480]{1,0:T(8,128)(2,1)}, bf16[1280,480]{1,0:T(8,128)(2,1)}, bf16[1280,384]{1,0:T(8,128)(2,1)}) custom-call(s32[8]{0:T(128)} %copy-done.45, f32[1,960]{1,0:T(1,128)} %reshape_tile.7.refs_1_, bf16[640,1280]{1,0:T(8,128)(2,1)} %get-tuple-element.239.refs_2_.refs_6_, bf16[640,1280]{1,0:T(8,128)(2,1)} %collective-permute-done.7.refs_3_.refs_7_, ...), custom_call_target="tpu_custom_call" | custom-call | flops 14949999616 | bytes 1024 | tf_op jit(solution)/shard_map/project/pallas_call | solution.py:170
  270.9 14.2 %project.7 = (bf16[1280,480]{1,0:T(8,128)(2,1)}, bf16[1280,480]{1,0:T(8,128)(2,1)}, bf16[1280,384]{1,0:T(8,128)(2,1)}) custom-call(s32[8]{0:T(128)} %copy-done.46, f32[1,960]{1,0:T(1,128)} %reshape_tile.7.refs_1_, bf16[640,1280]{1,0:T(8,128)(2,1)} %copy-done.5, bf16[640,1280]{1,0:T(8,128)(2,1)} %copy-done.16, bf16[1,1280,1344]{2,1,0:T(8,128)(2,1)} %bitcast.222, ...), custom_call_target="tpu_custom_call" | custom-call | flops 14949999616 | bytes 1024 | tf_op jit(solution)/shard_map/project/pallas_call | solution.py:170
  285.1 18.7 %attend.6 = (bf16[4,160,640]{2,1,0:T(8,128)(2,1)}, bf16[3,2,2560,128]{3,2,1,0:T(8,128)(2,1)}) custom-call(s32[8]{0:T(128)} %copy-done.40, bf16[1280,480]{1,0:T(8,128)(2,1)} %get-tuple-element.246.refs_1_, bf16[1280,480]{1,0:T(8,128)(2,1)} %get-tuple-element.249.refs_2_), custom_call_target="tpu_custom_call" | custom-call | flops 18400000000 | bytes 1024 | tf_op jit(solution)/shard_map/attend/pallas_call | solution.py:277
  307.5 18.7 %attend.7 = (bf16[4,160,640]{2,1,0:T(8,128)(2,1)}, bf16[3,2,2560,128]{3,2,1,0:T(8,128)(2,1)}) custom-call(s32[8]{0:T(128)} %copy-done.40, bf16[1280,480]{1,0:T(8,128)(2,1)} %get-tuple-element.253.refs_1_, bf16[1280,480]{1,0:T(8,128)(2,1)} %get-tuple-element.255.refs_2_), custom_call_target="tpu_custom_call" | custom-call | flops 18400000000 | bytes 1024 | tf_op jit(solution)/shard_map/attend/pallas_call | solution.py:277
  326.2 16.5 %all_to_all.46.refs_5_.refs_10_ = bf16[4,160,640]{2,1,0:T(8,128)(2,1)} all-to-all(bf16[4,160,640]{2,1,0:T(8,128)(2,1)} %get-tuple-element.259.o_ref), channel_id=1, replica_groups=mesh['seq'=4,'fsdp'=8] {'seq'}, dimensions={0} | all-to-all | bytes 1638400 | tf_op jit(solution)/shard_map/all_to_all | solution.py:1010
  352.7 18.6 %feed.3 = (f32[640,1280]{1,0:T(8,128)}, f32[640,1280]{1,0:T(8,128)}, bf16[640,384]{1,0:T(8,128)(2,1)}, bf16[640,1280]{1,0:T(8,128)(2,1)}) custom-call(s32[8]{0:T(128)} %copy-done.40, f32[1,1280]{1,0:T(1,128)} %get-tuple-element.416.refs_1_.refs_0_, f32[1,1280]{1,0:T(1,128)} %get-tuple-element.414.refs_2_.gain, ...), custom_call_target="tpu_custom_call" | custom-call | flops 19549999104 | bytes 1024 | tf_op jit(solution)/shard_map/feed/pallas_call | solution.py:446
  371.3 18.7 %feed_back.2 = (f32[640,1280]{1,0:T(8,128)}, bf16[640,1280]{1,0:T(8,128)(2,1)}, bf16[640,1408]{1,0:T(8,128)(2,1)}, bf16[640,128]{1,0:T(8,128)(2,1)}, bf16[640,12...) custom-call(s32[8]{0:T(128)} %copy-done.40, ...), custom_call_target="tpu_custom_call" | custom-call | flops 57500000 | bytes 1024 | tf_op jit(solution)/shard_map/feed_back/pallas_call | solution.py:585
  411.0 24.7 %attend_back.4.refs_1_ = bf16[2560,480]{1,0:T(8,128)(2,1)} custom-call(s32[8]{0:T(128)} %copy-done.40, f32[1,128]{1,0:T(1,128)} %pad_bitcast_fusion.1.factor, bf16[3,2,2560,128]{3,2,1,0:T(8,128)(2,1)} %get-tuple-element.269.saved, bf16[4,160,640]{2,1,0:T(8,128)(2,1)} %get-tuple-element.270.o_ref, bf16[4,160,640]{2,1,0:T(8,128)(2,1)} %copy-done.7), custom_call_target="tpu_custom_call" | custom-call | flops 57500000 | bytes 1024 | tf_op jit(solution)/shard_map/attend_back/pallas_call | solution.py:349
  436.6 24.7 %attend_back.5.refs_2_ = bf16[2560,480]{1,0:T(8,128)(2,1)} custom-call(s32[8]{0:T(128)} %copy-done.40, f32[1,128]{1,0:T(1,128)} %pad_bitcast_fusion.1.factor, bf16[3,2,2560,128]{3,2,1,0:T(8,128)(2,1)} %get-tuple-element.261.saved, bf16[4,160,640]{2,1,0:T(8,128)(2,1)} %get-tuple-element.259.o_ref, bf16[4,160,640]{2,1,0:T(8,128)(2,1)} %copy-done.9), custom_call_target="tpu_custom_call" | custom-call | flops 57500000 | bytes 1024 | tf_op jit(solution)/shard_map/attend_back/pallas_call | solution.py:349
  461.3 14.8 %project_back.4 = (bf16[640,1280]{1,0:T(8,128)(2,1)}, bf16[640,1280]{1,0:T(8,128)(2,1)}, bf16[1280,384]{1,0:T(8,128)(2,1)}) custom-call(s32[8]{0:T(128)} %copy-done.46, bf16[2560,480]{1,0:T(8,128)(2,1)} %attend_back.4.refs_1_, bf16[2560,480]{1,0:T(8,128)(2,1)} %attend_back.5.refs_2_, bf16[1,1280,1344]{2,1,0:T(8,128)(2,1)} %bitcast.223, ...), custom_call_target="tpu_custom_call" | custom-call | flops 57500000 | bytes 1024 | tf_op jit(solution)/shard_map/project_back/pallas_call | solution.py:758
  484.8 14.6 %project_sums.2 = (bf16[1280,768]{1,0:T(8,128)(2,1)}, bf16[1280,384]{1,0:T(8,128)(2,1)}) custom-call(s32[8]{0:T(128)} %copy-done.40, bf16[2560,480]{1,0:T(8,128)(2,1)} %attend_back.4.refs_1_, bf16[2560,480]{1,0:T(8,128)(2,1)} %attend_back.5.refs_2_, bf16[1280,384]{1,0:T(8,128)(2,1)} %get-tuple-element.289.refs_3_, ...), custom_call_target="tpu_custom_call" | custom-call | flops 57500000 | bytes 1024 | tf_op jit(solution)/shard_map/project_sums/pallas_call | solution.py:863
  529.3 24.4 %feed_back.3 = (f32[640,1280]{1,0:T(8,128)}, bf16[640,1280]{1,0:T(8,128)(2,1)}, bf16[640,1408]{1,0:T(8,128)(2,1)}, bf16[640,128]{1,0:T(8,128)(2,1)}, bf16[640,12...) custom-call(s32[8]{0:T(128)} %copy-done.40, ...), custom_call_target="tpu_custom_call" | custom-call | flops 57500000 | bytes 1024 | tf_op jit(solution)/shard_map/feed_back/pallas_call | solution.py:585
  581.2 25.0 %attend_back.6.refs_1_ = bf16[2560,480]{1,0:T(8,128)(2,1)} custom-call(s32[8]{0:T(128)} %copy-done.40, f32[1,128]{1,0:T(1,128)} %pad_bitcast_fusion.factor, bf16[3,2,2560,128]{3,2,1,0:T(8,128)(2,1)} %get-tuple-element.307.saved, bf16[4,160,640]{2,1,0:T(8,128)(2,1)} %get-tuple-element.308.o_ref, bf16[4,160,640]{2,1,0:T(8,128)(2,1)} %copy-done.6), custom_call_target="tpu_custom_call" | custom-call | flops 57500000 | bytes 1024 | tf_op jit(solution)/shard_map/attend_back/pallas_call | solution.py:349
  607.1 24.7 %attend_back.7.refs_2_ = bf16[2560,480]{1,0:T(8,128)(2,1)} custom-call(s32[8]{0:T(128)} %copy-done.40, f32[1,128]{1,0:T(1,128)} %pad_bitcast_fusion.factor, bf16[3,2,2560,128]{3,2,1,0:T(8,128)(2,1)} %get-tuple-element.235.saved, bf16[4,160,640]{2,1,0:T(8,128)(2,1)} %get-tuple-element.233.o_ref, bf16[4,160,640]{2,1,0:T(8,128)(2,1)} %copy-done.8), custom_call_target="tpu_custom_call" | custom-call | flops 57500000 | bytes 1024 | tf_op jit(solution)/shard_map/attend_back/pallas_call | solution.py:349
  633.0 14.6 %project_back.6 = (bf16[640,1280]{1,0:T(8,128)(2,1)}, bf16[640,1280]{1,0:T(8,128)(2,1)}, bf16[1280,384]{1,0:T(8,128)(2,1)}) custom-call(s32[8]{0:T(128)} %copy-done.46, bf16[2560,480]{1,0:T(8,128)(2,1)} %attend_back.6.refs_1_, bf16[2560,480]{1,0:T(8,128)(2,1)} %attend_back.7.refs_2_, bf16[1,1280,1344]{2,1,0:T(8,128)(2,1)} %bitcast.218, ...), custom_call_target="tpu_custom_call" | custom-call | flops 57500000 | bytes 1024 | tf_op jit(solution)/shard_map/project_back/pallas_call | solution.py:758
  658.6 14.6 %project_sums.3 = (bf16[1280,768]{1,0:T(8,128)(2,1)}, bf16[1280,384]{1,0:T(8,128)(2,1)}) custom-call(s32[8]{0:T(128)} %copy-done.40, bf16[2560,480]{1,0:T(8,128)(2,1)} %attend_back.6.refs_1_, bf16[2560,480]{1,0:T(8,128)(2,1)} %attend_back.7.refs_2_, bf16[1280,384]{1,0:T(8,128)(2,1)} %get-tuple-element.221.refs_3_, ...), custom_call_target="tpu_custom_call" | custom-call | flops 57500000 | bytes 1024 | tf_op jit(solution)/shard_map/project_sums/pallas_call | solution.py:863
  (265 shorter events, 237.9 us)
Async XLA Ops:
  7.2 74.4 %all-gather.5.cloned.1.call-start = ((), (), s32[]{:S(2)}) async-start(), calls=%async_computation.12 | async-start | bytes 4055040 | tf_op jit(solution)/shard_map/all_gather | solution.py:1002
  12.7 164.8 %all-gather.7.cloned.1.call-start = ((), (), s32[]{:S(2)}) async-start(), calls=%async_computation.13 | async-start | bytes 6635520 | tf_op jit(solution)/shard_map/all_gather | solution.py:1002
  15.4 66.3 %collective-permute-start.1 = (bf16[640,1280]{1,0:T(8,128)(2,1)}, bf16[640,1280]{1,0:T(8,128)(2,1)}, u32[]{:S(2)}, u32[]{:S(2)}) collective-permute-start(bf16[640,1280]{1,0:T(8,128)(2,1)} %multiply_convert_fusion.refs_2_.refs_6_), channel_id=1, source_target_pairs={{0,16},{8,24},{16,0},{24,8},{1,17},{9,25},{17,1},{25,9},{2,18},{10... | collective-permute-start | bytes 4915208 | tf_op jit(solution)/shard_map/ppermute | solution.py:880
  138.5 22.5 %all-to-all-start = ((bf16[4,160,640]{2,1,0:T(8,128)(2,1)}), bf16[4,160,640]{2,1,0:T(8,128)(2,1)S(1)}, u32[]{:S(2)}, u32[]{:S(2)}) async-start(bf16[4,160,640]{2,1,0:T(8,128)(2,1)} %get-tuple-element.308.o_ref), calls=%async_computation | async-start | bytes 1638400 | tf_op jit(solution)/shard_map/all_to_all | solution.py:1010
  142.1 101.4 %all-gather.9.cloned.1.call-start = ((), (), s32[]{:S(2)}) async-start(), calls=%async_computation.14 | async-start | bytes 4055040 | tf_op jit(solution)/shard_map/all_gather | solution.py:1002
  179.4 163.4 %all-gather.11.cloned.1.call-start = ((), (), s32[]{:S(2)}) async-start(), calls=%async_computation.15 | async-start | bytes 6635520 | tf_op jit(solution)/shard_map/all_gather | solution.py:1002
  210.5 33.0 %collective-permute-start.5 = (bf16[384,1280]{1,0:T(8,128)(2,1)}, bf16[384,1280]{1,0:T(8,128)(2,1)}, u32[]{:S(2)}, u32[]{:S(2)}) collective-permute-start(bf16[384,1280]{1,0:T(8,128)(2,1)} %slice.295), channel_id=1, source_target_pairs={{0,16},{8,24},{16,0},{24,8},{1,17},{9,25},{17,1},{25,9},{2,18},{10... | collective-permute-start | bytes 2949128 | tf_op jit(solution)/shard_map/ppermute | solution.py:880
  210.7 37.2 %collective-permute-start.7 = (bf16[640,1280]{1,0:T(8,128)(2,1)S(1)}, bf16[640,1280]{1,0:T(8,128)(2,1)}, u32[]{:S(2)}, u32[]{:S(2)}) collective-permute-start(bf16[640,1280]{1,0:T(8,128)(2,1)S(1)} %copy-done.4), channel_id=1, source_target_pairs={{0,8},{8,0},{16,24},{24,16},{1,9},{9,1},{17,25},{25,17},{2,10},{10... | collective-permute-start | bytes 4915208 | tf_op jit(solution)/shard_map/ppermute | solution.py:880
  246.5 17.2 %collective-permute-start.6 = (bf16[256,1280]{1,0:T(8,128)(2,1)S(1)}, bf16[256,1280]{1,0:T(8,128)(2,1)}, u32[]{:S(2)}, u32[]{:S(2)}) collective-permute-start(bf16[256,1280]{1,0:T(8,128)(2,1)S(1)} %slice.296), channel_id=1, source_target_pairs={{0,16},{8,24},{16,0},{24,8},{1,17},{9,25},{17,1},{25,9},{2,18},{10... | collective-permute-start | bytes 1966088 | tf_op jit(solution)/shard_map/ppermute | solution.py:880
  303.8 22.4 %all-to-all-start.2 = ((bf16[4,160,640]{2,1,0:T(8,128)(2,1)}), bf16[4,160,640]{2,1,0:T(8,128)(2,1)S(1)}, u32[]{:S(2)}, u32[]{:S(2)}) async-start(bf16[4,160,640]{2,1,0:T(8,128)(2,1)} %get-tuple-element.270.o_ref), calls=%async_computation.2 | async-start | bytes 1638400 | tf_op jit(solution)/shard_map/all_to_all | solution.py:1010
  390.0 15.5 %all-to-all-start.4 = ((bf16[4,160,640]{2,1,0:T(8,128)(2,1)}), bf16[4,160,640]{2,1,0:T(8,128)(2,1)S(1)}, u32[]{:S(2)}, u32[]{:S(2)}) async-start(bf16[4,160,640]{2,1,0:T(8,128)(2,1)} %get-tuple-element.271), calls=%async_computation.4 | async-start | bytes 1638400 | tf_op jit(solution)/shard_map/all_to_all | solution.py:1013
  393.5 88.4 %reduce-scatter.4.cloned.1.call-start = ((), (), s32[]{:S(2)}) async-start(), calls=%async_computation.16 | async-start | bytes 2211840 | tf_op jit(solution)/shard_map/reduce_scatter | solution.py:918
  406.4 29.3 %all-to-all-start.5 = ((bf16[4,160,640]{2,1,0:T(8,128)(2,1)}), bf16[4,160,640]{2,1,0:T(8,128)(2,1)S(1)}, u32[]{:S(2)}, u32[]{:S(2)}) async-start(bf16[4,160,640]{2,1,0:T(8,128)(2,1)} %get-tuple-element.280), calls=%async_computation.5 | async-start | bytes 1638400 | tf_op jit(solution)/shard_map/all_to_all | solution.py:1013
  409.9 163.7 %reduce-scatter.6.cloned.1.call-start = ((), (), s32[]{:S(2)}) async-start(), calls=%async_computation.17 | async-start | bytes 2211840 | tf_op jit(solution)/shard_map/reduce_scatter | solution.py:918
  483.0 24.2 %collective-permute-start.12 = (bf16[384,1280]{1,0:T(8,128)(2,1)}, bf16[384,1280]{1,0:T(8,128)(2,1)S(1)}, u32[]{:S(2)}, u32[]{:S(2)}) collective-permute-start(bf16[384,1280]{1,0:T(8,128)(2,1)} %slice.314), channel_id=1, source_target_pairs={{0,16},{8,24},{16,0},{24,8},{1,17},{9,25},{17,1},{25,9},{2,18},{10... | collective-permute-start | bytes 2949128 | tf_op jit(solution)/shard_map/ppermute | solution.py:880
  507.3 16.3 %collective-permute-start.13 = (bf16[256,1280]{1,0:T(8,128)(2,1)S(1)}, bf16[256,1280]{1,0:T(8,128)(2,1)S(1)}, u32[]{:S(2)}, u32[]{:S(2)}) collective-permute-start(bf16[256,1280]{1,0:T(8,128)(2,1)S(1)} %slice.315), channel_id=1, source_target_pairs={{0,16},{8,24},{16,0},{24,8},{1,17},{9,25},{17,1},{25,9},{2,18},{10... | collective-permute-start | bytes 1966088 | tf_op jit(solution)/shard_map/ppermute | solution.py:880
  557.2 96.2 %reduce-scatter.8.cloned.1.call-start = ((), (), s32[]{:S(2)}) async-start(), calls=%async_computation.18 | async-start | bytes 2211840 | tf_op jit(solution)/shard_map/reduce_scatter | solution.py:918
  574.8 31.4 %all-to-all-start.7 = ((bf16[4,160,640]{2,1,0:T(8,128)(2,1)}), bf16[4,160,640]{2,1,0:T(8,128)(2,1)S(1)}, u32[]{:S(2)}, u32[]{:S(2)}) async-start(bf16[4,160,640]{2,1,0:T(8,128)(2,1)} %get-tuple-element.319), calls=%async_computation.8 | async-start | bytes 1638400 | tf_op jit(solution)/shard_map/all_to_all | solution.py:1013
  578.6 53.2 %collective-permute-start.16 = (bf16[2,160,768]{2,1,0:T(8,128)(2,1)S(1)}, bf16[2,160,768]{2,1,0:T(8,128)(2,1)}, u32[]{:S(2)}, u32[]{:S(2)}) collective-permute-start(bf16[2,160,768]{2,1,0:T(8,128)(2,1)S(1)} %add_convert_fusion.3), channel_id=1, source_target_pairs={{0,16},{8,24},{16,0},{24,8},{1,17},{9,25},{17,1},{25,9},{2,18},{10... | collective-permute-start | bytes 1474568 | tf_op jit(solution)/shard_map/ppermute | solution.py:880
  654.5 23.2 %collective-permute-start.18 = (bf16[256,1280]{1,0:T(8,128)(2,1)}, bf16[256,1280]{1,0:T(8,128)(2,1)S(1)}, u32[]{:S(2)}, u32[]{:S(2)}) collective-permute-start(bf16[256,1280]{1,0:T(8,128)(2,1)} %slice.316), channel_id=1, source_target_pairs={{0,16},{8,24},{16,0},{24,8},{1,17},{9,25},{17,1},{25,9},{2,18},{10... | collective-permute-start | bytes 1966088 | tf_op jit(solution)/shard_map/ppermute | solution.py:880
  656.2 20.8 %collective-permute-start.20 = (bf16[160,768]{1,0:T(8,128)(2,1)S(1)}, bf16[160,768]{1,0:T(8,128)(2,1)S(1)}, u32[]{:S(2)}, u32[]{:S(2)}) collective-permute-start(bf16[160,768]{1,0:T(8,128)(2,1)S(1)} %add_convert_fusion.5), channel_id=1, source_target_pairs={{0,16},{8,24},{16,0},{24,8},{1,17},{9,25},{17,1},{25,9},{2,18},{10... | collective-permute-start | bytes 737288 | tf_op jit(solution)/shard_map/ppermute | solution.py:880
  698.9 28.9 %collective-permute-start.23 = (bf16[640,1280]{1,0:T(8,128)(2,1)}, bf16[640,1280]{1,0:T(8,128)(2,1)S(1)}, u32[]{:S(2)}, u32[]{:S(2)}) collective-permute-start(bf16[640,1280]{1,0:T(8,128)(2,1)} %get-tuple-element.344), channel_id=1, source_target_pairs={{0,8},{8,0},{16,24},{24,16},{1,9},{9,1},{17,25},{25,17},{2,10},{10... | collective-permute-start | bytes 4915208 | tf_op jit(solution)/shard_map/ppermute | solution.py:880
  698.9 24.5 %collective-permute-start.24 = (bf16[384,1280]{1,0:T(8,128)(2,1)}, bf16[384,1280]{1,0:T(8,128)(2,1)}, u32[]{:S(2)}, u32[]{:S(2)}) collective-permute-start(bf16[384,1280]{1,0:T(8,128)(2,1)} %slice.317), channel_id=1, source_target_pairs={{0,16},{8,24},{16,0},{24,8},{1,17},{9,25},{17,1},{25,9},{2,18},{10... | collective-permute-start | bytes 2949128 | tf_op jit(solution)/shard_map/ppermute | solution.py:880
  699.3 17.9 %all-to-all-start.8 = ((bf16[8,40,768]{2,1,0:T(8,128)(2,1)}), bf16[8,40,768]{2,1,0:T(8,128)(2,1)S(1)}, u32[]{:S(2)}, u32[]{:S(2)}) async-start(bf16[8,40,768]{2,1,0:T(8,128)(2,1)} %fusion.8), calls=%async_computation.11 | async-start | bytes 983040 | tf_op jit(solution)/shard_map/all_to_all | solution.py:909
  (66 other events, 522.2 us)
Sparse Core Ops, SparseCore 0:
  12.8 68.6 all-gather.4
  83.7 92.6 all-gather.6
  179.5 63.8 all-gather.8
  245.5 92.7 all-gather.10
  405.6 64.9 reduce-scatter.3
  507.4 66.1 reduce-scatter.5
  577.1 65.6 reduce-scatter.7
